TPU v7x, 128 devices: a whole 4x4x4 slice. The times are simulated.
128 devices in a mesh: view: 4 (over x), blk: 32 (over z, y, core).
Axes of the slice: x: 4, y: 4, z: 4, core: 2. Of those that a mesh axis runs over, the one named last changes fastest.
Arguments:
- estimate: float32 [1024, 128, 512], P('blk'), may hold values from 0.15 to 6.7
- views: float32 [4, 1024, 128, 512], P('view', 'blk'), may hold values from 0.15 to 6.7
- psf: float32 [4, 3, 33], P('view'), may hold values from 0.05 to 1
- offsets: int32 [4, 3], P('view'), may hold values from 0 to 16, as said below
Outputs:
- updated: float32 [1024, 128, 512], P('blk')
Inputs may be any that keep to these rules, and one draw needn't show every extreme that they name: Voxel p of a view's grid lies at voxel p + offsets of the estimate's grid along each dimension.
All inputs are finite; a program needn't handle non-finite values.
Results may differ from a plain program's by a relative error of at most 0.00007.
Values sent between devices are 32-bit elements; how exact they have to be, the bound alone decides.
No kernel may reach another device: no remote copies, remote signals or barrier semaphores. Data moves between devices by JAX's collectives and lax.ppermute only.
A program may use at most 192 MiB of HBM per device.

v0:
```python
import jax
import jax.numpy as jnp
from jax import lax
from jax.sharding import PartitionSpec as P

RADIUS = 16


background = 0.1


def shifted(block, axis, distance):
    devices = range(lax.axis_size(axis))
    route = [(i - distance, i) for i in devices if i - distance in devices]
    return lax.ppermute(block, axis, route)


def band_matrix(kernel_taps, shift_by, height, breadth, base):
    lag_index = (
        lax.broadcasted_iota(jnp.int32, (height, breadth), 0)
        - lax.broadcasted_iota(jnp.int32, (height, breadth), 1)
        + shift_by
        + base
    )
    flat_lags = lag_index.reshape(-1)
    tap_index = jnp.arange(kernel_taps.shape[0], dtype=jnp.int32)
    one_hot = (flat_lags[None, :] == tap_index[:, None]).astype(jnp.float32)
    band = jnp.dot(kernel_taps, one_hot, precision=lax.Precision.HIGHEST)
    return band.reshape(height, breadth)


def across(volume, band_y, band_z):
    section = jnp.einsum("rkz,pk->rpz", volume, band_y, precision=lax.Precision.HIGHEST)
    return jnp.einsum("ryk,pk->ryp", section, band_z, precision=lax.Precision.HIGHEST)


def across_back(volume, band_y, band_z):
    section = jnp.einsum("ryp,pk->ryk", volume, band_z, precision=lax.Precision.HIGHEST)
    return jnp.einsum("rpz,pk->rkz", section, band_y, precision=lax.Precision.HIGHEST)


def extend(volume):
    from_lower = shifted(volume[-RADIUS:], "blk", 1)
    from_upper = shifted(volume, "blk", -1)
    return jnp.concatenate([from_lower, volume, from_upper], axis=0)


def spill(spread_back, slab_rows):
    owned_rows = spread_back[RADIUS : RADIUS + slab_rows]
    from_upper = shifted(spread_back[:RADIUS], "blk", -1)
    from_lower = shifted(spread_back[RADIUS + slab_rows :], "blk", 1)
    owned_rows = owned_rows + jnp.pad(from_upper, ((slab_rows - RADIUS, 0), (0, 0), (0, 0)))
    owned_rows = owned_rows + from_lower
    return owned_rows


def body(estimate, views, psf, offsets):
    measured = views[0]
    kernel = psf[0] / jnp.sum(psf[0], axis=1, keepdims=True)
    shift_by = offsets[0]
    slab_rows, width_cells, depth_cells = estimate.shape
    band_y = band_matrix(kernel[1], shift_by[1], width_cells, width_cells, RADIUS)
    band_z = band_matrix(kernel[2], shift_by[2], depth_cells, depth_cells, RADIUS)
    band_x = band_matrix(kernel[0], shift_by[0], slab_rows, slab_rows + 3 * RADIUS, 2 * RADIUS)
    blurred = across(extend(estimate), band_y, band_z)
    forward = (
        jnp.einsum("im,myz->iyz", band_x, blurred, precision=lax.Precision.HIGHEST) + background
    )
    ratios = measured / forward
    spread = across_back(ratios, band_y, band_z)
    spread_back = jnp.einsum("im,iyz->myz", band_x, spread, precision=lax.Precision.HIGHEST)
    view_count = lax.axis_size("view")
    correction = lax.psum(spill(spread_back, slab_rows), "view")
    return estimate * correction / view_count


def solution(mesh):
    placed = (
        P("blk", None, None),
        P("view", "blk", None, None),
        P("view", None, None),
        P("view", None),
    )
    return jax.shard_map(
        body, mesh=mesh, in_specs=placed, out_specs=P("blk", None, None), check_vma=False
    )
```

profile of v0, /device:TPU:59, one launch (start us, length us, event | category | flops | bytes accessed | tf_op | source)
XLA Modules:
  0.0 545.1 jit_solution(1748639453527557189)
XLA Ops:
  6.5 0.0 copy-start
  6.5 0.0 copy-start.1
  6.5 0.0 all-reduce.3.cloned.1.call-start
  6.5 2.7 collective-permute-start.1
  9.3 4.8 slice.37
  14.1 5.1 collective-permute-start
  19.2 0.0 copy-done
  19.2 0.1 reduce_sum.9
  19.3 0.0 copy-done.1
  19.3 0.7 fusion.32
  19.9 0.7 add_add_fusion.1
  20.7 0.1 bitcast_divide_fusion.2
  20.7 0.6 add_add_fusion.2
  21.3 0.8 add_add_fusion
  22.1 0.1 fusion.29
  22.2 0.3 fusion.27
  22.5 0.3 fusion.22
  22.8 1.2 fusion.20
  24.0 8.3 %fusion.2 = pred[512,512,33]{1,0,2:T(32,128)(4,1)} fusion(s32[512,512]{1,0:T(8,128)S(1)} %add_add_fusion), kind=kLoop, calls=%fused_computation.3 | loop fusion | flops 8650752 | bytes 9699328 | tf_op jit(solution)/shard_map/eq | solution.py:27
  32.3 22.2 %fusion = f32[1,512,512]{2,0,1:T(1,128)S(1)} fusion(pred[512,512,33]{1,0,2:T(32,128)(4,1)} %fusion.2, f32[3,33]{1,0:T(4,128)S(1)} %bitcast_divide_fusion.2), kind=kOutput, calls=%fused_computation | convolution fusion | flops 103809024 | bytes 9699840 | tf_op jit(solution)/shard_map/dot_general | solution.py:28
  54.5 10.4 %collective-permute-done = f32[16,128,512]{2,1,0:T(8,128)} collective-permute-done((f32[16,128,512]{2,1,0:T(8,128)}, f32[16,128,512]{2,1,0:T(8,128)}, u32[]{:S(2)}, u32[]{:S(2)}) %collective-permute-start) | collective-permute-done | bytes 4194336 | tf_op jit(solution)/shard_map/ppermute | solution.py:15
  64.9 39.0 %collective-permute-done.1 = f32[32,128,512]{2,1,0:T(8,128)} collective-permute-done((f32[32,128,512]{2,1,0:T(8,128)}, f32[32,128,512]{2,1,0:T(8,128)}, u32[]{:S(2)}, u32[]{:S(2)}) %collective-permute-start.1) | collective-permute-done | bytes 8388640 | tf_op jit(solution)/shard_map/ppermute | solution.py:15
  103.9 25.6 %fusion.3 = f32[128,80,512]{2,0,1:T(8,128)S(1)} fusion(f32[128,128,1]{1,0,2:T(8,128)S(1)} %bitcast.53, f32[32,128,512]{2,1,0:T(8,128)} %collective-permute-done.1, f32[32,128,512]{2,1,0:T(8,128)} %param.4, f32[16,128,512]{2,1,0:T(8,128)} %collective-permute-done), kind=kOutput, calls=%fused_computation.4 | convolution fusion | flops 8063549440 | bytes 42008576 | tf_op jit(solution)/shard_map/rkz,pk->rpz/dot_general | solution.py:33
  129.5 37.1 %fusion.9 = f32[80,128,512]{2,1,0:T(8,128)} fusion(f32[128,80,512]{2,0,1:T(8,128)S(1)} %fusion.3, f32[1,512,512]{2,0,1:T(1,128)S(1)} %fusion), kind=kOutput, calls=%fused_computation.10 | convolution fusion | flops 32212254720 | bytes 42991616 | tf_op jit(solution)/shard_map/ryk,pk->ryp/dot_general | solution.py:34
  166.6 28.9 %fusion.11 = f32[32,128,512]{2,0,1:T(8,128)S(1)} fusion(f32[32,80,1]{1,0,2:T(8,128)S(1)} %bitcast.55, f32[80,128,512]{2,1,0:T(8,128)} %fusion.9), kind=kOutput, calls=%fused_computation.12 | convolution fusion | flops 2013265920 | bytes 29370368 | tf_op jit(solution)/shard_map/im,myz->iyz/dot_general | solution.py:67
  195.6 19.6 %fusion.16 = f32[32,128,512]{2,1,0:T(8,128)S(1)} fusion(f32[1,32,128,512]{3,2,1,0:T(8,128)} %param.5, f32[32,128,512]{2,0,1:T(8,128)S(1)} %fusion.11, f32[1,512,512]{2,0,1:T(1,128)S(1)} %fusion), kind=kOutput, calls=%fused_computation.19 | convolution fusion | flops 12889096192 | bytes 26214400 | tf_op jit(solution)/shard_map/ryp,pk->ryk/dot_general | solution.py:38
  215.2 8.3 %fusion.33 = f32[128,32,512]{2,0,1:T(8,128)S(1)} fusion(f32[128,128,1]{1,0,2:T(8,128)S(1)} %bitcast.54, f32[32,128,512]{2,1,0:T(8,128)S(1)} %fusion.16), kind=kOutput, calls=%fused_computation.47 | convolution fusion | flops 3221225472 | bytes 16842752 | tf_op jit(solution)/shard_map/rpz,pk->rkz/dot_general | solution.py:39
  223.5 21.4 %fusion.14 = f32[80,128,512]{2,0,1:T(8,128)S(1)} fusion(f32[32,80,1]{1,0,2:T(8,128)S(1)} %bitcast.56, f32[128,32,512]{2,0,1:T(8,128)S(1)} %fusion.33), kind=kOutput, calls=%fused_computation.16 | convolution fusion | flops 2013265920 | bytes 29370368 | tf_op jit(solution)/shard_map/im,iyz->myz/dot_general | solution.py:71
  244.9 4.5 slice.45
  249.4 1.9 collective-permute-start.3
  251.3 0.4 slice.44
  251.8 2.4 collective-permute-start.2
  254.2 49.6 %collective-permute-done.2 = f32[16,128,512]{2,0,1:T(8,128)} collective-permute-done((f32[16,128,512]{2,0,1:T(8,128)S(1)}, f32[16,128,512]{2,0,1:T(8,128)}, u32[]{:S(2)}, u32[]{:S(2)}) %collective-permute-start.2) | collective-permute-done | bytes 4194336 | tf_op jit(solution)/shard_map/ppermute | solution.py:15
  303.8 38.2 %collective-permute-done.3 = f32[32,128,512]{2,0,1:T(8,128)} collective-permute-done((f32[32,128,512]{2,0,1:T(8,128)}, f32[32,128,512]{2,0,1:T(8,128)}, u32[]{:S(2)}, u32[]{:S(2)}) %collective-permute-start.3) | collective-permute-done | bytes 8388640 | tf_op jit(solution)/shard_map/ppermute | solution.py:15
  342.0 8.1 %fusion.13 = f32[32,128,512]{2,0,1:T(8,128)} fusion(f32[32,128,512]{2,0,1:T(8,128)} %collective-permute-done.3, f32[80,128,512]{2,0,1:T(8,128)S(1)} %fusion.14, f32[16,128,512]{2,0,1:T(8,128)} %collective-permute-done.2), kind=kLoop, calls=%fused_computation.15 | loop fusion | flops 4194304 | bytes 29360128 | tf_op jit(solution)/shard_map/add | solution.py:53
  350.2 0.0 all-reduce.3.cloned.1.call-update
  350.2 161.3 %all-reduce.3.cloned.1.call-done = f32[32,128,512]{2,0,1:T(8,128)} async-done(((f32[32,128,512]{2,0,1:T(8,128)}), f32[32,128,512]{2,0,1:T(8,128)}) %all-reduce.3.cloned.1.call-update) | async-done | bytes 8388624 | tf_op jit(solution)/shard_map/psum | solution.py:73
  511.5 14.9 %fusion.18 = f32[32,128,512]{2,0,1:T(8,128)} fusion(f32[32,128,512]{2,0,1:T(8,128)} %all-reduce.3.cloned.1.call-done, f32[32,128,512]{2,1,0:T(8,128)} %param.4), kind=kLoop, calls=%fused_computation.23 | loop fusion | flops 4194304 | bytes 25165824 | tf_op jit(solution)/shard_map/div | solution.py:74
  526.4 11.6 %copy.8 = f32[32,128,512]{2,1,0:T(8,128)} copy(f32[32,128,512]{2,0,1:T(8,128)} %fusion.18) | data formatting | bytes 16777216 | tf_op jit(solution)/shard_map/div | solution.py:74
Async XLA Ops:
  6.5 12.6 %copy-start = (f32[1,3,33]{2,0,1:T(1,128)S(1)}, f32[1,3,33]{2,0,1:T(1,128)}, u32[]{:S(2)}) copy-start(f32[1,3,33]{2,0,1:T(1,128)} %param.6) | copy-start | bytes 1192
  6.5 12.7 %copy-start.1 = (s32[1,3]{1,0:T(1,128)S(1)}, s32[1,3]{1,0:T(1,128)}, u32[]{:S(2)}) copy-start(s32[1,3]{1,0:T(1,128)} %param.7) | copy-start | bytes 40
  6.5 505.0 %all-reduce.3.cloned.1.call-start = ((), (), s32[]{:S(2)}) async-start(), calls=%async_computation | async-start | bytes 16777216 | tf_op jit(solution)/shard_map/psum | solution.py:73
  6.5 97.3 %collective-permute-start.1 = (f32[32,128,512]{2,1,0:T(8,128)}, f32[32,128,512]{2,1,0:T(8,128)}, u32[]{:S(2)}, u32[]{:S(2)}) collective-permute-start(f32[32,128,512]{2,1,0:T(8,128)} %param.4), channel_id=1, source_target_pairs={{1,0},{2,1},{3,2},{4,3},{5,4},{6,5},{7,6},{8,7},{9,8},{10,9},{11,1... | collective-permute-start | bytes 25165832 | tf_op jit(solution)/shard_map/ppermute | solution.py:15
  14.1 50.8 %collective-permute-start = (f32[16,128,512]{2,1,0:T(8,128)}, f32[16,128,512]{2,1,0:T(8,128)}, u32[]{:S(2)}, u32[]{:S(2)}) collective-permute-start(f32[16,128,512]{2,1,0:T(8,128)} %slice.37), channel_id=1, source_target_pairs={{0,1},{1,2},{2,3},{3,4},{4,5},{5,6},{6,7},{7,8},{8,9},{9,10},{10,1... | collective-permute-start | bytes 12582920 | tf_op jit(solution)/shard_map/ppermute | solution.py:15
  249.4 92.6 %collective-permute-start.3 = (f32[32,128,512]{2,0,1:T(8,128)}, f32[32,128,512]{2,0,1:T(8,128)}, u32[]{:S(2)}, u32[]{:S(2)}) collective-permute-start(f32[32,128,512]{2,0,1:T(8,128)} %slice.45), channel_id=1, source_target_pairs={{0,1},{1,2},{2,3},{3,4},{4,5},{5,6},{6,7},{7,8},{8,9},{9,10},{10,1... | collective-permute-start | bytes 25165832 | tf_op jit(solution)/shard_map/ppermute | solution.py:15
  251.8 52.0 %collective-permute-start.2 = (f32[16,128,512]{2,0,1:T(8,128)S(1)}, f32[16,128,512]{2,0,1:T(8,128)}, u32[]{:S(2)}, u32[]{:S(2)}) collective-permute-start(f32[16,128,512]{2,0,1:T(8,128)S(1)} %slice.44), channel_id=1, source_target_pairs={{1,0},{2,1},{3,2},{4,3},{5,4},{6,5},{7,6},{8,7},{9,8},{10,9},{11,1... | collective-permute-start | bytes 12582920 | tf_op jit(solution)/shard_map/ppermute | solution.py:15
Sparse Core Ops, SparseCore 0:
  350.3 161.1 all-reduce.2
where the time goes:
time: 554 us; the launch traced here: 545 us
  waiting for transfers between devices  298 us (54%)
  matrix products  165 us (30%)
  other arithmetic  34 us (6%)
  local copies, waits for them, and re-layouts  22 us (4%)
  between operations  13.7 us (2%)
  starting transfers between devices  12.1 us (2%)
    psum x1, waiting for transfers between devices, body(): correction = lax.psum(spill(spread_back, slab_rows), 'view')  161 us
    ppermute x4, waiting for transfers between devices, shifted(): return lax.ppermute(block, axis, route)  137 us
    dot_general x1, matrix products, across(): jnp.einsum('ryk,pk->ryp', section, band_z, precision=lax.Precision.HIGHEST)  37.1 us
    dot_general x1, matrix products, body(): jnp.einsum('im,myz->iyz', band_x, blurred, precision=lax.Precision.HIGHEST)  28.9 us
    dot_general x1, matrix products, across(): jnp.einsum('rkz,pk->rpz', volume, band_y, precision=lax.Precision.HIGHEST)  25.6 us
    dot_general x3, matrix products, band_matrix(): band = jnp.dot(kernel_taps, one_hot, precision=lax.Precision.HIGHEST)  23.7 us
    dot_general x1, matrix products, body(): jnp.einsum('im,iyz->myz', band_x, spread, precision=lax.Precision.HIGHEST)  21.4 us
    dot_general x1, matrix products, across_back(): jnp.einsum('ryp,pk->ryk', volume, band_z, precision=lax.Precision.HIGHEST)  19.6 us
  transfers between devices with their start and end apart: 5, of which 5 were waited for; matrix products, arithmetic and copies ran while one was open for 7% of the time, Pallas kernels for 0%

commit v1 on v0

v1 whole, which is shorter than its diff:
```python
import jax
import jax.numpy as jnp
from jax import lax
from jax.experimental import pallas as pl
from jax.experimental.pallas import tpu as pltpu
from jax.sharding import PartitionSpec as P

RADIUS = 16
KERN = 33
LEFT = RADIUS
RIGHT = 2 * RADIUS
QUARTER = 128
WIDE = LEFT + QUARTER + RIGHT
SLAB = 32
TALL = LEFT + SLAB + RIGHT
VIEWS = 4
BACKGROUND = 0.1
VMEM = 48 * 1024 * 1024

f32 = jnp.float32
bf16 = jnp.bfloat16


def call(kernel, out_shape, grid, in_specs, out_specs, prefetch=0, aliases=None, flops=0, moved=0):
    return pl.pallas_call(
        kernel,
        out_shape=out_shape,
        grid_spec=pltpu.PrefetchScalarGridSpec(
            num_scalar_prefetch=prefetch, grid=grid, in_specs=in_specs, out_specs=out_specs
        ),
        input_output_aliases=aliases or {},
        compiler_params=pltpu.CompilerParams(vmem_limit_bytes=VMEM),
        cost_estimate=pl.CostEstimate(flops=flops, bytes_accessed=moved, transcendentals=0),
    )


def shape(*dims, dtype=f32):
    return jax.ShapeDtypeStruct(dims, dtype)


def halves(x):
    high = x.astype(bf16)
    low = (x - high.astype(f32)).astype(bf16)
    return high, low


def stacked(x, axis, blank=0):
    high, low = halves(x)
    parts = [high, low, high]
    if blank:
        dims = list(x.shape)
        dims[axis] = blank
        parts.append(jnp.zeros(dims, bf16))
    return jnp.concatenate(parts, axis=axis)


def dot(a, b):
    return lax.dot_general(a, b, (((1,), (0,)), ((), ())), preferred_element_type=f32)


def dot_nt(a, b):
    return lax.dot_general(a, b, (((1,), (1,)), ((), ())), preferred_element_type=f32)


def lag_taps(params, slot, dim, lag):
    value = jnp.zeros(lag.shape, f32)
    for tap in range(KERN):
        value = jnp.where(lag == tap, params[slot, dim, tap], value)
    return value


def thirds(value, part):
    high = value.astype(bf16).astype(f32)
    return jnp.where(part == 2, value - high, high).astype(bf16)


def grid_of(rows, columns):
    return (
        lax.broadcasted_iota(jnp.int32, (rows, columns), 0),
        lax.broadcasted_iota(jnp.int32, (rows, columns), 1),
    )


def bands_kernel(params, ax, az, ay, ayt, azt, axt):
    def offset(slot, dim):
        return params[slot, dim, KERN].astype(jnp.int32)

    row, lane = grid_of(SLAB, 256)
    part = lane // TALL
    spot = lane - part * TALL
    for slot in range(VIEWS):
        lag = row + offset(slot, 0) - spot + 2 * RADIUS
        lag = jnp.where(part < 3, lag, -1)
        ax[slot * SLAB : (slot + 1) * SLAB, :] = thirds(lag_taps(params, slot, 0, lag), part)
    row, lane = grid_of(QUARTER, 512)
    span = QUARTER + 2 * RADIUS
    part = lane // span
    spot = lane - part * span
    for slot in range(VIEWS):
        lag = jnp.where(part < 3, row - spot + 2 * RADIUS, -1)
        az[slot] = thirds(lag_taps(params, slot, 2, lag), part)
    row, lane = grid_of(128, 384)
    part = lane // 128
    spot = lane - part * 128
    for slot in range(VIEWS):
        lag = row + offset(slot, 1) - spot + RADIUS
        ay[slot] = thirds(lag_taps(params, slot, 1, lag), part)
        lag = spot + offset(slot, 1) - row + RADIUS
        ayt[slot] = thirds(lag_taps(params, slot, 1, lag), part)
    row, lane = grid_of(WIDE, 384)
    part = lane // 128
    spot = lane - part * 128
    for slot in range(VIEWS):
        lag = spot + offset(slot, 2) - row + 2 * RADIUS
        azt[slot] = thirds(lag_taps(params, slot, 2, lag), part)
    row, lane = grid_of(TALL, 384)
    part = lane // 128
    spot = lane - part * 128
    owner = spot // SLAB
    plane = spot - owner * SLAB
    value = jnp.zeros((TALL, 384), f32)
    for slot in range(VIEWS):
        lag = plane + offset(slot, 0) - row + 2 * RADIUS
        value = jnp.where(owner == slot, lag_taps(params, slot, 0, lag), value)
    axt[...] = thirds(value, part)


def bands(params):
    whole = pl.BlockSpec(memory_space=pltpu.VMEM)
    return pl.pallas_call(
        bands_kernel,
        out_shape=(
            shape(VIEWS * SLAB, 256, dtype=bf16),
            shape(VIEWS, QUARTER, 512, dtype=bf16),
            shape(VIEWS, 128, 384, dtype=bf16),
            shape(VIEWS, 128, 384, dtype=bf16),
            shape(VIEWS, WIDE, 384, dtype=bf16),
            shape(TALL, 384, dtype=bf16),
        ),
        in_specs=[pl.BlockSpec(memory_space=pltpu.SMEM)],
        out_specs=(whole,) * 6,
        compiler_params=pltpu.CompilerParams(vmem_limit_bytes=VMEM),
    )(params)


def window_kernel(spot, left, middle, right, out):
    q = spot[0]
    for i in range(middle.shape[0]):
        before = left[i].T[QUARTER - LEFT :, :]
        after = right[i].T[:RIGHT, :]
        out[i, :LEFT, :] = jnp.where(q > 0, before, 0.0)
        out[i, LEFT : LEFT + QUARTER, :] = middle[i].T
        out[i, LEFT + QUARTER :, :] = jnp.where(q < VIEWS - 1, after, 0.0)


def window(estimate, spot):
    n = 4
    block = (n, 128, QUARTER)
    return call(
        window_kernel,
        shape(SLAB, WIDE, 128),
        (SLAB // n,),
        [
            pl.BlockSpec(block, lambda i, s: (i, 0, jnp.maximum(s[0] - 1, 0))),
            pl.BlockSpec(block, lambda i, s: (i, 0, s[0])),
            pl.BlockSpec(block, lambda i, s: (i, 0, jnp.minimum(s[0] + 1, VIEWS - 1))),
        ],
        pl.BlockSpec((n, WIDE, 128), lambda i, s: (i, 0, 0)),
        prefetch=1,
        moved=9 << 20,
    )(spot, estimate, estimate, estimate)


def blur_x_kernel(ax, lower, middle, upper, out):
    for z in range(0, middle.shape[1], 2):
        columns = [
            jnp.concatenate([lower[:, c, :], middle[:, c, :], upper[:, c, :]], axis=0)
            for c in (z, z + 1)
        ]
        data = stacked(jnp.concatenate(columns, axis=1), 0, 256 - 3 * TALL)
        result = dot(ax[...], data)
        out[:, z, :] = result[:, :128]
        out[:, z + 1, :] = result[:, 128:]


def blur_x(ax, lower, middle, upper):
    n = 16
    return call(
        blur_x_kernel,
        shape(VIEWS * SLAB, WIDE, 128),
        (WIDE // n,),
        [
            pl.BlockSpec(ax.shape, lambda i: (0, 0)),
            pl.BlockSpec((LEFT, n, 128), lambda i: (0, i, 0)),
            pl.BlockSpec((SLAB, n, 128), lambda i: (0, i, 0)),
            pl.BlockSpec((RIGHT, n, 128), lambda i: (0, i, 0)),
        ],
        pl.BlockSpec((VIEWS * SLAB, n, 128), lambda i: (0, i, 0)),
        flops=6 << 30,
        moved=18 << 20,
    )(ax, lower, middle, upper)


def forward_kernel(starts, az, ay, blurred, out):
    start = starts[pl.program_id(0)]
    span = QUARTER + 2 * RADIUS
    for i in range(0, blurred.shape[0], 2):
        planes = [blurred[j, pl.ds(start, span), :] for j in (i, i + 1)]
        data = stacked(jnp.concatenate(planes, axis=1), 0, 512 - 3 * span)
        section = dot(az[0], data)
        section = jnp.concatenate([section[:, :128], section[:, 128:]], axis=0)
        result = dot_nt(ay[0], stacked(section, 1)) + BACKGROUND
        out[i] = result[:, :QUARTER]
        out[i + 1] = result[:, QUARTER:]


def forward_of(starts, az, ay, blurred):
    n = 4
    steps = SLAB // n
    return call(
        forward_kernel,
        shape(VIEWS * SLAB, 128, QUARTER),
        (VIEWS, steps),
        [
            pl.BlockSpec((1,) + az.shape[1:], lambda v, i, s: (v, 0, 0)),
            pl.BlockSpec((1,) + ay.shape[1:], lambda v, i, s: (v, 0, 0)),
            pl.BlockSpec((n, WIDE, 128), lambda v, i, s: (v * steps + i, 0, 0)),
        ],
        pl.BlockSpec((n, 128, QUARTER), lambda v, i, s: (v * steps + i, 0, 0)),
        prefetch=1,
        flops=20 << 30,
        moved=20 << 20,
    )(starts, az, ay, blurred)


def back_kernel(spot, ayt, azt, forward, measured, out):
    for i in range(0, forward.shape[0], 2):
        ratios = [measured[j] / forward[j] for j in (i, i + 1)]
        section = dot(ayt[0], stacked(jnp.concatenate(ratios, axis=1), 0))
        section = jnp.concatenate([section[:, :QUARTER], section[:, QUARTER:]], axis=0)
        result = dot_nt(azt[0], stacked(section, 1))
        out[i] = result[:, :128]
        out[i + 1] = result[:, 128:]


def back_of(slot, ayt, azt, forward, measured, spot):
    n = 4
    steps = SLAB // n
    return call(
        back_kernel,
        shape(SLAB, WIDE, 128),
        (steps,),
        [
            pl.BlockSpec((1,) + ayt.shape[1:], lambda i, s: (slot, 0, 0)),
            pl.BlockSpec((1,) + azt.shape[1:], lambda i, s: (slot, 0, 0)),
            pl.BlockSpec((n, 128, QUARTER), lambda i, s: (slot * steps + i, 0, 0)),
            pl.BlockSpec((n, 128, QUARTER), lambda i, s: (i, 0, s[0])),
        ],
        pl.BlockSpec((n, WIDE, 128), lambda i, s: (i, 0, 0)),
        prefetch=1,
        flops=5 << 30,
        moved=7 << 20,
    )(spot, ayt, azt, forward, measured)


def spread_x_kernel(axt, a, b, c, d, below, own, above):
    for z in range(0, a.shape[1], 2):
        columns = [
            jnp.concatenate([ref[:, k, :] for ref in (a, b, c, d)], axis=0) for k in (z, z + 1)
        ]
        result = dot(axt[...], stacked(jnp.concatenate(columns, axis=1), 0))
        for k in (0, 1):
            piece = result[:, k * 128 : (k + 1) * 128]
            below[:, z + k, :] = piece[:LEFT]
            own[:, z + k, :] = piece[LEFT : LEFT + SLAB]
            above[:, z + k, :] = piece[LEFT + SLAB :]


def spread_x(axt, spreads):
    n = 16
    sizes = (LEFT, SLAB, RIGHT)
    return call(
        spread_x_kernel,
        tuple(shape(k, WIDE, 128) for k in sizes),
        (WIDE // n,),
        [pl.BlockSpec(axt.shape, lambda i: (0, 0))]
        + [pl.BlockSpec((SLAB, n, 128), lambda i: (0, i, 0))] * VIEWS,
        tuple(pl.BlockSpec((k, n, 128), lambda i: (0, i, 0)) for k in sizes),
        flops=6 << 30,
        moved=18 << 20,
    )(axt, *spreads)


def finish_kernel(spot, estimate, own, lower, upper, near, far, *refs):
    out = refs[-1]
    q = spot[0]
    for i in range(estimate.shape[0]):
        opposite = jnp.concatenate([near[i], far[i]], axis=0)
        for step, piece in ((0, own[i]), (1, lower[i]), (2, opposite), (3, upper[i])):
            where = lax.rem(q + VIEWS - step, VIEWS)
            lanes = pl.ds(pl.multiple_of(where * QUARTER, QUARTER), QUARTER)
            out[i, :, lanes] = estimate[i, :, lanes] * piece.T / VIEWS


def finish(first, spot, estimate, pieces, before):
    n = 4
    planes = pieces[0].shape[0]
    base = first // n
    wide = pl.BlockSpec((n, 128, VIEWS * QUARTER), lambda i, s: (base + i, 0, 0))
    full = pl.BlockSpec((n, QUARTER, 128), lambda i, s: (i, 0, 0))
    half = pl.BlockSpec((n, QUARTER // 2, 128), lambda i, s: (i, 0, 0))
    specs = [wide, full, full, full, half, half]
    arrays = [spot, estimate, *pieces]
    aliases = {}
    if before is not None:
        specs.append(pl.BlockSpec(memory_space=pl.ANY))
        arrays.append(before)
        aliases = {len(arrays) - 1: 0}
    return call(
        finish_kernel,
        shape(*estimate.shape),
        (planes // n,),
        specs,
        wide,
        prefetch=1,
        aliases=aliases,
        moved=planes * 3 << 18,
    )(*arrays)


def along_blk(x, distance):
    size = lax.axis_size("blk")
    route = [(i, i + distance) for i in range(size) if 0 <= i + distance < size]
    return lax.ppermute(x, "blk", route)


def around_view(x, distance):
    return lax.ppermute(x, "view", [(i, (i + distance) % VIEWS) for i in range(VIEWS)])


def along_view(x, distance):
    route = [(i, i + distance) for i in range(VIEWS) if 0 <= i + distance < VIEWS]
    return lax.ppermute(x, "view", route)


def body(estimate, views, psf, offsets):
    q = lax.axis_index("view")
    spot = q[None]
    zero = jnp.zeros((1,), jnp.int32)
    recorded = views[0]
    kernel = psf[0] / jnp.sum(psf[0], axis=1, keepdims=True)
    mine = jnp.concatenate([kernel, offsets[0].astype(f32)[:, None]], axis=1)
    params = jnp.stack([mine] + [around_view(mine, s) for s in (1, 2, 3)])
    starts = params[:, 2, KERN].astype(jnp.int32)

    measured = {0: recorded}
    for s in (1, 3, 2):
        start = lax.rem(q + s, VIEWS) * QUARTER
        measured[s] = around_view(lax.dynamic_slice_in_dim(recorded, start, QUARTER, 2), s)

    middle = window(estimate, spot)
    upper = along_blk(middle, -1)
    lower = along_blk(middle[SLAB - LEFT :], 1)
    ax, az, ay, ayt, azt, axt = bands(params)
    blurred = blur_x(ax, lower, middle, upper)
    forward = forward_of(starts, az, ay, blurred)
    spreads = [None] * VIEWS
    for s in (0, 1, 3, 2):
        spreads[s] = back_of(s, ayt, azt, forward, measured[s], spot if s == 0 else zero)
    below, own, above = spread_x(axt, spreads)

    out = None
    half = SLAB // 2
    for first in (0, half):
        piece = own[first : first + half] + along_blk(above[first : first + half], 1)
        if first:
            piece = piece + along_blk(below, -1)
        from_right = along_view(piece[:, :LEFT], -1)
        from_left = along_view(piece[:, LEFT + QUARTER :], 1)
        piece = piece[:, LEFT : LEFT + QUARTER]
        piece = piece + jnp.pad(from_right, ((0, 0), (QUARTER - LEFT, 0), (0, 0)))
        piece = piece + jnp.pad(from_left, ((0, 0), (0, QUARTER - RIGHT), (0, 0)))
        left = around_view(piece, 1)
        right = around_view(piece, 3)
        near = around_view(left[:, : QUARTER // 2], 1)
        far = around_view(right[:, QUARTER // 2 :], 3)
        out = finish(first, spot, estimate, (piece, left, right, near, far), out)
    return out


def solution(mesh):
    placed = (
        P("blk", None, None),
        P("view", "blk", None, None),
        P("view", None, None),
        P("view", None),
    )
    return jax.shard_map(
        body, mesh=mesh, in_specs=placed, out_specs=P("blk", None, None), check_vma=False
    )
```

time: 554 us -> 286 us (0.52); the launches traced: 545 us -> 283 us
  waiting for transfers between devices: 298 us -> 106 us
  matrix products: 165 us -> 0 us
  Pallas kernels: 0 us -> 120 us
  other arithmetic: 34 us -> 1.45 us
  starting transfers between devices: 12.1 us -> 42 us
  between operations: 13.7 us -> 0.33 us
  local copies, waits for them, and re-layouts: 22 us -> 13.7 us
    dot_general x9 -> x0, matrix products: 165 us -> none  [the longest x1 37.1 us: across(): jnp.einsum('ryk,pk->ryp', section, band_z, precision=lax.Precision.HIGHEST)]
    psum x1 -> x0, waiting for transfers between devices: 161 us -> none  [body(): correction = lax.psum(spill(spread_back, slab_rows), 'view')]
    pallas_call x0 -> x11, Pallas kernels: none -> 120 us  [the longest x1 30.5 us: forward_of(): call(forward_kernel, shape(VIEWS * SLAB, 128, QUARTER), (VIEWS, steps), [...]
    ppermute x4 -> x23, waiting for transfers between devices: 137 us -> 106 us  [the longest x14 68 us: around_view(): lax.ppermute(x, 'view', [(i, (i + distance) % VIEWS) for i in range(VIEWS)])]
    ppermute x4 -> x23, starting transfers between devices: 12.1 us -> 42 us  [the longest x5 17.2 us: along_blk(): return lax.ppermute(x, 'blk', route)]
    div x1 -> x0, other arithmetic: 14.9 us -> none  [body(): return estimate * correction / view_count]
    div x1 -> x0, local copies, waits for them, and re-layouts: 11.6 us -> none  [body(): return estimate * correction / view_count]
    add x4 -> x3, other arithmetic: 10.2 us -> 0.67 us  [the longest x1 0.46 us: body(): piece = own[first:first + half] + along_blk(above[first:first + half], 1)]
  transfers between devices with their start and end apart: 5 -> 23, of which waited for: 5 -> 14; matrix products, arithmetic and copies ran while one was open for 7% -> 4% of each run, Pallas kernels for 0% -> 30%
where the time goes in v1:
time: 286 us; the launch traced here: 283 us
  Pallas kernels  120 us (42%)
  waiting for transfers between devices  106 us (37%)
  starting transfers between devices  42 us (15%)
  local copies, waits for them, and re-layouts  13.7 us (5%)
    ppermute x14, waiting for transfers between devices, around_view(): lax.ppermute(x, 'view', [(i, (i + distance) % VIEWS) for i in range(VIEWS)])  68 us
    ppermute x5, waiting for transfers between devices, along_blk(): return lax.ppermute(x, 'blk', route)  32.5 us
    pallas_call x1, Pallas kernels, forward_of(): call(forward_kernel, shape(VIEWS * SLAB, 128, QUARTER), (VIEWS, steps), [...  30.5 us
    pallas_call x4, Pallas kernels, back_of(): call(back_kernel, shape(SLAB, WIDE, 128), (steps,), [pl.BlockSpec((1,) +...  30.3 us
    ppermute x5, starting transfers between devices, along_blk(): return lax.ppermute(x, 'blk', route)  17.2 us
    pallas_call x1, Pallas kernels, blur_x(): call(blur_x_kernel, shape(VIEWS * SLAB, WIDE, 128), (WIDE // n,), [pl.Blo...  15.3 us
    pallas_call x1, Pallas kernels, spread_x(): call(spread_x_kernel, tuple((shape(k, WIDE, 128) for k in sizes)), (WIDE...  15.1 us
    ppermute x14, starting transfers between devices, around_view(): lax.ppermute(x, 'view', [(i, (i + distance) % VIEWS) for i in range(VIEWS)])  14.2 us
  transfers between devices with their start and end apart: 23, of which 14 were waited for; matrix products, arithmetic and copies ran while one was open for 4% of the time, Pallas kernels for 30%

profile of v1, /device:TPU:59, one launch (start us, length us, event | category | flops | bytes accessed | tf_op | source)
XLA Modules:
  0.0 283.3 jit_solution(1369401313848599525)
XLA Ops:
  0.0 6.0 %shard_map.47.middle = f32[32,176,128]{2,1,0:T(8,128)S(1)} custom-call(s32[1]{0:T(128)} %bitcast.spot, f32[32,128,512]{2,1,0:T(8,128)} %estimate.3, f32[32,128,512]{2,1,0:T(8,128)} %estimate.3, f32[32,128,512]{2,1,0:T(8,128)} %estimate.3), custom_call_target="tpu_custom_call" | custom-call | bytes 9437184 | tf_op jit(solution)/shard_map/pallas_call | solution.py:159
  6.1 2.6 collective-permute-start.4
  8.7 1.2 slice.65
  9.9 5.1 %collective-permute-start.3 = (f32[16,176,128]{2,1,0:T(8,128)}, f32[16,176,128]{2,1,0:T(8,128)}, u32[]{:S(2)}, u32[]{:S(2)}) collective-permute-start(f32[16,176,128]{2,1,0:T(8,128)} %slice.65), channel_id=1, source_target_pairs={{0,1},{1,2},{2,3},{3,4},{4,5},{5,6},{6,7},{7,8},{8,9},{9,10},{10,1... | collective-permute-start | bytes 4325384 | tf_op jit(solution)/shard_map/ppermute | solution.py:334
  15.3 1.9 collective-permute-start.1
  17.2 1.5 collective-permute-start.2
  18.7 5.5 %dynamic-slice_bitcast_fusion = (f32[32,128,128]{2,1,0:T(8,128)}, f32[32,128,128]{2,1,0:T(8,128)S(1)}, f32[32,128,128]{2,1,0:T(8,128)}) fusion(f32[1,32,128,512]{3,2,1,0:T(8,128)} %param.5, s32[]{:T(128)S(6)} %select_n.11, s32[]{:T(128)S(6)} %select_n.9, s32[]{:T(128)S(6)} %select_n.10), kind=kLoop, calls=%fused_computation | loop fusion | bytes 12582924 | tf_op jit(solution)/shard_map/dynamic_slice | solution.py:359
  24.3 2.4 collective-permute-start.7
  26.6 1.9 collective-permute-start.6
  28.5 12.0 %shard_map.46 = (bf16[128,256]{1,0:T(8,128)(2,1)S(1)}, bf16[4,128,512]{2,1,0:T(8,128)(2,1)S(1)}, bf16[4,128,384]{2,1,0:T(8,128)(2,1)S(1)}, bf16[4,128,384]{2,1,0...) custom-call(f32[4,3,34]{2,1,0:T(4,128)S(1)} %pad_maximum_fusion.params), custom_call_target="tpu_custom_call" | custom-call | tf_op jit(solution)/shard_map/pallas_call | solution.py:130
  41.0 3.1 %collective-permute-done.4.upper = f32[32,176,128]{2,1,0:T(8,128)} collective-permute-done((f32[32,176,128]{2,1,0:T(8,128)S(1)}, f32[32,176,128]{2,1,0:T(8,128)}, u32[]{:S(2)}, u32[]{:S(2)}) %collective-permute-start.4) | collective-permute-done | bytes 2883616 | tf_op jit(solution)/shard_map/ppermute | solution.py:334
  44.1 15.3 %shard_map.48.blurred = f32[128,176,128]{2,1,0:T(8,128)} custom-call(bf16[128,256]{1,0:T(8,128)(2,1)S(1)} %get-tuple-element.19.ax, f32[16,176,128]{2,1,0:T(8,128)} %collective-permute-done.3.lower, f32[32,176,128]{2,1,0:T(8,128)S(1)} %shard_map.47.middle, f32[32,176,128]{2,1,0:T(8,128)} %collective-permute-done.4.upper), custom_call_target="tpu_custom_call" | custom-call | flops 6442450944 | bytes 18874368 | tf_op jit(solution)/shard_map/pallas_call | solution.py:188
  59.4 30.5 %shard_map.49.forward = f32[128,128,128]{2,1,0:T(8,128)} custom-call(s32[4]{0:T(128)S(1)} %fusion.2.starts, bf16[4,128,512]{2,1,0:T(8,128)(2,1)S(1)} %get-tuple-element.17.az, bf16[4,128,384]{2,1,0:T(8,128)(2,1)S(1)} %get-tuple-element.18.ay, f32[128,176,128]{2,1,0:T(8,128)} %shard_map.48.blurred), custom_call_target="tpu_custom_call" | custom-call | flops 21474836480 | bytes 20971520 | tf_op jit(solution)/shard_map/pallas_call | solution.py:220
  89.9 7.8 %shard_map.50.a = f32[32,176,128]{2,1,0:T(8,128)S(1)} custom-call(s32[1]{0:T(128)} %bitcast.spot, bf16[4,128,384]{2,1,0:T(8,128)(2,1)S(1)} %get-tuple-element.15.ayt, bf16[4,176,384]{2,1,0:T(8,128)(2,1)S(1)} %get-tuple-element.16.azt, f32[128,128,128]{2,1,0:T(8,128)} %shard_map.49.forward, f32[32,128,512]{2,1,0:T(8,128)} %bitcast.17), custom_call_target="tpu_custom_call" | custom-call | flops 5368709120 | bytes 7340032 | tf_op jit(solution)/shard_map/pallas_call | solution.py:249
  97.7 1.5 copy-done
  99.2 16.2 %collective-permute-done.7.measured = f32[32,128,128]{2,1,0:T(8,128)S(1)} collective-permute-done((f32[32,128,128]{2,1,0:T(8,128)}, f32[32,128,128]{2,1,0:T(8,128)S(1)}, u32[]{:S(2)}, u32[]{:S(2)}) %collective-permute-start.7) | collective-permute-done | bytes 2097184 | tf_op jit(solution)/shard_map/ppermute | solution.py:338
  115.4 7.4 %shard_map.53.d = f32[32,176,128]{2,1,0:T(8,128)S(1)} custom-call(s32[1]{0:T(128)} %constant.26.clone.1.spot, bf16[4,128,384]{2,1,0:T(8,128)(2,1)S(1)} %get-tuple-element.15.ayt, bf16[4,176,384]{2,1,0:T(8,128)(2,1)S(1)} %get-tuple-element.16.azt, f32[128,128,128]{2,1,0:T(8,128)} %shard_map.49.forward, f32[32,128,128]{2,1,0:T(8,128)S(1)} %collective-permute-done.7.measured), custom_call_target="tpu_custom_call" | custom-call | flops 5368709120 | bytes 7340032 | tf_op jit(solution)/shard_map/pallas_call | solution.py:249
  122.9 7.6 %shard_map.51.b = f32[32,176,128]{2,1,0:T(8,128)S(1)} custom-call(s32[1]{0:T(128)} %constant.26.clone.1.spot, bf16[4,128,384]{2,1,0:T(8,128)(2,1)S(1)} %get-tuple-element.15.ayt, bf16[4,176,384]{2,1,0:T(8,128)(2,1)S(1)} %get-tuple-element.16.azt, f32[128,128,128]{2,1,0:T(8,128)} %shard_map.49.forward, f32[32,128,128]{2,1,0:T(8,128)S(1)} %collective-permute-done.5.measured), custom_call_target="tpu_custom_call" | custom-call | flops 5368709120 | bytes 7340032 | tf_op jit(solution)/shard_map/pallas_call | solution.py:249
  130.5 1.6 copy-done.2
  132.1 7.4 %shard_map.52.c = f32[32,176,128]{2,1,0:T(8,128)S(1)} custom-call(s32[1]{0:T(128)} %constant.26.clone.1.spot, bf16[4,128,384]{2,1,0:T(8,128)(2,1)S(1)} %get-tuple-element.15.ayt, bf16[4,176,384]{2,1,0:T(8,128)(2,1)S(1)} %get-tuple-element.16.azt, f32[128,128,128]{2,1,0:T(8,128)} %shard_map.49.forward, f32[32,128,128]{2,1,0:T(8,128)S(1)} %collective-permute-done.6.measured), custom_call_target="tpu_custom_call" | custom-call | flops 5368709120 | bytes 7340032 | tf_op jit(solution)/shard_map/pallas_call | solution.py:249
  139.6 1.6 copy-done.3
  141.1 15.1 %shard_map.54 = (f32[16,176,128]{2,1,0:T(8,128)S(1)}, f32[32,176,128]{2,1,0:T(8,128)S(1)}, f32[32,176,128]{2,1,0:T(8,128)}) custom-call(bf16[80,384]{1,0:T(8,128)(2,1)S(1)} %get-tuple-element.14.axt, f32[32,176,128]{2,1,0:T(8,128)} %copy-done, f32[32,176,128]{2,1,0:T(8,128)} %copy-done.2, f32[32,176,128]{2,1,0:T(8,128)} %copy-done.3, f32[32,176,128]{2,1,0:T(8,128)} %copy-done.1), custom_call_target="tpu_custom_call" | custom-call | flops 6442450944 | bytes 18874368 | tf_op jit(solution)/shard_map/pallas_call | solution.py:282
  156.3 1.9 collective-permute-start.9
  158.2 2.0 fusion.3
  160.2 5.8 %collective-permute-start.16 = (f32[16,176,128]{2,1,0:T(8,128)S(1)}, f32[16,176,128]{2,1,0:T(8,128)S(1)}, u32[]{:S(2)}, u32[]{:S(2)}) collective-permute-start(f32[16,176,128]{2,1,0:T(8,128)S(1)} %get-tuple-element.28), channel_id=1, source_target_pairs={{0,1},{1,2},{2,3},{3,4},{4,5},{5,6},{6,7},{7,8},{8,9},{9,10},{10,1... | collective-permute-start | bytes 4325384 | tf_op jit(solution)/shard_map/ppermute | solution.py:334
  165.9 1.9 collective-permute-start.8
  167.9 10.8 %collective-permute-done.9 = f32[16,176,128]{2,1,0:T(8,128)S(1)} collective-permute-done((f32[16,176,128]{2,1,0:T(8,128)S(1)}, f32[16,176,128]{2,1,0:T(8,128)S(1)}, u32[]{:S(2)}, u32[]{:S(2)}) %collective-permute-start.9) | collective-permute-done | bytes 1441824 | tf_op jit(solution)/shard_map/ppermute | solution.py:334
  178.7 3.2 %collective-permute-done.16 = f32[16,176,128]{2,1,0:T(8,128)S(1)} collective-permute-done((f32[16,176,128]{2,1,0:T(8,128)S(1)}, f32[16,176,128]{2,1,0:T(8,128)S(1)}, u32[]{:S(2)}, u32[]{:S(2)}) %collective-permute-start.16) | collective-permute-done | bytes 1441824 | tf_op jit(solution)/shard_map/ppermute | solution.py:334
  181.9 15.4 %collective-permute-done.8 = f32[16,176,128]{2,1,0:T(8,128)S(1)} collective-permute-done((f32[16,176,128]{2,1,0:T(8,128)S(1)}, f32[16,176,128]{2,1,0:T(8,128)S(1)}, u32[]{:S(2)}, u32[]{:S(2)}) %collective-permute-start.8) | collective-permute-done | bytes 1441824 | tf_op jit(solution)/shard_map/ppermute | solution.py:334
  197.8 1.9 collective-permute-start.18
  199.8 3.4 %collective-permute-start.17 = (f32[16,16,128]{2,1,0:T(8,128)S(1)}, f32[16,16,128]{2,1,0:T(8,128)S(1)}, u32[]{:S(2)}, u32[]{:S(2)}) collective-permute-start(f32[16,16,128]{2,1,0:T(8,128)S(1)} %slice.72), channel_id=1, source_target_pairs={{32,0},{64,32},{96,64},{33,1},{65,33},{97,65},{34,2},{66,34},{98,6... | collective-permute-start | bytes 393224 | tf_op jit(solution)/shard_map/ppermute | solution.py:343
  203.2 1.9 collective-permute-start.10
  205.1 3.4 %collective-permute-start.11 = (f32[16,32,128]{2,1,0:T(8,128)S(1)}, f32[16,32,128]{2,1,0:T(8,128)S(1)}, u32[]{:S(2)}, u32[]{:S(2)}) collective-permute-start(f32[16,32,128]{2,1,0:T(8,128)S(1)} %slice.68), channel_id=1, source_target_pairs={{0,32},{32,64},{64,96},{1,33},{33,65},{65,97},{2,34},{34,66},{66,9... | collective-permute-start | bytes 786440 | tf_op jit(solution)/shard_map/ppermute | solution.py:343
  208.9 1.3 collective-permute-start.19
  210.2 0.5 collective-permute-done.10
  210.7 4.7 %collective-permute-done.11 = f32[16,32,128]{2,1,0:T(8,128)S(1)} collective-permute-done((f32[16,32,128]{2,1,0:T(8,128)S(1)}, f32[16,32,128]{2,1,0:T(8,128)S(1)}, u32[]{:S(2)}, u32[]{:S(2)}) %collective-permute-start.11) | collective-permute-done | bytes 262176 | tf_op jit(solution)/shard_map/ppermute | solution.py:343
  215.6 1.5 collective-permute-start.12
  217.1 16.8 %collective-permute-done.20.upper = f32[16,128,128]{2,1,0:T(8,128)S(1)} collective-permute-done((f32[16,128,128]{2,1,0:T(8,128)S(1)}, f32[16,128,128]{2,1,0:T(8,128)S(1)}, u32[]{:S(2)}, u32[]{:S(2)}) %collective-permute-start.20) | collective-permute-done | bytes 1048608 | tf_op jit(solution)/shard_map/ppermute | solution.py:338
  234.2 3.7 %collective-permute-done.19.lower = f32[16,128,128]{2,1,0:T(8,128)S(1)} collective-permute-done((f32[16,128,128]{2,1,0:T(8,128)S(1)}, f32[16,128,128]{2,1,0:T(8,128)S(1)}, u32[]{:S(2)}, u32[]{:S(2)}) %collective-permute-start.19) | collective-permute-done | bytes 1048608 | tf_op jit(solution)/shard_map/ppermute | solution.py:338
  237.9 1.5 collective-permute-start.21
  239.4 17.0 %collective-permute-done.13.upper = f32[16,128,128]{2,1,0:T(8,128)S(1)} collective-permute-done((f32[16,128,128]{2,1,0:T(8,128)S(1)}, f32[16,128,128]{2,1,0:T(8,128)S(1)}, u32[]{:S(2)}, u32[]{:S(2)}) %collective-permute-start.13) | collective-permute-done | bytes 1048608 | tf_op jit(solution)/shard_map/ppermute | solution.py:338
  256.7 3.6 %collective-permute-done.12.lower = f32[16,128,128]{2,1,0:T(8,128)S(1)} collective-permute-done((f32[16,128,128]{2,1,0:T(8,128)S(1)}, f32[16,128,128]{2,1,0:T(8,128)S(1)}, u32[]{:S(2)}, u32[]{:S(2)}) %collective-permute-start.12) | collective-permute-done | bytes 1048608 | tf_op jit(solution)/shard_map/ppermute | solution.py:338
  260.4 1.5 collective-permute-start.14
  261.9 5.7 %collective-permute-done.22.far = f32[16,64,128]{2,1,0:T(8,128)S(1)} collective-permute-done((f32[16,64,128]{2,1,0:T(8,128)S(1)}, f32[16,64,128]{2,1,0:T(8,128)S(1)}, u32[]{:S(2)}, u32[]{:S(2)}) %collective-permute-start.22) | collective-permute-done | bytes 524320 | tf_op jit(solution)/shard_map/ppermute | solution.py:338
  267.6 3.9 %collective-permute-done.21.near = f32[16,64,128]{2,1,0:T(8,128)S(1)} collective-permute-done((f32[16,64,128]{2,1,0:T(8,128)S(1)}, f32[16,64,128]{2,1,0:T(8,128)S(1)}, u32[]{:S(2)}, u32[]{:S(2)}) %collective-permute-start.21) | collective-permute-done | bytes 524320 | tf_op jit(solution)/shard_map/ppermute | solution.py:338
  271.6 5.3 %shard_map.55.refs_0_ = f32[32,128,512]{2,1,0:T(8,128)} custom-call(s32[1]{0:T(128)} %bitcast.spot, f32[32,128,512]{2,1,0:T(8,128)} %estimate.3, f32[16,128,128]{2,1,0:T(8,128)S(1)} %fusion.own, f32[16,128,128]{2,1,0:T(8,128)S(1)} %collective-permute-done.19.lower, f32[16,128,128]{2,1,0:T(8,128)S(1)} %collective-permute-done.20.upper, ...), custom_call_target="tpu_custom_call" | custom-call | bytes 12582912 | tf_op jit(solution)/shard_map/pallas_call | solution.py:319
  276.9 1.1 collective-permute-done.14.near
  278.0 5.3 %shard_map.56 = f32[32,128,512]{2,1,0:T(8,128)} custom-call(s32[1]{0:T(128)} %bitcast.spot, f32[32,128,512]{2,1,0:T(8,128)} %estimate.3, f32[16,128,128]{2,1,0:T(8,128)S(1)} %fusion.1.own, f32[16,128,128]{2,1,0:T(8,128)S(1)} %collective-permute-done.12.lower, f32[16,128,128]{2,1,0:T(8,128)S(1)} %collective-permute-done.13.upper, ...), custom_call_target="tpu_custom_call", output_to_operand_aliasing={{}: (7, {})} | custom-call | bytes 12582912 | tf_op jit(solution)/shard_map/pallas_call | solution.py:319
  (43 shorter events, 2.6 us)
Async XLA Ops:
  6.0 8.9 %copy-start.5 = (s32[1,3]{1,0:T(1,128)S(1)}, s32[1,3]{1,0:T(1,128)}, u32[]{:S(2)}) copy-start(s32[1,3]{1,0:T(1,128)} %param.7) | copy-start | bytes 40
  6.1 9.0 %copy-start.4 = (f32[1,3,33]{2,0,1:T(1,128)S(1)}, f32[1,3,33]{2,0,1:T(1,128)}, u32[]{:S(2)}) copy-start(f32[1,3,33]{2,0,1:T(1,128)} %param.6) | copy-start | bytes 1192
  6.1 38.0 %collective-permute-start.4 = (f32[32,176,128]{2,1,0:T(8,128)S(1)}, f32[32,176,128]{2,1,0:T(8,128)}, u32[]{:S(2)}, u32[]{:S(2)}) collective-permute-start(f32[32,176,128]{2,1,0:T(8,128)S(1)} %shard_map.47.middle), channel_id=1, source_target_pairs={{1,0},{2,1},{3,2},{4,3},{5,4},{6,5},{7,6},{8,7},{9,8},{10,9},{11,1... | collective-permute-start | bytes 8650760 | tf_op jit(solution)/shard_map/ppermute | solution.py:334
  9.9 31.1 %collective-permute-start.3 = (f32[16,176,128]{2,1,0:T(8,128)}, f32[16,176,128]{2,1,0:T(8,128)}, u32[]{:S(2)}, u32[]{:S(2)}) collective-permute-start(f32[16,176,128]{2,1,0:T(8,128)} %slice.65), channel_id=1, source_target_pairs={{0,1},{1,2},{2,3},{3,4},{4,5},{5,6},{6,7},{7,8},{8,9},{9,10},{10,1... | collective-permute-start | bytes 4325384 | tf_op jit(solution)/shard_map/ppermute | solution.py:334
  15.3 8.9 %collective-permute-start.1 = (f32[3,34]{1,0:T(4,128)S(1)}, f32[3,34]{1,0:T(4,128)S(1)}, u32[]{:S(2)}, u32[]{:S(2)}) collective-permute-start(f32[3,34]{1,0:T(4,128)S(1)} %pad_maximum_fusion.1), channel_id=1, source_target_pairs={{0,64},{32,96},{64,0},{96,32},{1,65},{33,97},{65,1},{97,33},{2,66}... | collective-permute-start | bytes 1232 | tf_op jit(solution)/shard_map/ppermute | solution.py:338
  17.2 9.4 %collective-permute-start = (f32[3,34]{1,0:T(4,128)S(1)}, f32[3,34]{1,0:T(4,128)S(1)}, u32[]{:S(2)}, u32[]{:S(2)}) collective-permute-start(f32[3,34]{1,0:T(4,128)S(1)} %pad_maximum_fusion.1), channel_id=1, source_target_pairs={{0,32},{32,64},{64,96},{96,0},{1,33},{33,65},{65,97},{97,1},{2,34}... | collective-permute-start | bytes 1232 | tf_op jit(solution)/shard_map/ppermute | solution.py:338
  17.2 9.4 %collective-permute-start.2 = (f32[3,34]{1,0:T(4,128)S(1)}, f32[3,34]{1,0:T(4,128)S(1)}, u32[]{:S(2)}, u32[]{:S(2)}) collective-permute-start(f32[3,34]{1,0:T(4,128)S(1)} %pad_maximum_fusion.1), channel_id=1, source_target_pairs={{0,96},{32,0},{64,32},{96,64},{1,97},{33,1},{65,33},{97,65},{2,98}... | collective-permute-start | bytes 1232 | tf_op jit(solution)/shard_map/ppermute | solution.py:338
  24.3 91.1 %collective-permute-start.7 = (f32[32,128,128]{2,1,0:T(8,128)}, f32[32,128,128]{2,1,0:T(8,128)S(1)}, u32[]{:S(2)}, u32[]{:S(2)}) collective-permute-start(f32[32,128,128]{2,1,0:T(8,128)} %get-tuple-element.23), channel_id=1, source_target_pairs={{0,96},{32,0},{64,32},{96,64},{1,97},{33,1},{65,33},{97,65},{2,98}... | collective-permute-start | bytes 6291464 | tf_op jit(solution)/shard_map/ppermute | solution.py:338
  26.6 96.2 %collective-permute-start.5 = (f32[32,128,128]{2,1,0:T(8,128)S(1)}, f32[32,128,128]{2,1,0:T(8,128)S(1)}, u32[]{:S(2)}, u32[]{:S(2)}) collective-permute-start(f32[32,128,128]{2,1,0:T(8,128)S(1)} %get-tuple-element.24), channel_id=1, source_target_pairs={{0,32},{32,64},{64,96},{96,0},{1,33},{33,65},{65,97},{97,1},{2,34}... | collective-permute-start | bytes 6291464 | tf_op jit(solution)/shard_map/ppermute | solution.py:338
  26.6 105.5 %collective-permute-start.6 = (f32[32,128,128]{2,1,0:T(8,128)}, f32[32,128,128]{2,1,0:T(8,128)S(1)}, u32[]{:S(2)}, u32[]{:S(2)}) collective-permute-start(f32[32,128,128]{2,1,0:T(8,128)} %get-tuple-element.25), channel_id=1, source_target_pairs={{0,64},{32,96},{64,0},{96,32},{1,65},{33,97},{65,1},{97,33},{2,66}... | collective-permute-start | bytes 6291464 | tf_op jit(solution)/shard_map/ppermute | solution.py:338
  97.7 1.5 copy-start
  122.8 7.7 %copy-start.1 = (f32[32,176,128]{2,1,0:T(8,128)}, f32[32,176,128]{2,1,0:T(8,128)S(1)}, u32[]{:S(2)}) copy-start(f32[32,176,128]{2,1,0:T(8,128)S(1)} %shard_map.53.d) | copy-start | bytes 8650756
  130.5 1.6 copy-start.2
  139.6 1.6 copy-start.3
  156.3 22.4 %collective-permute-start.9 = (f32[16,176,128]{2,1,0:T(8,128)S(1)}, f32[16,176,128]{2,1,0:T(8,128)S(1)}, u32[]{:S(2)}, u32[]{:S(2)}) collective-permute-start(f32[16,176,128]{2,1,0:T(8,128)S(1)} %get-tuple-element.22), channel_id=1, source_target_pairs={{1,0},{2,1},{3,2},{4,3},{5,4},{6,5},{7,6},{8,7},{9,8},{10,9},{11,1... | collective-permute-start | bytes 4325384 | tf_op jit(solution)/shard_map/ppermute | solution.py:334
  160.2 21.7 %collective-permute-start.16 = (f32[16,176,128]{2,1,0:T(8,128)S(1)}, f32[16,176,128]{2,1,0:T(8,128)S(1)}, u32[]{:S(2)}, u32[]{:S(2)}) collective-permute-start(f32[16,176,128]{2,1,0:T(8,128)S(1)} %get-tuple-element.28), channel_id=1, source_target_pairs={{0,1},{1,2},{2,3},{3,4},{4,5},{5,6},{6,7},{7,8},{8,9},{9,10},{10,1... | collective-permute-start | bytes 4325384 | tf_op jit(solution)/shard_map/ppermute | solution.py:334
  165.9 31.4 %collective-permute-start.8 = (f32[16,176,128]{2,1,0:T(8,128)S(1)}, f32[16,176,128]{2,1,0:T(8,128)S(1)}, u32[]{:S(2)}, u32[]{:S(2)}) collective-permute-start(f32[16,176,128]{2,1,0:T(8,128)S(1)} %get-tuple-element.29), channel_id=1, source_target_pairs={{0,1},{1,2},{2,3},{3,4},{4,5},{5,6},{6,7},{7,8},{8,9},{9,10},{10,1... | collective-permute-start | bytes 4325384 | tf_op jit(solution)/shard_map/ppermute | solution.py:334
  197.8 10.7 %collective-permute-start.18 = (f32[16,32,128]{2,1,0:T(8,128)S(1)}, f32[16,32,128]{2,1,0:T(8,128)S(1)}, u32[]{:S(2)}, u32[]{:S(2)}) collective-permute-start(f32[16,32,128]{2,1,0:T(8,128)S(1)} %slice.73), channel_id=1, source_target_pairs={{0,32},{32,64},{64,96},{1,33},{33,65},{65,97},{2,34},{34,66},{66,9... | collective-permute-start | bytes 786440 | tf_op jit(solution)/shard_map/ppermute | solution.py:343
  199.8 8.7 %collective-permute-start.17 = (f32[16,16,128]{2,1,0:T(8,128)S(1)}, f32[16,16,128]{2,1,0:T(8,128)S(1)}, u32[]{:S(2)}, u32[]{:S(2)}) collective-permute-start(f32[16,16,128]{2,1,0:T(8,128)S(1)} %slice.72), channel_id=1, source_target_pairs={{32,0},{64,32},{96,64},{33,1},{65,33},{97,65},{34,2},{66,34},{98,6... | collective-permute-start | bytes 393224 | tf_op jit(solution)/shard_map/ppermute | solution.py:343
  203.2 7.5 %collective-permute-start.10 = (f32[16,16,128]{2,1,0:T(8,128)S(1)}, f32[16,16,128]{2,1,0:T(8,128)S(1)}, u32[]{:S(2)}, u32[]{:S(2)}) collective-permute-start(f32[16,16,128]{2,1,0:T(8,128)S(1)} %slice.67), channel_id=1, source_target_pairs={{32,0},{64,32},{96,64},{33,1},{65,33},{97,65},{34,2},{66,34},{98,6... | collective-permute-start | bytes 393224 | tf_op jit(solution)/shard_map/ppermute | solution.py:343
  205.1 10.3 %collective-permute-start.11 = (f32[16,32,128]{2,1,0:T(8,128)S(1)}, f32[16,32,128]{2,1,0:T(8,128)S(1)}, u32[]{:S(2)}, u32[]{:S(2)}) collective-permute-start(f32[16,32,128]{2,1,0:T(8,128)S(1)} %slice.68), channel_id=1, source_target_pairs={{0,32},{32,64},{64,96},{1,33},{33,65},{65,97},{2,34},{34,66},{66,9... | collective-permute-start | bytes 786440 | tf_op jit(solution)/shard_map/ppermute | solution.py:343
  208.6 25.3 %collective-permute-start.20 = (f32[16,128,128]{2,1,0:T(8,128)S(1)}, f32[16,128,128]{2,1,0:T(8,128)S(1)}, u32[]{:S(2)}, u32[]{:S(2)}) collective-permute-start(f32[16,128,128]{2,1,0:T(8,128)S(1)} %fusion.own), channel_id=1, source_target_pairs={{0,96},{32,0},{64,32},{96,64},{1,97},{33,1},{65,33},{97,65},{2,98}... | collective-permute-start | bytes 3145736 | tf_op jit(solution)/shard_map/ppermute | solution.py:338
  208.9 29.0 %collective-permute-start.19 = (f32[16,128,128]{2,1,0:T(8,128)S(1)}, f32[16,128,128]{2,1,0:T(8,128)S(1)}, u32[]{:S(2)}, u32[]{:S(2)}) collective-permute-start(f32[16,128,128]{2,1,0:T(8,128)S(1)} %fusion.own), channel_id=1, source_target_pairs={{0,32},{32,64},{64,96},{96,0},{1,33},{33,65},{65,97},{97,1},{2,34}... | collective-permute-start | bytes 3145736 | tf_op jit(solution)/shard_map/ppermute | solution.py:338
  215.5 40.9 %collective-permute-start.13 = (f32[16,128,128]{2,1,0:T(8,128)S(1)}, f32[16,128,128]{2,1,0:T(8,128)S(1)}, u32[]{:S(2)}, u32[]{:S(2)}) collective-permute-start(f32[16,128,128]{2,1,0:T(8,128)S(1)} %fusion.1.own), channel_id=1, source_target_pairs={{0,96},{32,0},{64,32},{96,64},{1,97},{33,1},{65,33},{97,65},{2,98}... | collective-permute-start | bytes 3145736 | tf_op jit(solution)/shard_map/ppermute | solution.py:338
  215.6 44.7 %collective-permute-start.12 = (f32[16,128,128]{2,1,0:T(8,128)S(1)}, f32[16,128,128]{2,1,0:T(8,128)S(1)}, u32[]{:S(2)}, u32[]{:S(2)}) collective-permute-start(f32[16,128,128]{2,1,0:T(8,128)S(1)} %fusion.1.own), channel_id=1, source_target_pairs={{0,32},{32,64},{64,96},{96,0},{1,33},{33,65},{65,97},{97,1},{2,34}... | collective-permute-start | bytes 3145736 | tf_op jit(solution)/shard_map/ppermute | solution.py:338
  234.0 33.7 %collective-permute-start.22 = (f32[16,64,128]{2,1,0:T(8,128)S(1)}, f32[16,64,128]{2,1,0:T(8,128)S(1)}, u32[]{:S(2)}, u32[]{:S(2)}) collective-permute-start(f32[16,64,128]{2,1,0:T(8,128)S(1)} %slice.75), channel_id=1, source_target_pairs={{0,96},{32,0},{64,32},{96,64},{1,97},{33,1},{65,33},{97,65},{2,98}... | collective-permute-start | bytes 1572872 | tf_op jit(solution)/shard_map/ppermute | solution.py:338
  237.9 33.7 %collective-permute-start.21 = (f32[16,64,128]{2,1,0:T(8,128)S(1)}, f32[16,64,128]{2,1,0:T(8,128)S(1)}, u32[]{:S(2)}, u32[]{:S(2)}) collective-permute-start(f32[16,64,128]{2,1,0:T(8,128)S(1)} %slice.74), channel_id=1, source_target_pairs={{0,32},{32,64},{64,96},{96,0},{1,33},{33,65},{65,97},{97,1},{2,34}... | collective-permute-start | bytes 1572872 | tf_op jit(solution)/shard_map/ppermute | solution.py:338
  256.5 20.4 %collective-permute-start.15 = (f32[16,64,128]{2,1,0:T(8,128)S(1)}, f32[16,64,128]{2,1,0:T(8,128)S(1)}, u32[]{:S(2)}, u32[]{:S(2)}) collective-permute-start(f32[16,64,128]{2,1,0:T(8,128)S(1)} %slice.70), channel_id=1, source_target_pairs={{0,96},{32,0},{64,32},{96,64},{1,97},{33,1},{65,33},{97,65},{2,98}... | collective-permute-start | bytes 1572872 | tf_op jit(solution)/shard_map/ppermute | solution.py:338
  260.4 17.6 %collective-permute-start.14 = (f32[16,64,128]{2,1,0:T(8,128)S(1)}, f32[16,64,128]{2,1,0:T(8,128)S(1)}, u32[]{:S(2)}, u32[]{:S(2)}) collective-permute-start(f32[16,64,128]{2,1,0:T(8,128)S(1)} %slice.69), channel_id=1, source_target_pairs={{0,32},{32,64},{64,96},{96,0},{1,33},{33,65},{65,97},{97,1},{2,34}... | collective-permute-start | bytes 1572872 | tf_op jit(solution)/shard_map/ppermute | solution.py:338

commit v2 on v0

v2 whole, which is shorter than its diff:
```python
import jax
import jax.numpy as jnp
from jax import lax
from jax.experimental import pallas as pl
from jax.experimental.pallas import tpu as pltpu
from jax.sharding import PartitionSpec as P

RADIUS = 16
KERN = 33
LEFT = RADIUS
RIGHT = 2 * RADIUS
QUARTER = 128
WIDE = LEFT + QUARTER + RIGHT
SLAB = 32
TALL = LEFT + SLAB + RIGHT
VIEWS = 4
BACKGROUND = 0.1
ALL = (0, 1, 3, 2)
ROWS = 64
PACKED = ROWS // 2
CHUNK = ROWS + PACKED
CUT = 80
ODD = WIDE + 1
SKEW = CHUNK + 1
FREE = 1 << 10
LONG = 1 << 38
SPANS = ((0, 80), (32, 128))
VMEM = 48 * 1024 * 1024

f32 = jnp.float32
bf16 = jnp.bfloat16


def call(kernel, out_shape, grid, in_specs, out_specs, prefetch=0, aliases=None, flops=0, moved=0):
    return pl.pallas_call(
        kernel,
        out_shape=out_shape,
        grid_spec=pltpu.PrefetchScalarGridSpec(
            num_scalar_prefetch=prefetch, grid=grid, in_specs=in_specs, out_specs=out_specs
        ),
        input_output_aliases=aliases or {},
        compiler_params=pltpu.CompilerParams(vmem_limit_bytes=VMEM),
        cost_estimate=pl.CostEstimate(flops=flops, bytes_accessed=moved, transcendentals=0),
    )


def shape(*dims, dtype=f32):
    return jax.ShapeDtypeStruct(dims, dtype)


def halves(x):
    high = x.astype(bf16)
    low = (x - high.astype(f32)).astype(bf16)
    return high, low


def stacked(x, axis, blank=0):
    high, low = halves(x)
    parts = [high, low, high]
    if blank:
        dims = list(x.shape)
        dims[axis] = blank
        parts.append(jnp.zeros(dims, bf16))
    return jnp.concatenate(parts, axis=axis)


def paired(x, total):
    high, low = halves(x)
    parts = [high, low]
    if total > 2 * x.shape[0]:
        parts.append(jnp.zeros((total - 2 * x.shape[0], x.shape[1]), bf16))
    return jnp.concatenate(parts, axis=0)


def dot(a, b):
    return lax.dot_general(a, b, (((1,), (0,)), ((), ())), preferred_element_type=f32)


def dot_nt(a, b):
    return lax.dot_general(a, b, (((1,), (1,)), ((), ())), preferred_element_type=f32)


def lag_taps(params, slot, dim, lag):
    value = jnp.zeros(lag.shape, f32)
    for tap in range(KERN):
        value = jnp.where(lag == tap, params[slot, dim, tap], value)
    return value


def thirds(value, part):
    high = value.astype(bf16).astype(f32)
    return jnp.where(part == 2, value - high, high).astype(bf16)


def split(value):
    high = value.astype(bf16).astype(f32)
    return high, value - high


def grid_of(rows, columns):
    return (
        lax.broadcasted_iota(jnp.int32, (rows, columns), 0),
        lax.broadcasted_iota(jnp.int32, (rows, columns), 1),
    )


def spread_band(params, offset, slots, band):
    total = band.shape[1]
    count = SLAB * len(slots)
    row, lane = grid_of(TALL, total)
    part = lane // count
    spot = lane - part * count
    owner = spot // SLAB
    plane = spot - owner * SLAB
    value = jnp.zeros((TALL, total), f32)
    for place, slot in enumerate(slots):
        lag = plane + offset(slot, 0) - row + 2 * RADIUS
        value = jnp.where(owner == place, lag_taps(params, slot, 0, lag), value)
    high, low = split(value)
    band[:TALL, :] = jnp.where(part < 2, high, 0.0).astype(bf16)
    band[TALL:, :] = jnp.where(part < 1, low, 0.0).astype(bf16)


def bands_kernel(params, *refs):
    ax, az, ay, ayt, wz, every = refs[-6:]

    def offset(slot, dim):
        return params[slot, dim, KERN].astype(jnp.int32)

    row, lane = grid_of(SLAB, 256)
    part = lane // TALL
    spot = lane - part * TALL
    for slot in range(VIEWS):
        lag = row + offset(slot, 0) - spot + 2 * RADIUS
        lag = jnp.where(part < 3, lag, -1)
        ax[slot * SLAB : (slot + 1) * SLAB, :] = thirds(lag_taps(params, slot, 0, lag), part)
    row, lane = grid_of(128, 128)
    part = lane // 32
    tail = lane - part * 32 + 128
    edge = lane % 64
    edge = jnp.where(edge < RIGHT, QUARTER + edge, edge - RIGHT - LEFT)
    for slot in range(VIEWS):
        high, low = split(lag_taps(params, slot, 2, row - lane + 2 * RADIUS))
        az[slot, :, 0:128] = high.astype(bf16)
        az[slot, :, 128:256] = high.astype(bf16)
        az[slot, :, 256:384] = low.astype(bf16)
        lag = jnp.where(part < 3, row - tail + 2 * RADIUS, -1)
        az[slot, :, 384:512] = thirds(lag_taps(params, slot, 2, lag), part)
        high, low = split(lag_taps(params, slot, 1, row + offset(slot, 1) - lane + RADIUS))
        ay[slot, :, 0:128] = high.astype(bf16)
        ay[slot, :, 128:256] = high.astype(bf16)
        ay[slot, :, 256:384] = low.astype(bf16)
        high, low = split(lag_taps(params, slot, 2, row + offset(slot, 2) - lane + RADIUS))
        wz[slot, :128, 0:128] = high.astype(bf16)
        wz[slot, 128:, 0:128] = high.astype(bf16)
        wz[slot, :128, 128:256] = low.astype(bf16)
        wz[slot, 128:, 128:256] = jnp.zeros((128, 128), bf16)
        lag = row + offset(slot, 2) - edge + RADIUS
        lag = jnp.where(lane % 64 < RIGHT + LEFT, lag, -1)
        high, low = split(lag_taps(params, slot, 2, lag))
        wz[slot, :128, 256:384] = jnp.where(lane < 64, high, low).astype(bf16)
        wz[slot, 128:, 256:384] = jnp.where(lane < 64, high, 0.0).astype(bf16)
    row, lane = grid_of(ROWS, 256)
    for chunk, (first, last) in enumerate(SPANS):
        count = last - first
        part = lane // count
        spot = first + lane - part * count
        for slot in range(VIEWS):
            lag = spot + offset(slot, 1) - (row + chunk * ROWS) + RADIUS
            high, low = split(lag_taps(params, slot, 1, lag))
            ayt[chunk, slot, :ROWS, :] = jnp.where(part < 2, high, 0.0).astype(bf16)
            ayt[chunk, slot, ROWS:, :] = jnp.where(part < 1, low, 0.0).astype(bf16)
    spread_band(params, offset, ALL, every)


def bands(params, after):
    whole = pl.BlockSpec(memory_space=pltpu.VMEM)
    shapes = (
        shape(VIEWS * SLAB, 256, dtype=bf16),
        shape(VIEWS, QUARTER, 512, dtype=bf16),
        shape(VIEWS, 128, 384, dtype=bf16),
        shape(2, VIEWS, 2 * ROWS, 256, dtype=bf16),
        shape(VIEWS, 256, 384, dtype=bf16),
        shape(2 * TALL, 256, dtype=bf16),
    )
    return pl.pallas_call(
        bands_kernel,
        out_shape=shapes,
        in_specs=[pl.BlockSpec(memory_space=pltpu.SMEM)]
        + [pl.BlockSpec(memory_space=pl.ANY)] * len(after),
        out_specs=(whole,) * len(shapes),
        compiler_params=pltpu.CompilerParams(vmem_limit_bytes=VMEM),
        cost_estimate=pl.CostEstimate(flops=FREE, bytes_accessed=FREE, transcendentals=0),
    )(params, *after)


def pack_kernel(psf, offsets, *refs):
    out = refs[-1]
    taps = psf[...]
    out[:, :KERN] = taps / jnp.sum(taps, axis=1, keepdims=True)
    out[:, KERN:] = offsets[...]


def pack(psf, offsets, after):
    return small(pack_kernel, shape(3, KERN + 1), (psf, offsets), after, FREE)


def mark_kernel(*refs):
    refs[-1][...] = jnp.zeros(refs[-1].shape, f32)


def mark(after):
    return small(mark_kernel, shape(8, 128), (), after, LONG)


def window_kernel(spot, left, middle, right, *refs):
    out, low, flat = refs[-3:]
    q = spot[0]
    planes = middle.shape[0]
    for i in range(planes):
        before = left[i].T[QUARTER - LEFT :, :]
        after = right[i].T[:RIGHT, :]
        at = i * ODD
        flat[at : at + LEFT, :] = jnp.where(q > 0, before, 0.0)
        flat[at + LEFT : at + LEFT + QUARTER, :] = middle[i].T
        flat[at + LEFT + QUARTER : at + WIDE, :] = jnp.where(q < VIEWS - 1, after, 0.0)
    for z in range(WIDE):
        row = flat[pl.ds(z, planes, ODD), :]
        out[z] = row
        low[z] = row


def window(estimate, spot, after):
    n = LEFT
    block = (n, 128, QUARTER)
    return pl.pallas_call(
        window_kernel,
        out_shape=(shape(WIDE, SLAB, 128), shape(WIDE, LEFT, 128)),
        grid_spec=pltpu.PrefetchScalarGridSpec(
            num_scalar_prefetch=1,
            grid=(SLAB // n,),
            in_specs=[
                pl.BlockSpec(block, lambda i, s: (i, 0, jnp.maximum(s[0] - 1, 0))),
                pl.BlockSpec(block, lambda i, s: (i, 0, s[0])),
                pl.BlockSpec(block, lambda i, s: (i, 0, jnp.minimum(s[0] + 1, VIEWS - 1))),
            ]
            + [pl.BlockSpec(memory_space=pl.ANY)] * len(after),
            out_specs=(
                pl.BlockSpec((WIDE, n, 128), lambda i, s: (0, i, 0)),
                pl.BlockSpec((WIDE, n, 128), lambda i, s: (0, 0, 0)),
            ),
            scratch_shapes=[pltpu.VMEM((n * ODD + 7, 128), f32)],
        ),
        compiler_params=pltpu.CompilerParams(vmem_limit_bytes=VMEM),
        cost_estimate=pl.CostEstimate(flops=FREE, bytes_accessed=FREE, transcendentals=0),
    )(spot, estimate, estimate, estimate, *after)


def cut_kernel(first, rows, steps, spot, recorded, *refs):
    n = len(steps)
    outs, holds = refs[-2 * n - 2 : -n - 2], refs[-n - 2 : -2]
    sems, out_sems = refs[-2:]
    moves = []
    for k, step in enumerate(steps):
        quarter = lax.rem(spot[0] + step, VIEWS)
        lanes = pl.ds(pl.multiple_of(quarter * QUARTER, QUARTER), QUARTER)
        source = recorded.at[:, pl.ds(first, rows), lanes]
        moves.append(pltpu.make_async_copy(source, holds[k], sems.at[k]))
    for move in moves:
        move.start()
    writes = [pltpu.make_async_copy(holds[k], outs[k], out_sems.at[k]) for k in range(n)]
    for move, write in zip(moves, writes):
        move.wait()
        write.start()
    for write in writes:
        write.wait()


def cut(recorded, spot, first, rows, steps, after=()):
    hbm = pl.BlockSpec(memory_space=pl.ANY)
    return pl.pallas_call(
        lambda *refs: cut_kernel(first, rows, steps, *refs),
        out_shape=(shape(SLAB, rows, QUARTER),) * len(steps),
        in_specs=[pl.BlockSpec(memory_space=pltpu.SMEM)] + [hbm] * (1 + len(after)),
        out_specs=(hbm,) * len(steps),
        scratch_shapes=[pltpu.VMEM((SLAB, rows, QUARTER), f32)] * len(steps)
        + [pltpu.SemaphoreType.DMA((len(steps),))] * 2,
        compiler_params=pltpu.CompilerParams(vmem_limit_bytes=VMEM),
        cost_estimate=pl.CostEstimate(flops=FREE, bytes_accessed=FREE, transcendentals=0),
    )(spot, recorded, *after)


def forward_kernel(starts, ax, az, ay, lower, middle, upper, *refs):
    out, blurred = refs[-2:]
    slot = pl.program_id(0)

    @pl.when(slot == 0)
    def _():
        def some(group, carry):
            at = group * 8
            columns = [
                jnp.concatenate([lower[at + z], middle[at + z], upper[at + z]], axis=0)
                for z in range(8)
            ]
            data = stacked(jnp.concatenate(columns, axis=1), 0, 256 - 3 * TALL)
            result = dot(ax[...], data)
            for z in range(8):
                blurred[pl.ds(at + z, VIEWS * SLAB, ODD), :] = result[:, z * 128 : z * 128 + 128]
            return carry

        lax.fori_loop(0, WIDE // 8, some, 0)

    start = starts[slot]
    span = QUARTER + 2 * RADIUS
    many = 8

    def planes(group, carry):
        first = slot * SLAB + group * many
        data = jnp.concatenate(
            [blurred[pl.ds((first + i) * ODD + start, span), :] for i in range(many)], axis=1
        )
        high, low = halves(data)
        blank = jnp.zeros((32, many * 128), bf16)
        data = [high[:128], low[:128], high[:128], high[128:], low[128:], high[128:], blank]
        section = dot(az[0], jnp.concatenate(data, axis=0))
        section = jnp.concatenate([section[:, i * 128 : i * 128 + 128] for i in range(many)], axis=0)
        result = dot_nt(ay[0], stacked(section, 1)) + BACKGROUND
        for i in range(many):
            out[group * many + i] = result[:, i * QUARTER : (i + 1) * QUARTER]
        return carry

    lax.fori_loop(0, SLAB // many, planes, 0)


def forward_of(starts, ax, az, ay, lower, middle, upper):
    def once(x):
        return pl.BlockSpec(x.shape, lambda v, s: (0,) * x.ndim, pipeline_mode=pl.Buffered(1))

    return pl.pallas_call(
        forward_kernel,
        out_shape=shape(VIEWS * SLAB, 128, QUARTER),
        grid_spec=pltpu.PrefetchScalarGridSpec(
            num_scalar_prefetch=1,
            grid=(VIEWS,),
            in_specs=[
                once(ax),
                pl.BlockSpec((1,) + az.shape[1:], lambda v, s: (v, 0, 0)),
                pl.BlockSpec((1,) + ay.shape[1:], lambda v, s: (v, 0, 0)),
                once(lower),
                once(middle),
                once(upper),
            ],
            out_specs=pl.BlockSpec((SLAB, 128, QUARTER), lambda v, s: (v, 0, 0)),
            scratch_shapes=[pltpu.VMEM((VIEWS * SLAB * ODD + 8, 128), f32)],
        ),
        compiler_params=pltpu.CompilerParams(vmem_limit_bytes=VMEM),
        cost_estimate=pl.CostEstimate(flops=FREE, bytes_accessed=FREE, transcendentals=0),
    )(starts, ax, az, ay, lower, middle, upper)


def adjoint_kernel(chunk, extra, *refs):
    n = VIEWS
    pieces = chunk + 1
    first, last = SPANS[chunk]
    bounds = ((first, CUT), (CUT, 128))[:pieces]
    spot, band, ayt, wz, forward = refs[:5]
    refs = list(refs[5:])
    measured = []
    for slot in ALL:
        if slot == 0:
            lanes = pl.ds(pl.multiple_of(spot[0] * QUARTER, QUARTER), QUARTER)
            whole = refs.pop(0)
            measured.append([whole.at[:, pl.ds(a, b - a), lanes] for a, b in bounds])
        else:
            measured.append([refs.pop(0).at[:, pl.ds(first, CUT - first), :]])
            if chunk:
                measured[-1].append(refs.pop(0))
    refs = refs[extra:]
    outs, refs = refs[:6], refs[6:]
    hold, kept, spread = refs[0], refs[1 : 1 + pieces], refs[1 + pieces]
    totals = refs[2 + pieces : 5 + pieces]
    sems, out_sems = refs[-2:]
    copies = []
    for k, slot in enumerate(ALL):
        source = forward.at[pl.ds(slot * SLAB, SLAB), pl.ds(first, last - first), :]
        moves = [pltpu.make_async_copy(source, hold.at[k], sems.at[k, 0])]
        for piece in range(pieces):
            target = kept[piece].at[k]
            moves.append(pltpu.make_async_copy(measured[k][piece], target, sems.at[k, 1 + piece]))
        for move in moves:
            move.start()
        copies.append(moves)

    many = 8
    lane = lax.broadcasted_iota(jnp.int32, (PACKED, 128), 1)
    for k, slot in enumerate(ALL):
        for move in copies[k]:
            move.wait()

        def planes(group, carry, k=k, slot=slot):
            ratios = []
            for i in range(many):
                p = group * many + i
                if chunk == 0:
                    seen = kept[0][k, p]
                else:
                    seen = jnp.concatenate([kept[0][k, p], kept[1][k, p]], axis=0)
                ratios.append(seen / hold[k, p])
            data = paired(jnp.concatenate(ratios, axis=1), 256)
            section = dot(ayt[chunk, slot], data)
            section = section[:ROWS] + section[ROWS:]
            rows = [section[:, i * QUARTER : (i + 1) * QUARTER] for i in range(many)]
            high, low = halves(jnp.concatenate(rows, axis=0))
            result = dot(jnp.concatenate([high, low], axis=1), wz[slot])
            center = result[:, :128] + result[:, 128:256]
            edge = result[:, 256:384]
            edge = edge + pltpu.roll(edge, 64, 1)
            base = pl.multiple_of(group * (many * SKEW), 8) + k * SLAB * SKEW
            for i in range(many):
                at = base + i * SKEW
                spread[pl.ds(at, ROWS), :] = center[i * ROWS : (i + 1) * ROWS]
                packed = edge[i * ROWS : (i + 1) * ROWS]
                packed = jnp.where(lane < 64, packed[:PACKED], packed[PACKED:])
                spread[pl.ds(at + ROWS, PACKED), :] = packed
            return carry

        lax.fori_loop(0, SLAB // many, planes, 0)

    total = band.shape[1]
    step = 8

    centers = ROWS // step

    def sends(group, edge):
        at = pl.ds(pl.multiple_of(group * step, step), step)
        to = pl.ds(pl.multiple_of((group - edge * centers) * step, step), step)
        return [
            pltpu.make_async_copy(
                totals[k].at[at], outs[3 * edge + k].at[to], out_sems.at[k, group]
            )
            for k in range(3)
        ]

    def some(group, edge):
        at = group * step
        columns = [spread[pl.ds(at + r, n * SLAB, SKEW), :] for r in range(step)]
        result = dot(band[...], paired(jnp.concatenate(columns, axis=1), total))
        result = result[:TALL] + result[TALL:]
        for r in range(step):
            piece = result[:, r * 128 : (r + 1) * 128]
            totals[0][at + r] = piece[:LEFT]
            totals[1][at + r] = piece[LEFT : LEFT + SLAB]
            totals[2][at + r] = piece[LEFT + SLAB :]
        for move in sends(group, edge):
            move.start()
        return edge

    lax.fori_loop(centers, CHUNK // step, lambda group, c: some(group, 1), 1)
    lax.fori_loop(0, centers, lambda group, c: some(group, 0), 0)
    for group in range(CHUNK // step):
        for move in sends(group, int(group >= centers)):
            move.wait()


def adjoint(chunk, spot, band, ayt, wz, forward, recorded, measured, after):
    n = VIEWS
    vmem = pl.BlockSpec(memory_space=pltpu.VMEM)
    hbm = pl.BlockSpec(memory_space=pl.ANY)
    first, last = SPANS[chunk]
    rows = (CUT - first, 128 - CUT)[: chunk + 1]
    sizes = (LEFT, SLAB, RIGHT)
    arrays = [forward]
    for slot in ALL:
        if slot:
            arrays += [measured[piece][slot] for piece in range(chunk + 1)]
        else:
            arrays.append(recorded)
    arrays += after
    return pl.pallas_call(
        lambda *refs: adjoint_kernel(chunk, len(after), *refs),
        out_shape=tuple(shape(r, k, 128) for r in (ROWS, PACKED) for k in sizes),
        in_specs=[pl.BlockSpec(memory_space=pltpu.SMEM)] + [vmem] * 3 + [hbm] * len(arrays),
        out_specs=(hbm,) * 6,
        scratch_shapes=[pltpu.VMEM((n, SLAB, last - first, QUARTER), f32)]
        + [pltpu.VMEM((n, SLAB, k, QUARTER), f32) for k in rows]
        + [pltpu.VMEM((n * SLAB * SKEW + 8, 128), f32)]
        + [pltpu.VMEM((CHUNK, k, 128), f32) for k in sizes]
        + [
            pltpu.SemaphoreType.DMA((n, chunk + 2)),
            pltpu.SemaphoreType.DMA((3, CHUNK // 8)),
        ],
        compiler_params=pltpu.CompilerParams(vmem_limit_bytes=VMEM),
        cost_estimate=pl.CostEstimate(flops=FREE, bytes_accessed=FREE, transcendentals=0),
    )(spot, band, ayt, wz, *arrays)


def added(own, up, down):
    half = SLAB // 2
    whole = own[...] + up[...]
    return whole[:, :half], whole[:, half:] + down[...]


def edges_kernel(own, up, down, *refs):
    rights, lefts = refs[-2:]
    near, far = added(own, up, down)
    lane = lax.broadcasted_iota(jnp.int32, (1, SLAB // 2, 128), 2) % 64
    rights[...] = jnp.where(lane < RIGHT, near, pltpu.roll(far, RIGHT, 2))
    lefts[...] = jnp.where(lane < RIGHT + LEFT, near, pltpu.roll(far, LEFT, 2))


def center_kernel(own, up, down, *refs):
    refs[-1][...] = jnp.concatenate(added(own, up, down), axis=1)


def small(kernel, out_shape, arrays, after, flops):
    vmem = pl.BlockSpec(memory_space=pltpu.VMEM)
    hbm = pl.BlockSpec(memory_space=pl.ANY)
    return pl.pallas_call(
        kernel,
        out_shape=out_shape,
        in_specs=[vmem] * len(arrays) + [hbm] * len(after),
        out_specs=jax.tree.map(lambda _: vmem, out_shape),
        compiler_params=pltpu.CompilerParams(vmem_limit_bytes=VMEM),
        cost_estimate=pl.CostEstimate(flops=flops, bytes_accessed=FREE, transcendentals=0),
    )(*arrays, *after)


def settle_edges(own, up, down, after):
    packed = shape(PACKED, SLAB // 2, 128)
    return small(edges_kernel, (packed, packed), (own, up, down), after, FREE)


def settle_center(own, up, down, after):
    return small(center_kernel, shape(ROWS, SLAB, 128), (own, up, down), after, FREE)


def merge_kernel(center, rights, lefts, *refs):
    out = refs[-1]
    lane = lax.broadcasted_iota(jnp.int32, (SLAB // 2, 128), 1)
    turns = (((0, 64), (96, 32)), ((80, 16), (64, 0)))
    for piece in (0, 1):
        for r in range(PACKED):
            extra = []
            for group in (0, 1):
                low, high = rights[r], lefts[r]
                if turns[0][group][piece]:
                    low = pltpu.roll(low, turns[0][group][piece], 1)
                if turns[1][group][piece]:
                    high = pltpu.roll(high, turns[1][group][piece], 1)
                high = jnp.where(lane >= QUARTER - LEFT, high, 0.0)
                extra.append(jnp.where(lane < RIGHT, low, high))
            at = piece * PACKED + r
            out[:, at, :] = center[at] + jnp.concatenate(extra, axis=0)


def merge(center, rights, lefts, after):
    arrays = (center, rights, lefts)
    return small(merge_kernel, shape(SLAB, ROWS, 128), arrays, after, FREE)


def finish_kernel(count, spot, estimate, *refs):
    out = refs[-1]
    first = 0
    for piece in refs[:count]:
        rows = slice(first, first + piece.shape[1])
        out[:, rows, :] = estimate[:, rows, :] * piece[...] / VIEWS
        first = first + piece.shape[1]


def finish(chunk, step, spot, estimate, pieces, before, after, flops):
    n = 32
    place = pl.BlockSpec(
        (n, ROWS, QUARTER), lambda i, s: (i, chunk, lax.rem(s[0] + (VIEWS - step), VIEWS))
    )
    specs = [place] + [
        pl.BlockSpec((n, piece.shape[1], QUARTER), lambda i, s: (i, 0, 0)) for piece in pieces
    ]
    arrays = [spot, estimate, *pieces]
    aliases = {}
    if before is not None:
        specs.append(pl.BlockSpec(memory_space=pl.ANY))
        arrays.append(before)
        aliases = {len(arrays) - 1: 0}
    arrays += after
    specs += [pl.BlockSpec(memory_space=pl.ANY)] * len(after)
    return call(
        lambda *refs: finish_kernel(len(pieces), *refs),
        shape(*estimate.shape),
        (SLAB // n,),
        specs,
        place,
        prefetch=1,
        aliases=aliases,
        flops=flops,
        moved=FREE,
    )(*arrays)


def along_blk(x, distance):
    size = lax.axis_size("blk")
    route = [(i, i + distance) for i in range(size) if 0 <= i + distance < size]
    return lax.ppermute(x, "blk", route)


def around_view(x, distance):
    return lax.ppermute(x, "view", [(i, (i + distance) % VIEWS) for i in range(VIEWS)])


def along_view(x, distance):
    route = [(i, i + distance) for i in range(VIEWS) if 0 <= i + distance < VIEWS]
    return lax.ppermute(x, "view", route)


def body(estimate, views, psf, offsets):
    q = lax.axis_index("view")
    spot = q[None]
    recorded = views[0]
    middle, last = window(estimate, spot, ())
    upper = along_blk(middle, -1)
    lower = along_blk(last, 1)

    mine = pack(psf[0], offsets[0].astype(f32)[:, None], (middle,))
    params = jnp.stack([mine] + [around_view(mine, s) for s in (1, 2, 3)])
    others = (1, 3, 2)
    pieces = cut(recorded, spot, 0, CUT, others, (params,))
    measured = ({s: around_view(piece, s) for s, piece in zip(others, pieces)}, {})
    starts = params[:, 2, KERN].astype(jnp.int32)
    ax, az, ay, ayt, wz, every = bands(params, pieces)
    forward = forward_of(starts, ax, az, ay, lower, middle, upper)
    pieces = cut(recorded, spot, CUT, 128 - CUT, others, (forward,))
    measured[1].update({s: around_view(piece, s) for s, piece in zip(others, pieces)})

    def spill(parts):
        below, own, above = parts
        return own, along_blk(above, 1), along_blk(below, -1)

    def margins(edges):
        rights, lefts = edges
        return along_view(rights, 1), along_view(lefts, -1)

    def gather(piece):
        left = around_view(piece, 1)
        right = around_view(piece, 3)
        near = around_view(left[:, : ROWS // 2], 1)
        far = around_view(right[:, ROWS // 2 :], 3)
        return piece, left, right, near, far

    def adjoint_of(chunk, after):
        return adjoint(chunk, spot, every, ayt, wz, forward, recorded, measured, after)

    parts0 = adjoint_of(0, pieces)
    spilled0 = spill(parts0[3:]), spill(parts0[:3])
    margins0 = margins(settle_edges(*spilled0[0], (mark((measured[1][1], measured[1][3])),)))
    center0 = settle_center(*spilled0[1], (measured[1][2],))
    piece0 = merge(center0, *margins0, ())
    gathered0 = gather(piece0)
    parts1 = adjoint_of(1, (piece0,))
    spilled1 = spill(parts1[3:]), spill(parts1[:3])
    margins1 = margins(settle_edges(*spilled1[0], gathered0[1:3]))
    center1 = settle_center(*spilled1[1], ())
    piece1 = merge(center1, *margins1, gathered0[3:])
    gathered1 = gather(piece1)
    out = None
    for chunk, gathered in enumerate((gathered0, gathered1)):
        piece, left, right, near, far = gathered
        for step, parts in ((0, (piece,)), (1, (left,)), (3, (right,)), (2, (near, far))):
            after = (piece1,) if out is None else ()
            flops = LONG if (chunk, step) == (1, 1) else FREE
            out = finish(chunk, step, spot, estimate, parts, out, after, flops)
    return out


def solution(mesh):
    placed = (
        P("blk", None, None),
        P("view", "blk", None, None),
        P("view", None, None),
        P("view", None),
    )
    return jax.shard_map(
        body, mesh=mesh, in_specs=placed, out_specs=P("blk", None, None), check_vma=False
    )
```

time: 554 us -> 238 us (0.43)
  waiting for transfers between devices: 298 us -> 71.4 us
  matrix products: 165 us -> 0 us
  Pallas kernels: 0 us -> 93.1 us
  starting transfers between devices: 12.1 us -> 65 us
  other arithmetic: 34 us -> 0.24 us
  local copies, waits for them, and re-layouts: 22 us -> 3.15 us
  between operations: 13.7 us -> 0.41 us
    dot_general x9 -> x0, matrix products: 165 us -> none  [the longest x1 37.1 us: across(): jnp.einsum('ryk,pk->ryp', section, band_z, precision=lax.Precision.HIGHEST)]
    psum x1 -> x0, waiting for transfers between devices: 161 us -> none  [body(): correction = lax.psum(spill(spread_back, slab_rows), 'view')]
    pallas_call x0 -> x23, Pallas kernels: none -> 93.1 us  [the longest x2 31.7 us: adjoint(): pl.pallas_call(lambda *refs: adjoint_kernel(chunk, len(after), *refs), ou...]
    ppermute x4 -> x31, waiting for transfers between devices: 137 us -> 71.4 us  [the longest x17 33.5 us: around_view(): lax.ppermute(x, 'view', [(i, (i + distance) % VIEWS) for i in range(VIEWS)])]
    ppermute x4 -> x31, starting transfers between devices: 12.1 us -> 65 us  [the longest x10 33.7 us: along_blk(): return lax.ppermute(x, 'blk', route)]
    div x2 -> x0, other arithmetic: 15 us -> none  [the longest x1 14.9 us: body(): return estimate * correction / view_count]
    div x1 -> x0, local copies, waits for them, and re-layouts: 11.6 us -> none  [body(): return estimate * correction / view_count]
    add x4 -> x0, other arithmetic: 10.2 us -> none  [the longest x1 8.14 us: spill(): owned_rows = owned_rows + from_lower]
  transfers between devices with their start and end apart: 5 -> 31, of which waited for: 5 -> 14; matrix products, arithmetic and copies ran while one was open for 7% -> 1% of each run, Pallas kernels for 0% -> 36%
where the time goes in v2:
time: 238 us; the launch traced here: 233 us
  Pallas kernels  93.1 us (39%)
  waiting for transfers between devices  71.4 us (30%)
  starting transfers between devices  65 us (27%)
  local copies, waits for them, and re-layouts  3.15 us (1%)
    ppermute x10, starting transfers between devices, along_blk(): return lax.ppermute(x, 'blk', route)  33.7 us
    ppermute x17, waiting for transfers between devices, around_view(): lax.ppermute(x, 'view', [(i, (i + distance) % VIEWS) for i in range(VIEWS)])  33.5 us
    pallas_call x2, Pallas kernels, adjoint(): pl.pallas_call(lambda *refs: adjoint_kernel(chunk, len(after), *refs), ou...  31.7 us
    ppermute x10, waiting for transfers between devices, along_blk(): return lax.ppermute(x, 'blk', route)  22.3 us
    pallas_call x1, Pallas kernels, forward_of(): pl.pallas_call(forward_kernel, out_shape=shape(VIEWS * SLAB, 128, QUARTER...  19.2 us
    pallas_call x8, Pallas kernels, finish(): call(lambda *refs: finish_kernel(len(pieces), *refs), shape(*estimate.sha...  19.1 us
    ppermute x17, starting transfers between devices, around_view(): lax.ppermute(x, 'view', [(i, (i + distance) % VIEWS) for i in range(VIEWS)])  18.1 us
    ppermute x4, waiting for transfers between devices, along_view(): return lax.ppermute(x, 'view', route)  15.5 us
  transfers between devices with their start and end apart: 31, of which 14 were waited for; matrix products, arithmetic and copies ran while one was open for 1% of the time, Pallas kernels for 36%

profile of v2, /device:TPU:59, one launch (start us, length us, event | category | flops | bytes accessed | tf_op | source)
XLA Modules:
  0.0 233.3 jit_solution(15673665494394752985)
XLA Ops:
  0.0 5.4 %shard_map.46 = (f32[176,32,128]{2,1,0:T(8,128)S(1)}, f32[176,16,128]{2,1,0:T(8,128)}) custom-call(s32[1]{0:T(128)} %bitcast.spot.refs_0_, f32[32,128,512]{2,1,0:T(8,128)} %refs_1_.15, f32[32,128,512]{2,1,0:T(8,128)} %refs_1_.15, f32[32,128,512]{2,1,0:T(8,128)} %refs_1_.15), custom_call_target="tpu_custom_call" | custom-call | flops 1024 | bytes 1024 | tf_op jit(solution)/shard_map/pallas_call | solution.py:236
  5.4 2.6 %collective-permute-start.4 = (f32[176,32,128]{2,1,0:T(8,128)S(1)}, f32[176,32,128]{2,1,0:T(8,128)}, u32[]{:S(2)}, u32[]{:S(2)}) collective-permute-start(f32[176,32,128]{2,1,0:T(8,128)S(1)} %get-tuple-element.35.refs_0_.middle), channel_id=1, source_target_pairs={{1,0},{2,1},{3,2},{4,3},{5,4},{6,5},{7,6},{8,7},{9,8},{10,9},{11,1... | collective-permute-start | bytes 8650760 | tf_op jit(solution)/shard_map/ppermute | solution.py:602
  8.0 5.1 %collective-permute-start.3 = (f32[176,16,128]{2,1,0:T(8,128)}, f32[176,16,128]{2,1,0:T(8,128)}, u32[]{:S(2)}, u32[]{:S(2)}) collective-permute-start(f32[176,16,128]{2,1,0:T(8,128)} %get-tuple-element.45), channel_id=1, source_target_pairs={{0,1},{1,2},{2,3},{3,4},{4,5},{5,6},{6,7},{7,8},{8,9},{9,10},{10,1... | collective-permute-start | bytes 4325384 | tf_op jit(solution)/shard_map/ppermute | solution.py:602
  15.4 1.8 collective-permute-start.2
  18.4 2.3 shard_map.48
  22.5 2.5 %collective-permute-start.9 = (f32[32,80,128]{2,1,0:T(8,128)S(1)}, f32[32,80,128]{2,1,0:T(8,128)}, u32[]{:S(2)}, u32[]{:S(2)}) collective-permute-start(f32[32,80,128]{2,1,0:T(8,128)S(1)} %get-tuple-element.38.refs_2_), channel_id=1, source_target_pairs={{0,64},{32,96},{64,0},{96,32},{1,65},{33,97},{65,1},{97,33},{2,66}... | collective-permute-start | bytes 3932168 | tf_op jit(solution)/shard_map/ppermute | solution.py:606
  25.0 6.9 %shard_map.49 = (bf16[128,256]{1,0:T(8,128)(2,1)S(1)}, bf16[4,128,512]{2,1,0:T(8,128)(2,1)S(1)}, bf16[4,128,384]{2,1,0:T(8,128)(2,1)S(1)}, bf16[2,4,128,256]{3,2...) custom-call(f32[4,3,34]{2,1,0:T(4,128)S(1)} %pad_maximum_fusion.refs_2_.params, ...), custom_call_target="tpu_custom_call" | custom-call | flops 1024 | bytes 1024 | tf_op jit(solution)/shard_map/pallas_call | solution.py:186
  32.2 11.2 %collective-permute-done.4.upper = f32[176,32,128]{2,1,0:T(8,128)} collective-permute-done((f32[176,32,128]{2,1,0:T(8,128)S(1)}, f32[176,32,128]{2,1,0:T(8,128)}, u32[]{:S(2)}, u32[]{:S(2)}) %collective-permute-start.4) | collective-permute-done | bytes 2883616 | tf_op jit(solution)/shard_map/ppermute | solution.py:602
  43.4 19.2 %shard_map.50.refs_2_.refs_4_ = f32[128,128,128]{2,1,0:T(8,128)} custom-call(s32[4]{0:T(128)S(1)} %fusion.starts, bf16[128,256]{1,0:T(8,128)(2,1)S(1)} %get-tuple-element.42.ax, bf16[4,128,512]{2,1,0:T(8,128)(2,1)S(1)} %get-tuple-element.43.az, bf16[4,128,384]{2,1,0:T(8,128)(2,1)S(1)} %get-tuple-element.44.ay, f32[176,16,128]{2,1,0:T(8,128)} %collective-permute-done.3.lower, ...), custom_call_target="tpu_custom_call" | custom-call | flops 1024 | bytes 1024 | tf_op jit(solution)/shard_map/pallas_call | solution.py:339
  62.6 2.6 %shard_map.51 = (f32[32,48,128]{2,1,0:T(8,128)S(1)}, f32[32,48,128]{2,1,0:T(8,128)S(1)}, f32[32,48,128]{2,1,0:T(8,128)}) custom-call(s32[1]{0:T(128)} %bitcast.spot.refs_0_, f32[32,128,512]{2,1,0:T(8,128)} %bitcast.14, f32[128,128,128]{2,1,0:T(8,128)} %shard_map.50.refs_2_.refs_4_), custom_call_target="tpu_custom_call" | custom-call | flops 1024 | bytes 1024 | tf_op jit(solution)/shard_map/pallas_call | solution.py:281
  65.2 1.3 collective-permute-start.6
  66.7 1.9 collective-permute-start.10
  68.6 13.7 %collective-permute-done.9.refs_8_.refs_10_ = f32[32,80,128]{2,1,0:T(8,128)} collective-permute-done((f32[32,80,128]{2,1,0:T(8,128)S(1)}, f32[32,80,128]{2,1,0:T(8,128)}, u32[]{:S(2)}, u32[]{:S(2)}) %collective-permute-start.9) | collective-permute-done | bytes 1310752 | tf_op jit(solution)/shard_map/ppermute | solution.py:606
  82.2 14.9 %shard_map.52 = (f32[64,16,128]{2,1,0:T(8,128)}, f32[64,32,128]{2,1,0:T(8,128)}, f32[64,32,128]{2,1,0:T(8,128)}, f32[32,16,128]{2,1,0:T(8,128)}, f32[32,32,128]{2,1,0:T(8,128)S(1)}, /*index=5*/f32[32,32,128]{2,1,0:T(8,128)}) custom-call(s32[1]{0:T(128)} %bitcast.spot.refs_0_, bf16[160,256]{1,0:T(8,128)(2,1)S(1)} %get-tuple-element.39.refs_1_, ...), custom_call_target="tpu_custom_call" | custom-call | flops 1024 | bytes 1024 | tf_op jit(solution)/shard_map/pallas_call | solution.py:479
  97.2 5.1 %collective-permute-start.13 = (f32[32,32,128]{2,1,0:T(8,128)}, f32[32,32,128]{2,1,0:T(8,128)}, u32[]{:S(2)}, u32[]{:S(2)}) collective-permute-start(f32[32,32,128]{2,1,0:T(8,128)} %get-tuple-element.53), channel_id=1, source_target_pairs={{0,1},{1,2},{2,3},{3,4},{4,5},{5,6},{6,7},{7,8},{8,9},{9,10},{10,1... | collective-permute-start | bytes 1572872 | tf_op jit(solution)/shard_map/ppermute | solution.py:602
  102.3 1.9 collective-permute-start.14
  104.2 5.8 %collective-permute-start.11 = (f32[64,32,128]{2,1,0:T(8,128)}, f32[64,32,128]{2,1,0:T(8,128)}, u32[]{:S(2)}, u32[]{:S(2)}) collective-permute-start(f32[64,32,128]{2,1,0:T(8,128)} %get-tuple-element.50), channel_id=1, source_target_pairs={{0,1},{1,2},{2,3},{3,4},{4,5},{5,6},{6,7},{7,8},{8,9},{9,10},{10,1... | collective-permute-start | bytes 3145736 | tf_op jit(solution)/shard_map/ppermute | solution.py:602
  110.0 1.9 collective-permute-start.12
  112.4 1.6 shard_map.55
  114.0 1.9 collective-permute-start.15
  115.9 5.7 %collective-permute-start.16 = (f32[32,16,128]{2,1,0:T(8,128)S(1)}, f32[32,16,128]{2,1,0:T(8,128)S(1)}, u32[]{:S(2)}, u32[]{:S(2)}) collective-permute-start(f32[32,16,128]{2,1,0:T(8,128)S(1)} %get-tuple-element.56), channel_id=1, source_target_pairs={{32,0},{64,32},{96,64},{33,1},{65,33},{97,65},{34,2},{66,34},{98,6... | collective-permute-start | bytes 786440 | tf_op jit(solution)/shard_map/ppermute | solution.py:611
  121.6 1.4 collective-permute-done.12.down
  123.0 1.5 shard_map.53.center
  124.5 1.8 collective-permute-done.15.rights
  126.2 5.0 %collective-permute-done.16.lefts = f32[32,16,128]{2,1,0:T(8,128)S(1)} collective-permute-done((f32[32,16,128]{2,1,0:T(8,128)S(1)}, f32[32,16,128]{2,1,0:T(8,128)S(1)}, u32[]{:S(2)}, u32[]{:S(2)}) %collective-permute-start.16) | collective-permute-done | bytes 262176 | tf_op jit(solution)/shard_map/ppermute | solution.py:611
  133.9 16.8 %shard_map.57 = (f32[64,16,128]{2,1,0:T(8,128)S(1)}, f32[64,32,128]{2,1,0:T(8,128)}, f32[64,32,128]{2,1,0:T(8,128)}, f32[32,16,128]{2,1,0:T(8,128)S(1)}, f32[32,...) custom-call(s32[1]{0:T(128)} %bitcast.spot.refs_0_, bf16[160,256]{1,0:T(8,128)(2,1)S(1)} %copy-done.10, ...), custom_call_target="tpu_custom_call" | custom-call | flops 1024 | bytes 1024 | tf_op jit(solution)/shard_map/pallas_call | solution.py:479
  150.7 5.1 %collective-permute-start.17 = (f32[64,32,128]{2,1,0:T(8,128)}, f32[64,32,128]{2,1,0:T(8,128)S(1)}, u32[]{:S(2)}, u32[]{:S(2)}) collective-permute-start(f32[64,32,128]{2,1,0:T(8,128)} %get-tuple-element.58), channel_id=1, source_target_pairs={{0,1},{1,2},{2,3},{3,4},{4,5},{5,6},{6,7},{7,8},{8,9},{9,10},{10,1... | collective-permute-start | bytes 3145736 | tf_op jit(solution)/shard_map/ppermute | solution.py:602
  155.9 1.9 collective-permute-start.19
  157.8 2.4 %collective-permute-start.18 = (f32[64,16,128]{2,1,0:T(8,128)S(1)}, f32[64,16,128]{2,1,0:T(8,128)S(1)}, u32[]{:S(2)}, u32[]{:S(2)}) collective-permute-start(f32[64,16,128]{2,1,0:T(8,128)S(1)} %get-tuple-element.59), channel_id=1, source_target_pairs={{1,0},{2,1},{3,2},{4,3},{5,4},{6,5},{7,6},{8,7},{9,8},{10,9},{11,1... | collective-permute-start | bytes 1572872 | tf_op jit(solution)/shard_map/ppermute | solution.py:602
  160.2 1.9 collective-permute-start.20
  162.2 1.8 collective-permute-start.25
  164.0 9.2 %collective-permute-done.20.down = f32[32,16,128]{2,1,0:T(8,128)S(1)} collective-permute-done((f32[32,16,128]{2,1,0:T(8,128)S(1)}, f32[32,16,128]{2,1,0:T(8,128)S(1)}, u32[]{:S(2)}, u32[]{:S(2)}) %collective-permute-start.20) | collective-permute-done | bytes 262176 | tf_op jit(solution)/shard_map/ppermute | solution.py:602
  173.6 3.6 %collective-permute-start.23 = (f32[32,16,128]{2,1,0:T(8,128)S(1)}, f32[32,16,128]{2,1,0:T(8,128)S(1)}, u32[]{:S(2)}, u32[]{:S(2)}) collective-permute-start(f32[32,16,128]{2,1,0:T(8,128)S(1)} %get-tuple-element.63), channel_id=1, source_target_pairs={{0,32},{32,64},{64,96},{1,33},{33,65},{65,97},{2,34},{34,66},{66,9... | collective-permute-start | bytes 786440 | tf_op jit(solution)/shard_map/ppermute | solution.py:611
  177.3 1.9 collective-permute-start.24
  180.7 1.9 collective-permute-done.23.rights
  182.6 6.8 %collective-permute-done.24.lefts = f32[32,16,128]{2,1,0:T(8,128)S(1)} collective-permute-done((f32[32,16,128]{2,1,0:T(8,128)S(1)}, f32[32,16,128]{2,1,0:T(8,128)S(1)}, u32[]{:S(2)}, u32[]{:S(2)}) %collective-permute-start.24) | collective-permute-done | bytes 262176 | tf_op jit(solution)/shard_map/ppermute | solution.py:611
  190.5 1.8 collective-permute-start.27
  192.3 2.3 %shard_map.61.refs_3_ = f32[32,128,512]{2,1,0:T(8,128)} custom-call(s32[1]{0:T(128)} %bitcast.spot.refs_0_, f32[32,128,512]{2,1,0:T(8,128)} %refs_1_.15, f32[32,64,128]{2,1,0:T(8,128)S(1)} %copy-done.1, f32[32,64,128]{2,1,0:T(8,128)S(1)} %shard_map.60.refs_3_.refs_2_), custom_call_target="tpu_custom_call" | custom-call | flops 1024 | bytes 1024 | tf_op jit(solution)/shard_map/pallas_call | solution.py:586
  194.7 2.4 %shard_map.62.refs_3_ = f32[32,128,512]{2,1,0:T(8,128)} custom-call(s32[1]{0:T(128)} %bitcast.spot.refs_0_, f32[32,128,512]{2,1,0:T(8,128)} %refs_1_.15, f32[32,64,128]{2,1,0:T(8,128)S(1)} %collective-permute-done.21.refs_0_.refs_2_, f32[32,128,512]{2,1,0:T(8,128)} %shard_map.61.refs_3_), custom_call_target="tpu_custom_call", output_to_operand_aliasing={{}: (3, {})} | custom-call | flops 1024 | bytes 1024 | tf_op jit(solution)/shard_map/pallas_call | solution.py:586
  197.1 2.4 %shard_map.63.refs_4_ = f32[32,128,512]{2,1,0:T(8,128)} custom-call(s32[1]{0:T(128)} %bitcast.spot.refs_0_, f32[32,128,512]{2,1,0:T(8,128)} %refs_1_.15, f32[32,64,128]{2,1,0:T(8,128)S(1)} %collective-permute-done.22.refs_1_.refs_2_, f32[32,128,512]{2,1,0:T(8,128)} %shard_map.62.refs_3_), custom_call_target="tpu_custom_call", output_to_operand_aliasing={{}: (3, {})} | custom-call | flops 1024 | bytes 1024 | tf_op jit(solution)/shard_map/pallas_call | solution.py:586
  199.4 2.4 %shard_map.64.refs_3_ = f32[32,128,512]{2,1,0:T(8,128)} custom-call(s32[1]{0:T(128)} %bitcast.spot.refs_0_, f32[32,128,512]{2,1,0:T(8,128)} %refs_1_.15, f32[32,32,128]{2,1,0:T(8,128)S(1)} %collective-permute-done.25.refs_0_.refs_2_, f32[32,32,128]{2,1,0:T(8,128)S(1)} %collective-permute-done.26.refs_1_.refs_3_, ...), custom_call_target="tpu_custom_call", output_to_operand_aliasing={{}: (4, {})} | custom-call | flops 1024 | bytes 1024 | tf_op jit(solution)/shard_map/pallas_call | solution.py:586
  201.8 2.3 %shard_map.65.refs_3_ = f32[32,128,512]{2,1,0:T(8,128)} custom-call(s32[1]{0:T(128)} %bitcast.spot.refs_0_, f32[32,128,512]{2,1,0:T(8,128)} %refs_1_.15, f32[32,64,128]{2,1,0:T(8,128)S(1)} %shard_map.60.refs_3_.refs_2_, f32[32,128,512]{2,1,0:T(8,128)} %shard_map.64.refs_3_), custom_call_target="tpu_custom_call", output_to_operand_aliasing={{}: (3, {})} | custom-call | flops 1024 | bytes 1024 | tf_op jit(solution)/shard_map/pallas_call | solution.py:586
  204.1 11.4 %collective-permute-done.27.refs_2_ = f32[32,64,128]{2,1,0:T(8,128)S(1)} collective-permute-done((f32[32,64,128]{2,1,0:T(8,128)S(1)}, f32[32,64,128]{2,1,0:T(8,128)S(1)}, u32[]{:S(2)}, u32[]{:S(2)}) %collective-permute-start.27) | collective-permute-done | bytes 1048608 | tf_op jit(solution)/shard_map/ppermute | solution.py:606
  217.4 1.4 collective-permute-start.30
  218.7 2.3 %shard_map.66.refs_3_ = f32[32,128,512]{2,1,0:T(8,128)} custom-call(s32[1]{0:T(128)} %bitcast.spot.refs_0_, f32[32,128,512]{2,1,0:T(8,128)} %refs_1_.15, f32[32,64,128]{2,1,0:T(8,128)S(1)} %collective-permute-done.27.refs_2_, f32[32,128,512]{2,1,0:T(8,128)} %shard_map.65.refs_3_), custom_call_target="tpu_custom_call", output_to_operand_aliasing={{}: (3, {})} | custom-call | flops 274877906944 | bytes 1024 | tf_op jit(solution)/shard_map/pallas_call | solution.py:586
  221.1 2.4 %shard_map.67.refs_4_ = f32[32,128,512]{2,1,0:T(8,128)} custom-call(s32[1]{0:T(128)} %bitcast.spot.refs_0_, f32[32,128,512]{2,1,0:T(8,128)} %refs_1_.15, f32[32,64,128]{2,1,0:T(8,128)S(1)} %collective-permute-done.29.refs_2_, f32[32,128,512]{2,1,0:T(8,128)} %shard_map.66.refs_3_), custom_call_target="tpu_custom_call", output_to_operand_aliasing={{}: (3, {})} | custom-call | flops 1024 | bytes 1024 | tf_op jit(solution)/shard_map/pallas_call | solution.py:586
  223.5 6.1 %collective-permute-done.28.refs_2_ = f32[32,32,128]{2,1,0:T(8,128)} collective-permute-done((f32[32,32,128]{2,1,0:T(8,128)}, f32[32,32,128]{2,1,0:T(8,128)}, u32[]{:S(2)}, u32[]{:S(2)}) %collective-permute-start.28) | collective-permute-done | bytes 524320 | tf_op jit(solution)/shard_map/ppermute | solution.py:606
  230.7 2.6 %shard_map.68 = f32[32,128,512]{2,1,0:T(8,128)} custom-call(s32[1]{0:T(128)} %bitcast.spot.refs_0_, f32[32,128,512]{2,1,0:T(8,128)} %refs_1_.15, f32[32,32,128]{2,1,0:T(8,128)} %collective-permute-done.28.refs_2_, f32[32,32,128]{2,1,0:T(8,128)} %collective-permute-done.30.refs_3_, f32[32,128,512]{2,1,0:T(8,128)} %shard_map.67.refs_4_), custom_call_target="tpu_custom_call", output_to_operand_aliasing={{}: (4, {})} | custom-call | flops 1024 | bytes 1024 | tf_op jit(solution)/shard_map/pallas_call | solution.py:586
  (72 shorter events, 14.8 us)
Async XLA Ops:
  0.0 13.1 %copy-start.12 = (s32[1,3]{1,0:T(1,128)S(1)}, s32[1,3]{1,0:T(1,128)}, u32[]{:S(2)}) copy-start(s32[1,3]{1,0:T(1,128)} %param.7) | copy-start | bytes 40
  0.0 13.2 %copy-start.11 = (f32[1,3,33]{2,0,1:T(1,128)S(1)}, f32[1,3,33]{2,0,1:T(1,128)}, u32[]{:S(2)}) copy-start(f32[1,3,33]{2,0,1:T(1,128)} %param.6) | copy-start | bytes 1192
  5.4 38.0 %collective-permute-start.4 = (f32[176,32,128]{2,1,0:T(8,128)S(1)}, f32[176,32,128]{2,1,0:T(8,128)}, u32[]{:S(2)}, u32[]{:S(2)}) collective-permute-start(f32[176,32,128]{2,1,0:T(8,128)S(1)} %get-tuple-element.35.refs_0_.middle), channel_id=1, source_target_pairs={{1,0},{2,1},{3,2},{4,3},{5,4},{6,5},{7,6},{8,7},{9,8},{10,9},{11,1... | collective-permute-start | bytes 8650760 | tf_op jit(solution)/shard_map/ppermute | solution.py:602
  8.0 24.2 %collective-permute-start.3 = (f32[176,16,128]{2,1,0:T(8,128)}, f32[176,16,128]{2,1,0:T(8,128)}, u32[]{:S(2)}, u32[]{:S(2)}) collective-permute-start(f32[176,16,128]{2,1,0:T(8,128)} %get-tuple-element.45), channel_id=1, source_target_pairs={{0,1},{1,2},{2,3},{3,4},{4,5},{5,6},{6,7},{7,8},{8,9},{9,10},{10,1... | collective-permute-start | bytes 4325384 | tf_op jit(solution)/shard_map/ppermute | solution.py:602
  13.2 3.9 %collective-permute-start = (f32[3,34]{1,0:T(4,128)S(1)}, f32[3,34]{1,0:T(4,128)S(1)}, u32[]{:S(2)}, u32[]{:S(2)}) collective-permute-start(f32[3,34]{1,0:T(4,128)S(1)} %shard_map.47), channel_id=1, source_target_pairs={{0,32},{32,64},{64,96},{96,0},{1,33},{33,65},{65,97},{97,1},{2,34}... | collective-permute-start | bytes 1232 | tf_op jit(solution)/shard_map/ppermute | solution.py:606
  14.5 3.9 %collective-permute-start.1 = (f32[3,34]{1,0:T(4,128)S(1)}, f32[3,34]{1,0:T(4,128)S(1)}, u32[]{:S(2)}, u32[]{:S(2)}) collective-permute-start(f32[3,34]{1,0:T(4,128)S(1)} %shard_map.47), channel_id=1, source_target_pairs={{0,64},{32,96},{64,0},{96,32},{1,65},{33,97},{65,1},{97,33},{2,66}... | collective-permute-start | bytes 1232 | tf_op jit(solution)/shard_map/ppermute | solution.py:606
  15.4 3.1 %collective-permute-start.2 = (f32[3,34]{1,0:T(4,128)S(1)}, f32[3,34]{1,0:T(4,128)S(1)}, u32[]{:S(2)}, u32[]{:S(2)}) collective-permute-start(f32[3,34]{1,0:T(4,128)S(1)} %shard_map.47), channel_id=1, source_target_pairs={{0,96},{32,0},{64,32},{96,64},{1,97},{33,1},{65,33},{97,65},{2,98}... | collective-permute-start | bytes 1232 | tf_op jit(solution)/shard_map/ppermute | solution.py:606
  20.8 4.2 %copy-start.6 = (f32[32,80,128]{2,1,0:T(8,128)}, f32[32,80,128]{2,1,0:T(8,128)S(1)}, u32[]{:S(2)}) copy-start(f32[32,80,128]{2,1,0:T(8,128)S(1)} %get-tuple-element.38.refs_2_) | copy-start | bytes 3932164
  20.8 46.0 %collective-permute-start.5 = (f32[32,80,128]{2,1,0:T(8,128)S(1)}, f32[32,80,128]{2,1,0:T(8,128)}, u32[]{:S(2)}, u32[]{:S(2)}) collective-permute-start(f32[32,80,128]{2,1,0:T(8,128)S(1)} %get-tuple-element.36.refs_0_), channel_id=1, source_target_pairs={{0,32},{32,64},{64,96},{96,0},{1,33},{33,65},{65,97},{97,1},{2,34}... | collective-permute-start | bytes 3932168 | tf_op jit(solution)/shard_map/ppermute | solution.py:606
  21.8 46.8 %collective-permute-start.7 = (f32[32,80,128]{2,1,0:T(8,128)S(1)}, f32[32,80,128]{2,1,0:T(8,128)}, u32[]{:S(2)}, u32[]{:S(2)}) collective-permute-start(f32[32,80,128]{2,1,0:T(8,128)S(1)} %get-tuple-element.37.refs_1_), channel_id=1, source_target_pairs={{0,96},{32,0},{64,32},{96,64},{1,97},{33,1},{65,33},{97,65},{2,98}... | collective-permute-start | bytes 3932168 | tf_op jit(solution)/shard_map/ppermute | solution.py:606
  22.5 59.7 %collective-permute-start.9 = (f32[32,80,128]{2,1,0:T(8,128)S(1)}, f32[32,80,128]{2,1,0:T(8,128)}, u32[]{:S(2)}, u32[]{:S(2)}) collective-permute-start(f32[32,80,128]{2,1,0:T(8,128)S(1)} %get-tuple-element.38.refs_2_), channel_id=1, source_target_pairs={{0,64},{32,96},{64,0},{96,32},{1,65},{33,97},{65,1},{97,33},{2,66}... | collective-permute-start | bytes 3932168 | tf_op jit(solution)/shard_map/ppermute | solution.py:606
  31.9 50.3 %copy-start.2 = (bf16[4,256,384]{2,1,0:T(8,128)(2,1)}, bf16[4,256,384]{2,1,0:T(8,128)(2,1)S(1)}, u32[]{:S(2)}) copy-start(bf16[4,256,384]{2,1,0:T(8,128)(2,1)S(1)} %get-tuple-element.41.refs_3_) | copy-start | bytes 2359300
  31.9 50.3 %copy-start.4 = (bf16[2,4,128,256]{3,2,1,0:T(8,128)(2,1)}, bf16[2,4,128,256]{3,2,1,0:T(8,128)(2,1)S(1)}, u32[]{:S(2)}) copy-start(bf16[2,4,128,256]{3,2,1,0:T(8,128)(2,1)S(1)} %get-tuple-element.40.refs_2_) | copy-start | bytes 1572868
  31.9 50.3 %copy-start.9 = (bf16[160,256]{1,0:T(8,128)(2,1)}, bf16[160,256]{1,0:T(8,128)(2,1)S(1)}, u32[]{:S(2)}) copy-start(bf16[160,256]{1,0:T(8,128)(2,1)S(1)} %get-tuple-element.39.refs_1_) | copy-start | bytes 245764
  65.2 39.0 %collective-permute-start.6 = (f32[32,48,128]{2,1,0:T(8,128)S(1)}, f32[32,48,128]{2,1,0:T(8,128)S(1)}, u32[]{:S(2)}, u32[]{:S(2)}) collective-permute-start(f32[32,48,128]{2,1,0:T(8,128)S(1)} %get-tuple-element.46.refs_9_), channel_id=1, source_target_pairs={{0,32},{32,64},{64,96},{96,0},{1,33},{33,65},{65,97},{97,1},{2,34}... | collective-permute-start | bytes 2359304 | tf_op jit(solution)/shard_map/ppermute | solution.py:606
  66.5 43.5 %collective-permute-start.8 = (f32[32,48,128]{2,1,0:T(8,128)S(1)}, f32[32,48,128]{2,1,0:T(8,128)S(1)}, u32[]{:S(2)}, u32[]{:S(2)}) collective-permute-start(f32[32,48,128]{2,1,0:T(8,128)S(1)} %get-tuple-element.47.refs_10_), channel_id=1, source_target_pairs={{0,96},{32,0},{64,32},{96,64},{1,97},{33,1},{65,33},{97,65},{2,98}... | collective-permute-start | bytes 2359304 | tf_op jit(solution)/shard_map/ppermute | solution.py:606
  66.7 56.2 %collective-permute-start.10 = (f32[32,48,128]{2,1,0:T(8,128)}, f32[32,48,128]{2,1,0:T(8,128)}, u32[]{:S(2)}, u32[]{:S(2)}) collective-permute-start(f32[32,48,128]{2,1,0:T(8,128)} %get-tuple-element.48.refs_11_), channel_id=1, source_target_pairs={{0,64},{32,96},{64,0},{96,32},{1,65},{33,97},{65,1},{97,33},{2,66}... | collective-permute-start | bytes 2359304 | tf_op jit(solution)/shard_map/ppermute | solution.py:606
  97.2 15.3 %collective-permute-start.13 = (f32[32,32,128]{2,1,0:T(8,128)}, f32[32,32,128]{2,1,0:T(8,128)}, u32[]{:S(2)}, u32[]{:S(2)}) collective-permute-start(f32[32,32,128]{2,1,0:T(8,128)} %get-tuple-element.53), channel_id=1, source_target_pairs={{0,1},{1,2},{2,3},{3,4},{4,5},{5,6},{6,7},{7,8},{8,9},{9,10},{10,1... | collective-permute-start | bytes 1572872 | tf_op jit(solution)/shard_map/ppermute | solution.py:602
  102.3 10.1 %collective-permute-start.14 = (f32[32,16,128]{2,1,0:T(8,128)}, f32[32,16,128]{2,1,0:T(8,128)}, u32[]{:S(2)}, u32[]{:S(2)}) collective-permute-start(f32[32,16,128]{2,1,0:T(8,128)} %get-tuple-element.54), channel_id=1, source_target_pairs={{1,0},{2,1},{3,2},{4,3},{5,4},{6,5},{7,6},{8,7},{9,8},{10,9},{11,1... | collective-permute-start | bytes 786440 | tf_op jit(solution)/shard_map/ppermute | solution.py:602
  104.2 18.7 %collective-permute-start.11 = (f32[64,32,128]{2,1,0:T(8,128)}, f32[64,32,128]{2,1,0:T(8,128)}, u32[]{:S(2)}, u32[]{:S(2)}) collective-permute-start(f32[64,32,128]{2,1,0:T(8,128)} %get-tuple-element.50), channel_id=1, source_target_pairs={{0,1},{1,2},{2,3},{3,4},{4,5},{5,6},{6,7},{7,8},{8,9},{9,10},{10,1... | collective-permute-start | bytes 3145736 | tf_op jit(solution)/shard_map/ppermute | solution.py:602
  110.0 12.9 %collective-permute-start.12 = (f32[64,16,128]{2,1,0:T(8,128)}, f32[64,16,128]{2,1,0:T(8,128)}, u32[]{:S(2)}, u32[]{:S(2)}) collective-permute-start(f32[64,16,128]{2,1,0:T(8,128)} %get-tuple-element.51), channel_id=1, source_target_pairs={{1,0},{2,1},{3,2},{4,3},{5,4},{6,5},{7,6},{8,7},{9,8},{10,9},{11,1... | collective-permute-start | bytes 1572872 | tf_op jit(solution)/shard_map/ppermute | solution.py:602
  111.9 11.0 %copy-start.8 = (f32[64,32,128]{2,1,0:T(8,128)S(1)}, f32[64,32,128]{2,1,0:T(8,128)}, u32[]{:S(2)}) copy-start(f32[64,32,128]{2,1,0:T(8,128)} %get-tuple-element.49.own) | copy-start | bytes 3145732
  112.0 21.9 %copy-start.3 = (bf16[4,256,384]{2,1,0:T(8,128)(2,1)S(1)}, bf16[4,256,384]{2,1,0:T(8,128)(2,1)}, u32[]{:S(2)}) copy-start(bf16[4,256,384]{2,1,0:T(8,128)(2,1)} %copy-done.2) | copy-start | bytes 2359300
  112.0 21.9 %copy-start.5 = (bf16[2,4,128,256]{3,2,1,0:T(8,128)(2,1)S(1)}, bf16[2,4,128,256]{3,2,1,0:T(8,128)(2,1)}, u32[]{:S(2)}) copy-start(bf16[2,4,128,256]{3,2,1,0:T(8,128)(2,1)} %copy-done.4) | copy-start | bytes 1572868
  112.0 21.9 %copy-start.10 = (bf16[160,256]{1,0:T(8,128)(2,1)S(1)}, bf16[160,256]{1,0:T(8,128)(2,1)}, u32[]{:S(2)}) copy-start(bf16[160,256]{1,0:T(8,128)(2,1)} %copy-done.9) | copy-start | bytes 245764
  114.0 12.2 %collective-permute-start.15 = (f32[32,16,128]{2,1,0:T(8,128)S(1)}, f32[32,16,128]{2,1,0:T(8,128)S(1)}, u32[]{:S(2)}, u32[]{:S(2)}) collective-permute-start(f32[32,16,128]{2,1,0:T(8,128)S(1)} %get-tuple-element.55), channel_id=1, source_target_pairs={{0,32},{32,64},{64,96},{1,33},{33,65},{65,97},{2,34},{34,66},{66,9... | collective-permute-start | bytes 786440 | tf_op jit(solution)/shard_map/ppermute | solution.py:611
  115.9 15.3 %collective-permute-start.16 = (f32[32,16,128]{2,1,0:T(8,128)S(1)}, f32[32,16,128]{2,1,0:T(8,128)S(1)}, u32[]{:S(2)}, u32[]{:S(2)}) collective-permute-start(f32[32,16,128]{2,1,0:T(8,128)S(1)} %get-tuple-element.56), channel_id=1, source_target_pairs={{32,0},{64,32},{96,64},{33,1},{65,33},{97,65},{34,2},{66,34},{98,6... | collective-permute-start | bytes 786440 | tf_op jit(solution)/shard_map/ppermute | solution.py:611
  132.4 1.5 copy-start
  132.4 27.8 %collective-permute-start.21 = (f32[32,64,128]{2,1,0:T(8,128)S(1)}, f32[32,64,128]{2,1,0:T(8,128)S(1)}, u32[]{:S(2)}, u32[]{:S(2)}) collective-permute-start(f32[32,64,128]{2,1,0:T(8,128)S(1)} %shard_map.56.refs_12_.refs_2_), channel_id=1, source_target_pairs={{0,32},{32,64},{64,96},{96,0},{1,33},{33,65},{65,97},{97,1},{2,34}... | collective-permute-start | bytes 3145736 | tf_op jit(solution)/shard_map/ppermute | solution.py:606
  133.6 28.6 %collective-permute-start.22 = (f32[32,64,128]{2,1,0:T(8,128)S(1)}, f32[32,64,128]{2,1,0:T(8,128)S(1)}, u32[]{:S(2)}, u32[]{:S(2)}) collective-permute-start(f32[32,64,128]{2,1,0:T(8,128)S(1)} %shard_map.56.refs_12_.refs_2_), channel_id=1, source_target_pairs={{0,96},{32,0},{64,32},{96,64},{1,97},{33,1},{65,33},{97,65},{2,98}... | collective-permute-start | bytes 3145736 | tf_op jit(solution)/shard_map/ppermute | solution.py:606
  150.7 41.6 %copy-start.1 = (f32[32,64,128]{2,1,0:T(8,128)S(1)}, f32[32,64,128]{2,1,0:T(8,128)}, u32[]{:S(2)}) copy-start(f32[32,64,128]{2,1,0:T(8,128)} %copy-done) | copy-start | bytes 3145732
  150.7 28.5 %collective-permute-start.17 = (f32[64,32,128]{2,1,0:T(8,128)}, f32[64,32,128]{2,1,0:T(8,128)S(1)}, u32[]{:S(2)}, u32[]{:S(2)}) collective-permute-start(f32[64,32,128]{2,1,0:T(8,128)} %get-tuple-element.58), channel_id=1, source_target_pairs={{0,1},{1,2},{2,3},{3,4},{4,5},{5,6},{6,7},{7,8},{8,9},{9,10},{10,1... | collective-permute-start | bytes 3145736 | tf_op jit(solution)/shard_map/ppermute | solution.py:602
  155.9 17.5 %collective-permute-start.19 = (f32[32,32,128]{2,1,0:T(8,128)S(1)}, f32[32,32,128]{2,1,0:T(8,128)S(1)}, u32[]{:S(2)}, u32[]{:S(2)}) collective-permute-start(f32[32,32,128]{2,1,0:T(8,128)S(1)} %get-tuple-element.61), channel_id=1, source_target_pairs={{0,1},{1,2},{2,3},{3,4},{4,5},{5,6},{6,7},{7,8},{8,9},{9,10},{10,1... | collective-permute-start | bytes 1572872 | tf_op jit(solution)/shard_map/ppermute | solution.py:602
  157.8 19.5 %collective-permute-start.18 = (f32[64,16,128]{2,1,0:T(8,128)S(1)}, f32[64,16,128]{2,1,0:T(8,128)S(1)}, u32[]{:S(2)}, u32[]{:S(2)}) collective-permute-start(f32[64,16,128]{2,1,0:T(8,128)S(1)} %get-tuple-element.59), channel_id=1, source_target_pairs={{1,0},{2,1},{3,2},{4,3},{5,4},{6,5},{7,6},{8,7},{9,8},{10,9},{11,1... | collective-permute-start | bytes 1572872 | tf_op jit(solution)/shard_map/ppermute | solution.py:602
  160.2 13.0 %collective-permute-start.20 = (f32[32,16,128]{2,1,0:T(8,128)S(1)}, f32[32,16,128]{2,1,0:T(8,128)S(1)}, u32[]{:S(2)}, u32[]{:S(2)}) collective-permute-start(f32[32,16,128]{2,1,0:T(8,128)S(1)} %get-tuple-element.62), channel_id=1, source_target_pairs={{1,0},{2,1},{3,2},{4,3},{5,4},{6,5},{7,6},{8,7},{9,8},{10,9},{11,1... | collective-permute-start | bytes 786440 | tf_op jit(solution)/shard_map/ppermute | solution.py:602
  162.2 27.2 %collective-permute-start.25 = (f32[32,32,128]{2,1,0:T(8,128)S(1)}, f32[32,32,128]{2,1,0:T(8,128)S(1)}, u32[]{:S(2)}, u32[]{:S(2)}) collective-permute-start(f32[32,32,128]{2,1,0:T(8,128)S(1)} %slice.21), channel_id=1, source_target_pairs={{0,32},{32,64},{64,96},{96,0},{1,33},{33,65},{65,97},{97,1},{2,34}... | collective-permute-start | bytes 1572872 | tf_op jit(solution)/shard_map/ppermute | solution.py:606
  173.2 16.2 %collective-permute-start.26 = (f32[32,32,128]{2,1,0:T(8,128)S(1)}, f32[32,32,128]{2,1,0:T(8,128)S(1)}, u32[]{:S(2)}, u32[]{:S(2)}) collective-permute-start(f32[32,32,128]{2,1,0:T(8,128)S(1)} %slice.22), channel_id=1, source_target_pairs={{0,96},{32,0},{64,32},{96,64},{1,97},{33,1},{65,33},{97,65},{2,98}... | collective-permute-start | bytes 1572872 | tf_op jit(solution)/shard_map/ppermute | solution.py:606
  173.6 9.0 %collective-permute-start.23 = (f32[32,16,128]{2,1,0:T(8,128)S(1)}, f32[32,16,128]{2,1,0:T(8,128)S(1)}, u32[]{:S(2)}, u32[]{:S(2)}) collective-permute-start(f32[32,16,128]{2,1,0:T(8,128)S(1)} %get-tuple-element.63), channel_id=1, source_target_pairs={{0,32},{32,64},{64,96},{1,33},{33,65},{65,97},{2,34},{34,66},{66,9... | collective-permute-start | bytes 786440 | tf_op jit(solution)/shard_map/ppermute | solution.py:611
  177.3 12.1 %collective-permute-start.24 = (f32[32,16,128]{2,1,0:T(8,128)S(1)}, f32[32,16,128]{2,1,0:T(8,128)S(1)}, u32[]{:S(2)}, u32[]{:S(2)}) collective-permute-start(f32[32,16,128]{2,1,0:T(8,128)S(1)} %get-tuple-element.64), channel_id=1, source_target_pairs={{32,0},{64,32},{96,64},{33,1},{65,33},{97,65},{34,2},{66,34},{98,6... | collective-permute-start | bytes 786440 | tf_op jit(solution)/shard_map/ppermute | solution.py:611
  179.2 1.2 copy-start.7
  190.5 25.0 %collective-permute-start.27 = (f32[32,64,128]{2,1,0:T(8,128)S(1)}, f32[32,64,128]{2,1,0:T(8,128)S(1)}, u32[]{:S(2)}, u32[]{:S(2)}) collective-permute-start(f32[32,64,128]{2,1,0:T(8,128)S(1)} %shard_map.60.refs_3_.refs_2_), channel_id=1, source_target_pairs={{0,32},{32,64},{64,96},{96,0},{1,33},{33,65},{65,97},{97,1},{2,34}... | collective-permute-start | bytes 3145736 | tf_op jit(solution)/shard_map/ppermute | solution.py:606
  192.3 24.2 %collective-permute-start.29 = (f32[32,64,128]{2,1,0:T(8,128)S(1)}, f32[32,64,128]{2,1,0:T(8,128)S(1)}, u32[]{:S(2)}, u32[]{:S(2)}) collective-permute-start(f32[32,64,128]{2,1,0:T(8,128)S(1)} %shard_map.60.refs_3_.refs_2_), channel_id=1, source_target_pairs={{0,96},{32,0},{64,32},{96,64},{1,97},{33,1},{65,33},{97,65},{2,98}... | collective-permute-start | bytes 3145736 | tf_op jit(solution)/shard_map/ppermute | solution.py:606
  216.4 13.2 %collective-permute-start.28 = (f32[32,32,128]{2,1,0:T(8,128)}, f32[32,32,128]{2,1,0:T(8,128)}, u32[]{:S(2)}, u32[]{:S(2)}) collective-permute-start(f32[32,32,128]{2,1,0:T(8,128)} %slice.23), channel_id=1, source_target_pairs={{0,32},{32,64},{64,96},{96,0},{1,33},{33,65},{65,97},{97,1},{2,34}... | collective-permute-start | bytes 1572872 | tf_op jit(solution)/shard_map/ppermute | solution.py:606
  217.4 13.3 %collective-permute-start.30 = (f32[32,32,128]{2,1,0:T(8,128)}, f32[32,32,128]{2,1,0:T(8,128)}, u32[]{:S(2)}, u32[]{:S(2)}) collective-permute-start(f32[32,32,128]{2,1,0:T(8,128)} %slice.24), channel_id=1, source_target_pairs={{0,96},{32,0},{64,32},{96,64},{1,97},{33,1},{65,33},{97,65},{2,98}... | collective-permute-start | bytes 1572872 | tf_op jit(solution)/shard_map/ppermute | solution.py:606

commit v3 on v2

--- a/solution.py
+++ b/solution.py
@@ -16,6 +16,7 @@
 VIEWS = 4
 BACKGROUND = 0.1
 ALL = (0, 1, 3, 2)
+OTHERS = (1, 3, 2)
 ROWS = 64
 PACKED = ROWS // 2
 CHUNK = ROWS + PACKED
@@ -23,7 +24,7 @@
 ODD = WIDE + 1
 SKEW = CHUNK + 1
 FREE = 1 << 10
-LONG = 1 << 38
+MICROSECOND = 1 << 30
 SPANS = ((0, 80), (32, 128))
 VMEM = 48 * 1024 * 1024
 
@@ -209,13 +210,57 @@
     refs[-1][...] = jnp.zeros(refs[-1].shape, f32)
 
 
-def mark(after):
-    return small(mark_kernel, shape(8, 128), (), after, LONG)
-
-
-def window_kernel(spot, left, middle, right, *refs):
-    out, low, flat = refs[-3:]
+def mark(after, cost):
+    return small(mark_kernel, shape(8, 128), (), after, cost * MICROSECOND)
+
+
+def cut_moves(first, rows, q, recorded, holds, outs, sems):
+    reads, writes = [], []
+    for k, step in enumerate(OTHERS):
+        quarter = lax.rem(q + step, VIEWS)
+        lanes = pl.ds(pl.multiple_of(quarter * QUARTER, QUARTER), QUARTER)
+        source = recorded.at[:, pl.ds(first, rows), lanes]
+        reads.append(pltpu.make_async_copy(source, holds[k], sems.at[0, k]))
+        writes.append(pltpu.make_async_copy(holds[k], outs[k], sems.at[1, k]))
+    return reads, writes
+
+
+def cut_shapes(rows):
+    return (shape(SLAB, rows, QUARTER),) * len(OTHERS)
+
+
+def cut_scratch(rows):
+    holds = [pltpu.VMEM((SLAB, rows, QUARTER), f32)] * len(OTHERS)
+    return holds + [pltpu.SemaphoreType.DMA((2, len(OTHERS)))]
+
+
+def cut_steps(step, last, reads, writes):
+    @pl.when(step == 0)
+    def _():
+        for move in reads:
+            move.start()
+
+    @pl.when(step == 1)
+    def _():
+        for move, write in zip(reads, writes):
+            move.wait()
+            write.start()
+
+    def done():
+        @pl.when(step == last)
+        def _():
+            for write in writes:
+                write.wait()
+
+    return done
+
+
+def window_kernel(spot, left, middle, right, recorded, out, low, *refs):
+    n = len(OTHERS)
+    cuts, flat, holds, sems = refs[:n], refs[n], refs[n + 1 : 2 * n + 1], refs[-1]
     q = spot[0]
+    moves = cut_moves(0, CUT, q, recorded, holds, cuts, sems)
+    done = cut_steps(pl.program_id(0), SLAB // LEFT - 1, *moves)
     planes = middle.shape[0]
     for i in range(planes):
         before = left[i].T[QUARTER - LEFT :, :]
@@ -228,14 +273,16 @@
         row = flat[pl.ds(z, planes, ODD), :]
         out[z] = row
         low[z] = row
-
-
-def window(estimate, spot, after):
+    done()
+
+
+def window(estimate, spot, recorded):
+    hbm = pl.BlockSpec(memory_space=pl.ANY)
     n = LEFT
     block = (n, 128, QUARTER)
     return pl.pallas_call(
         window_kernel,
-        out_shape=(shape(WIDE, SLAB, 128), shape(WIDE, LEFT, 128)),
+        out_shape=(shape(WIDE, SLAB, 128), shape(WIDE, LEFT, 128)) + cut_shapes(CUT),
         grid_spec=pltpu.PrefetchScalarGridSpec(
             num_scalar_prefetch=1,
             grid=(SLAB // n,),
@@ -243,76 +290,61 @@
                 pl.BlockSpec(block, lambda i, s: (i, 0, jnp.maximum(s[0] - 1, 0))),
                 pl.BlockSpec(block, lambda i, s: (i, 0, s[0])),
                 pl.BlockSpec(block, lambda i, s: (i, 0, jnp.minimum(s[0] + 1, VIEWS - 1))),
-            ]
-            + [pl.BlockSpec(memory_space=pl.ANY)] * len(after),
+                hbm,
+            ],
             out_specs=(
                 pl.BlockSpec((WIDE, n, 128), lambda i, s: (0, i, 0)),
                 pl.BlockSpec((WIDE, n, 128), lambda i, s: (0, 0, 0)),
-            ),
-            scratch_shapes=[pltpu.VMEM((n * ODD + 7, 128), f32)],
+            )
+            + (hbm,) * len(OTHERS),
+            scratch_shapes=[pltpu.VMEM((n * ODD + 7, 128), f32)] + cut_scratch(CUT),
         ),
-        compiler_params=pltpu.CompilerParams(vmem_limit_bytes=VMEM),
+        compiler_params=pltpu.CompilerParams(vmem_limit_bytes=62 * 1024 * 1024),
         cost_estimate=pl.CostEstimate(flops=FREE, bytes_accessed=FREE, transcendentals=0),
-    )(spot, estimate, estimate, estimate, *after)
-
-
-def cut_kernel(first, rows, steps, spot, recorded, *refs):
-    n = len(steps)
-    outs, holds = refs[-2 * n - 2 : -n - 2], refs[-n - 2 : -2]
-    sems, out_sems = refs[-2:]
-    moves = []
-    for k, step in enumerate(steps):
-        quarter = lax.rem(spot[0] + step, VIEWS)
-        lanes = pl.ds(pl.multiple_of(quarter * QUARTER, QUARTER), QUARTER)
-        source = recorded.at[:, pl.ds(first, rows), lanes]
-        moves.append(pltpu.make_async_copy(source, holds[k], sems.at[k]))
-    for move in moves:
-        move.start()
-    writes = [pltpu.make_async_copy(holds[k], outs[k], out_sems.at[k]) for k in range(n)]
-    for move, write in zip(moves, writes):
-        move.wait()
-        write.start()
-    for write in writes:
-        write.wait()
-
-
-def cut(recorded, spot, first, rows, steps, after=()):
-    hbm = pl.BlockSpec(memory_space=pl.ANY)
-    return pl.pallas_call(
-        lambda *refs: cut_kernel(first, rows, steps, *refs),
-        out_shape=(shape(SLAB, rows, QUARTER),) * len(steps),
-        in_specs=[pl.BlockSpec(memory_space=pltpu.SMEM)] + [hbm] * (1 + len(after)),
-        out_specs=(hbm,) * len(steps),
-        scratch_shapes=[pltpu.VMEM((SLAB, rows, QUARTER), f32)] * len(steps)
-        + [pltpu.SemaphoreType.DMA((len(steps),))] * 2,
-        compiler_params=pltpu.CompilerParams(vmem_limit_bytes=VMEM),
-        cost_estimate=pl.CostEstimate(flops=FREE, bytes_accessed=FREE, transcendentals=0),
-    )(spot, recorded, *after)
-
-
-def forward_kernel(starts, ax, az, ay, lower, middle, upper, *refs):
-    out, blurred = refs[-2:]
+    )(spot, estimate, estimate, estimate, recorded)
+
+
+def forward_kernel(starts, ax, az, ay, lower, middle, upper, recorded, out, *refs):
+    n = len(OTHERS)
+    cuts, refs = refs[:n], refs[n:]
+    blurred, planes_of, load_sems = refs[0], refs[1:4], refs[4]
+    holds, sems = refs[5:-1], refs[-1]
     slot = pl.program_id(0)
+    moves = cut_moves(CUT, 128 - CUT, starts[VIEWS], recorded, holds, cuts, sems)
+    done = cut_steps(slot, VIEWS - 1, *moves)
+    step = 16
+
+    def loads(group):
+        at = pl.ds(pl.multiple_of(group * step, step), step)
+        return [
+            pltpu.make_async_copy(ref.at[at], planes_of[k].at[at], load_sems.at[k, group])
+            for k, ref in enumerate((lower, middle, upper))
+        ]
 
     @pl.when(slot == 0)
     def _():
+        for group in range(WIDE // step):
+            for move in loads(group):
+                move.start()
+
         def some(group, carry):
-            at = group * 8
+            for move in loads(group):
+                move.wait()
+            at = group * step
             columns = [
-                jnp.concatenate([lower[at + z], middle[at + z], upper[at + z]], axis=0)
-                for z in range(8)
+                jnp.concatenate([ref[at + z] for ref in planes_of], axis=0) for z in range(step)
             ]
             data = stacked(jnp.concatenate(columns, axis=1), 0, 256 - 3 * TALL)
             result = dot(ax[...], data)
-            for z in range(8):
+            for z in range(step):
                 blurred[pl.ds(at + z, VIEWS * SLAB, ODD), :] = result[:, z * 128 : z * 128 + 128]
             return carry
 
-        lax.fori_loop(0, WIDE // 8, some, 0)
+        lax.fori_loop(0, WIDE // step, some, 0)
 
     start = starts[slot]
     span = QUARTER + 2 * RADIUS
-    many = 8
+    many = SLAB
 
     def planes(group, carry):
         first = slot * SLAB + group * many
@@ -330,15 +362,19 @@
         return carry
 
     lax.fori_loop(0, SLAB // many, planes, 0)
-
-
-def forward_of(starts, ax, az, ay, lower, middle, upper):
+    done()
+
+
+def forward_of(starts, ax, az, ay, lower, middle, upper, recorded):
+    hbm = pl.BlockSpec(memory_space=pl.ANY)
+    rows = 128 - CUT
+
     def once(x):
         return pl.BlockSpec(x.shape, lambda v, s: (0,) * x.ndim, pipeline_mode=pl.Buffered(1))
 
     return pl.pallas_call(
         forward_kernel,
-        out_shape=shape(VIEWS * SLAB, 128, QUARTER),
+        out_shape=(shape(VIEWS * SLAB, 128, QUARTER),) + cut_shapes(rows),
         grid_spec=pltpu.PrefetchScalarGridSpec(
             num_scalar_prefetch=1,
             grid=(VIEWS,),
@@ -346,16 +382,21 @@
                 once(ax),
                 pl.BlockSpec((1,) + az.shape[1:], lambda v, s: (v, 0, 0)),
                 pl.BlockSpec((1,) + ay.shape[1:], lambda v, s: (v, 0, 0)),
-                once(lower),
-                once(middle),
-                once(upper),
+                hbm,
+                hbm,
+                hbm,
+                hbm,
             ],
-            out_specs=pl.BlockSpec((SLAB, 128, QUARTER), lambda v, s: (v, 0, 0)),
-            scratch_shapes=[pltpu.VMEM((VIEWS * SLAB * ODD + 8, 128), f32)],
+            out_specs=(pl.BlockSpec((SLAB, 128, QUARTER), lambda v, s: (v, 0, 0)),)
+            + (hbm,) * len(OTHERS),
+            scratch_shapes=[pltpu.VMEM((VIEWS * SLAB * ODD + 8, 128), f32)]
+            + [pltpu.VMEM(x.shape, f32) for x in (lower, middle, upper)]
+            + [pltpu.SemaphoreType.DMA((3, WIDE // 16))]
+            + cut_scratch(rows),
         ),
         compiler_params=pltpu.CompilerParams(vmem_limit_bytes=VMEM),
         cost_estimate=pl.CostEstimate(flops=FREE, bytes_accessed=FREE, transcendentals=0),
-    )(starts, ax, az, ay, lower, middle, upper)
+    )(starts, ax, az, ay, lower, middle, upper, recorded)
 
 
 def adjoint_kernel(chunk, extra, *refs):
@@ -376,7 +417,7 @@
             if chunk:
                 measured[-1].append(refs.pop(0))
     refs = refs[extra:]
-    outs, refs = refs[:6], refs[6:]
+    outs, refs = refs[:5], refs[5:]
     hold, kept, spread = refs[0], refs[1 : 1 + pieces], refs[1 + pieces]
     totals = refs[2 + pieces : 5 + pieces]
     sems, out_sems = refs[-2:]
@@ -391,7 +432,7 @@
             move.start()
         copies.append(moves)
 
-    many = 8
+    many = SLAB
     lane = lax.broadcasted_iota(jnp.int32, (PACKED, 128), 1)
     for k, slot in enumerate(ALL):
         for move in copies[k]:
@@ -427,17 +468,16 @@
         lax.fori_loop(0, SLAB // many, planes, 0)
 
     total = band.shape[1]
-    step = 8
+    step = 32
 
     centers = ROWS // step
 
     def sends(group, edge):
         at = pl.ds(pl.multiple_of(group * step, step), step)
         to = pl.ds(pl.multiple_of((group - edge * centers) * step, step), step)
+        targets = outs[0].at[at], outs[1 + 2 * edge].at[to], outs[2 + 2 * edge].at[to]
         return [
-            pltpu.make_async_copy(
-                totals[k].at[at], outs[3 * edge + k].at[to], out_sems.at[k, group]
-            )
+            pltpu.make_async_copy(totals[k].at[at], targets[k], out_sems.at[k, group])
             for k in range(3)
         ]
 
@@ -478,16 +518,17 @@
     arrays += after
     return pl.pallas_call(
         lambda *refs: adjoint_kernel(chunk, len(after), *refs),
-        out_shape=tuple(shape(r, k, 128) for r in (ROWS, PACKED) for k in sizes),
+        out_shape=(shape(CHUNK, LEFT, 128),)
+        + tuple(shape(r, k, 128) for r in (ROWS, PACKED) for k in sizes[1:]),
         in_specs=[pl.BlockSpec(memory_space=pltpu.SMEM)] + [vmem] * 3 + [hbm] * len(arrays),
-        out_specs=(hbm,) * 6,
+        out_specs=(hbm,) * 5,
         scratch_shapes=[pltpu.VMEM((n, SLAB, last - first, QUARTER), f32)]
         + [pltpu.VMEM((n, SLAB, k, QUARTER), f32) for k in rows]
         + [pltpu.VMEM((n * SLAB * SKEW + 8, 128), f32)]
         + [pltpu.VMEM((CHUNK, k, 128), f32) for k in sizes]
         + [
             pltpu.SemaphoreType.DMA((n, chunk + 2)),
-            pltpu.SemaphoreType.DMA((3, CHUNK // 8)),
+            pltpu.SemaphoreType.DMA((3, CHUNK // 32)),
         ],
         compiler_params=pltpu.CompilerParams(vmem_limit_bytes=VMEM),
         cost_estimate=pl.CostEstimate(flops=FREE, bytes_accessed=FREE, transcendentals=0),
@@ -497,19 +538,19 @@
 def added(own, up, down):
     half = SLAB // 2
     whole = own[...] + up[...]
-    return whole[:, :half], whole[:, half:] + down[...]
+    return whole[:, :half], whole[:, half:] + down
 
 
 def edges_kernel(own, up, down, *refs):
     rights, lefts = refs[-2:]
-    near, far = added(own, up, down)
+    near, far = added(own, up, down[ROWS:])
     lane = lax.broadcasted_iota(jnp.int32, (1, SLAB // 2, 128), 2) % 64
     rights[...] = jnp.where(lane < RIGHT, near, pltpu.roll(far, RIGHT, 2))
     lefts[...] = jnp.where(lane < RIGHT + LEFT, near, pltpu.roll(far, LEFT, 2))
 
 
 def center_kernel(own, up, down, *refs):
-    refs[-1][...] = jnp.concatenate(added(own, up, down), axis=1)
+    refs[-1][...] = jnp.concatenate(added(own, up, down[:ROWS]), axis=1)
 
 
 def small(kernel, out_shape, arrays, after, flops):
@@ -527,7 +568,7 @@
 
 def settle_edges(own, up, down, after):
     packed = shape(PACKED, SLAB // 2, 128)
-    return small(edges_kernel, (packed, packed), (own, up, down), after, FREE)
+    return small(edges_kernel, (packed, packed), (own, up, down), after, 5 * MICROSECOND)
 
 
 def settle_center(own, up, down, after):
@@ -535,7 +576,6 @@
 
 
 def merge_kernel(center, rights, lefts, *refs):
-    out = refs[-1]
     lane = lax.broadcasted_iota(jnp.int32, (SLAB // 2, 128), 1)
     turns = (((0, 64), (96, 32)), ((80, 16), (64, 0)))
     for piece in (0, 1):
@@ -550,12 +590,12 @@
                 high = jnp.where(lane >= QUARTER - LEFT, high, 0.0)
                 extra.append(jnp.where(lane < RIGHT, low, high))
             at = piece * PACKED + r
-            out[:, at, :] = center[at] + jnp.concatenate(extra, axis=0)
+            refs[piece - 2][:, r, :] = center[at] + jnp.concatenate(extra, axis=0)
 
 
 def merge(center, rights, lefts, after):
     arrays = (center, rights, lefts)
-    return small(merge_kernel, shape(SLAB, ROWS, 128), arrays, after, FREE)
+    return small(merge_kernel, (shape(SLAB, PACKED, 128),) * 2, arrays, after, FREE)
 
 
 def finish_kernel(count, spot, estimate, *refs):
@@ -567,7 +607,7 @@
         first = first + piece.shape[1]
 
 
-def finish(chunk, step, spot, estimate, pieces, before, after, flops):
+def finish(chunk, step, spot, estimate, pieces, before, after):
     n = 32
     place = pl.BlockSpec(
         (n, ROWS, QUARTER), lambda i, s: (i, chunk, lax.rem(s[0] + (VIEWS - step), VIEWS))
@@ -591,7 +631,7 @@
         place,
         prefetch=1,
         aliases=aliases,
-        flops=flops,
+        flops=FREE,
         moved=FREE,
     )(*arrays)
 
@@ -615,58 +655,54 @@
     q = lax.axis_index("view")
     spot = q[None]
     recorded = views[0]
-    middle, last = window(estimate, spot, ())
+    middle, last, *pieces = window(estimate, spot, recorded)
     upper = along_blk(middle, -1)
     lower = along_blk(last, 1)
 
     mine = pack(psf[0], offsets[0].astype(f32)[:, None], (middle,))
     params = jnp.stack([mine] + [around_view(mine, s) for s in (1, 2, 3)])
-    others = (1, 3, 2)
-    pieces = cut(recorded, spot, 0, CUT, others, (params,))
-    measured = ({s: around_view(piece, s) for s, piece in zip(others, pieces)}, {})
-    starts = params[:, 2, KERN].astype(jnp.int32)
-    ax, az, ay, ayt, wz, every = bands(params, pieces)
-    forward = forward_of(starts, ax, az, ay, lower, middle, upper)
-    pieces = cut(recorded, spot, CUT, 128 - CUT, others, (forward,))
-    measured[1].update({s: around_view(piece, s) for s, piece in zip(others, pieces)})
+    measured = ({s: around_view(piece, s) for s, piece in zip(OTHERS, pieces)}, {})
+    starts = jnp.concatenate([params[:, 2, KERN].astype(jnp.int32), spot])
+    ax, az, ay, ayt, wz, every = bands(params, ())
+    forward, *pieces = forward_of(starts, ax, az, ay, lower, middle, upper, recorded)
+    measured[1].update({s: around_view(piece, s) for s, piece in zip(OTHERS, pieces)})
 
     def spill(parts):
-        below, own, above = parts
-        return own, along_blk(above, 1), along_blk(below, -1)
+        below, own, above, own_edge, above_edge = parts
+        down = along_blk(below, -1)
+        return (own_edge, along_blk(above_edge, 1), down), (own, along_blk(above, 1), down)
 
     def margins(edges):
         rights, lefts = edges
         return along_view(rights, 1), along_view(lefts, -1)
 
     def gather(piece):
-        left = around_view(piece, 1)
-        right = around_view(piece, 3)
-        near = around_view(left[:, : ROWS // 2], 1)
-        far = around_view(right[:, ROWS // 2 :], 3)
-        return piece, left, right, near, far
+        near, far = piece
+        left = around_view(near, 1), around_view(far, 1)
+        right = around_view(near, 3), around_view(far, 3)
+        opposite = around_view(left[0], 1), around_view(right[1], 3)
+        return piece, left, right, opposite
 
     def adjoint_of(chunk, after):
         return adjoint(chunk, spot, every, ayt, wz, forward, recorded, measured, after)
 
-    parts0 = adjoint_of(0, pieces)
-    spilled0 = spill(parts0[3:]), spill(parts0[:3])
-    margins0 = margins(settle_edges(*spilled0[0], (mark((measured[1][1], measured[1][3])),)))
+    parts0 = adjoint_of(0, ())
+    spilled0 = spill(parts0)
+    margins0 = margins(settle_edges(*spilled0[0], (mark((measured[1][1], measured[1][3]), 16),)))
     center0 = settle_center(*spilled0[1], (measured[1][2],))
     piece0 = merge(center0, *margins0, ())
     gathered0 = gather(piece0)
-    parts1 = adjoint_of(1, (piece0,))
-    spilled1 = spill(parts1[3:]), spill(parts1[:3])
-    margins1 = margins(settle_edges(*spilled1[0], gathered0[1:3]))
+    parts1 = adjoint_of(1, tuple(piece0))
+    spilled1 = spill(parts1)
+    margins1 = margins(settle_edges(*spilled1[0], (mark((gathered0[1][0], gathered0[2][1]), 8),)))
     center1 = settle_center(*spilled1[1], ())
-    piece1 = merge(center1, *margins1, gathered0[3:])
+    piece1 = merge(center1, *margins1, gathered0[3] + (gathered0[1][1], gathered0[2][0]))
     gathered1 = gather(piece1)
     out = None
     for chunk, gathered in enumerate((gathered0, gathered1)):
-        piece, left, right, near, far = gathered
-        for step, parts in ((0, (piece,)), (1, (left,)), (3, (right,)), (2, (near, far))):
-            after = (piece1,) if out is None else ()
-            flops = LONG if (chunk, step) == (1, 1) else FREE
-            out = finish(chunk, step, spot, estimate, parts, out, after, flops)
+        for step, parts in zip((0, 1, 3, 2), gathered):
+            after = () if out is not None else (gathered1[1][0], gathered1[2][1])
+            out = finish(chunk, step, spot, estimate, parts, out, after)
     return out
 
 

time: 238 us -> 212 us (0.89)
  Pallas kernels: 93.1 us -> 68.5 us
    pallas_call x2, Pallas kernels: 31.7 us -> 17.3 us  [adjoint(): pl.pallas_call(lambda *refs: adjoint_kernel(chunk, len(after), *refs), ou...]
    pallas_call x3 -> x1, Pallas kernels: 24.2 us -> 15.1 us  [forward_of(): pl.pallas_call(forward_kernel, out_shape=(shape(VIEWS * SLAB, 128, QUARTE...]
    ppermute x4, waiting for transfers between devices: 15.5 us -> 8.35 us  [along_view(): return lax.ppermute(x, 'view', route)]
    ppermute x10 -> x8, waiting for transfers between devices: 22.3 us -> 28.7 us  [along_blk(): return lax.ppermute(x, 'blk', route)]
    ppermute x17 -> x21, starting transfers between devices: 18.1 us -> 21.5 us  [around_view(): lax.ppermute(x, 'view', [(i, (i + distance) % VIEWS) for i in range(VIEWS)])]
    ppermute x17 -> x21, waiting for transfers between devices: 33.5 us -> 36.5 us  [around_view(): lax.ppermute(x, 'view', [(i, (i + distance) % VIEWS) for i in range(VIEWS)])]
    pallas_call x8 -> x9, Pallas kernels: 5.8 us -> 2.93 us  [small(): pl.pallas_call(kernel, out_shape=out_shape, in_specs=[vmem] * len(arrays)...]
    ppermute x10 -> x8, starting transfers between devices: 33.7 us -> 31.3 us  [along_blk(): return lax.ppermute(x, 'blk', route)]
  transfers between devices with their start and end apart: 31 -> 33, of which waited for: 14 -> 13; matrix products, arithmetic and copies ran while one was open for 1% -> 0% of each run, Pallas kernels for 36% -> 27%
where the time goes in v3:
time: 212 us; the launch traced here: 209 us
  waiting for transfers between devices  73.5 us (35%)
  Pallas kernels  68.5 us (32%)
  starting transfers between devices  63.5 us (30%)
  local copies, waits for them, and re-layouts  2.99 us (1%)
    ppermute x21, waiting for transfers between devices, around_view(): lax.ppermute(x, 'view', [(i, (i + distance) % VIEWS) for i in range(VIEWS)])  36.5 us
    ppermute x8, starting transfers between devices, along_blk(): return lax.ppermute(x, 'blk', route)  31.3 us
    ppermute x8, waiting for transfers between devices, along_blk(): return lax.ppermute(x, 'blk', route)  28.7 us
    ppermute x21, starting transfers between devices, around_view(): lax.ppermute(x, 'view', [(i, (i + distance) % VIEWS) for i in range(VIEWS)])  21.5 us
    pallas_call x8, Pallas kernels, finish(): call(lambda *refs: finish_kernel(len(pieces), *refs), shape(*estimate.sha...  18.7 us
    pallas_call x2, Pallas kernels, adjoint(): pl.pallas_call(lambda *refs: adjoint_kernel(chunk, len(after), *refs), ou...  17.3 us
    pallas_call x1, Pallas kernels, forward_of(): pl.pallas_call(forward_kernel, out_shape=(shape(VIEWS * SLAB, 128, QUARTE...  15.1 us
    ppermute x4, starting transfers between devices, along_view(): return lax.ppermute(x, 'view', route)  10.7 us
  transfers between devices with their start and end apart: 33, of which 13 were waited for; matrix products, arithmetic and copies ran while one was open for 0% of the time, Pallas kernels for 27%

profile of v3, /device:TPU:59, one launch (start us, length us, event | category | flops | bytes accessed | tf_op | source)
XLA Modules:
  0.0 209.2 jit_solution(6978318070457862561)
XLA Ops:
  0.0 7.6 %shard_map.46 = (f32[176,32,128]{2,1,0:T(8,128)}, f32[176,16,128]{2,1,0:T(8,128)}, f32[32,80,128]{2,1,0:T(8,128)}, f32[32,80,128]{2,1,0:T(8,128)}, f32[32,80,128]{2,1,0:T(8,128)}) custom-call(s32[1]{0:T(128)} %bitcast.spot.refs_0_, f32[32,128,512]{2,1,0:T(8,128)} %refs_1_.15, f32[32,128,512]{2,1,0:T(8,128)} %refs_1_.15, f32[32,128,512]{2,1,0:T(8,128)} %refs_1_.15, ...), custom_call_target="tpu_custom_call" | custom-call | flops 1024 | bytes 1024 | tf_op jit(solution)/shard_map/pallas_call | solution.py:283
  7.6 2.6 %collective-permute-start.4 = (f32[176,32,128]{2,1,0:T(8,128)}, f32[176,32,128]{2,1,0:T(8,128)}, u32[]{:S(2)}, u32[]{:S(2)}) collective-permute-start(f32[176,32,128]{2,1,0:T(8,128)} %get-tuple-element.38.refs_0_.middle), channel_id=1, source_target_pairs={{1,0},{2,1},{3,2},{4,3},{5,4},{6,5},{7,6},{8,7},{9,8},{10,9},{11,1... | collective-permute-start | bytes 8650760 | tf_op jit(solution)/shard_map/ppermute | solution.py:642
  10.2 5.1 %collective-permute-start.3 = (f32[176,16,128]{2,1,0:T(8,128)}, f32[176,16,128]{2,1,0:T(8,128)S(1)}, u32[]{:S(2)}, u32[]{:S(2)}) collective-permute-start(f32[176,16,128]{2,1,0:T(8,128)} %get-tuple-element.45), channel_id=1, source_target_pairs={{0,1},{1,2},{2,3},{3,4},{4,5},{5,6},{6,7},{7,8},{8,9},{9,10},{10,1... | collective-permute-start | bytes 4325384 | tf_op jit(solution)/shard_map/ppermute | solution.py:642
  15.4 1.8 copy-done
  17.4 2.3 %collective-permute-start.1 = (f32[3,34]{1,0:T(4,128)S(1)}, f32[3,34]{1,0:T(4,128)S(1)}, u32[]{:S(2)}, u32[]{:S(2)}) collective-permute-start(f32[3,34]{1,0:T(4,128)S(1)} %shard_map.47), channel_id=1, source_target_pairs={{0,64},{32,96},{64,0},{96,32},{1,65},{33,97},{65,1},{97,33},{2,66}... | collective-permute-start | bytes 1232 | tf_op jit(solution)/shard_map/ppermute | solution.py:646
  19.7 1.5 collective-permute-start
  21.4 2.7 %collective-permute-start.7 = (f32[32,80,128]{2,1,0:T(8,128)}, f32[32,80,128]{2,1,0:T(8,128)S(1)}, u32[]{:S(2)}, u32[]{:S(2)}) collective-permute-start(f32[32,80,128]{2,1,0:T(8,128)} %get-tuple-element.49), channel_id=1, source_target_pairs={{0,96},{32,0},{64,32},{96,64},{1,97},{33,1},{65,33},{97,65},{2,98}... | collective-permute-start | bytes 3932168 | tf_op jit(solution)/shard_map/ppermute | solution.py:646
  24.3 6.9 %shard_map.48 = (bf16[128,256]{1,0:T(8,128)(2,1)S(1)}, bf16[4,128,512]{2,1,0:T(8,128)(2,1)S(1)}, bf16[4,128,384]{2,1,0:T(8,128)(2,1)S(1)}, bf16[2,4,128,256]{3,2...) custom-call(f32[4,3,34]{2,1,0:T(4,128)S(1)} %pad_maximum_fusion.params), custom_call_target="tpu_custom_call" | custom-call | flops 1024 | bytes 1024 | tf_op jit(solution)/shard_map/pallas_call | solution.py:187
  31.6 14.3 %collective-permute-done.4.upper = f32[176,32,128]{2,1,0:T(8,128)} collective-permute-done((f32[176,32,128]{2,1,0:T(8,128)}, f32[176,32,128]{2,1,0:T(8,128)}, u32[]{:S(2)}, u32[]{:S(2)}) %collective-permute-start.4) | collective-permute-done | bytes 2883616 | tf_op jit(solution)/shard_map/ppermute | solution.py:642
  45.8 15.1 %shard_map.49 = (f32[128,128,128]{2,1,0:T(8,128)}, f32[32,48,128]{2,1,0:T(8,128)S(1)}, f32[32,48,128]{2,1,0:T(8,128)S(1)}, f32[32,48,128]{2,1,0:T(8,128)S(1)}) custom-call(s32[5]{0:T(128)S(1)} %pad_add_fusion.starts, bf16[128,256]{1,0:T(8,128)(2,1)S(1)} %get-tuple-element.42.ax, bf16[4,128,512]{2,1,0:T(8,128)(2,1)S(1)} %get-tuple-element.43.az, ...), custom_call_target="tpu_custom_call" | custom-call | flops 1024 | bytes 1024 | tf_op jit(solution)/shard_map/pallas_call | solution.py:375
  60.9 1.3 collective-permute-start.6
  62.5 1.8 collective-permute-start.10
  64.3 17.3 %collective-permute-done.9.refs_8_.refs_10_ = f32[32,80,128]{2,1,0:T(8,128)S(1)} collective-permute-done((f32[32,80,128]{2,1,0:T(8,128)}, f32[32,80,128]{2,1,0:T(8,128)S(1)}, u32[]{:S(2)}, u32[]{:S(2)}) %collective-permute-start.9) | collective-permute-done | bytes 1310752 | tf_op jit(solution)/shard_map/ppermute | solution.py:646
  82.7 8.1 %shard_map.50 = (f32[96,16,128]{2,1,0:T(8,128)S(1)}, f32[64,32,128]{2,1,0:T(8,128)S(1)}, f32[64,32,128]{2,1,0:T(8,128)S(1)}, f32[32,32,128]{2,1,0:T(8,128)S(1)}, f32[32,32,128]{2,1,0:T(8,128)S(1)}) custom-call(s32[1]{0:T(128)} %bitcast.spot.refs_0_, bf16[160,256]{1,0:T(8,128)(2,1)S(1)} %get-tuple-element.39.refs_1_, ...), custom_call_target="tpu_custom_call" | custom-call | flops 1024 | bytes 1024 | tf_op jit(solution)/shard_map/pallas_call | solution.py:519
  90.8 4.6 %collective-permute-start.13 = (f32[32,32,128]{2,1,0:T(8,128)S(1)}, f32[32,32,128]{2,1,0:T(8,128)S(1)}, u32[]{:S(2)}, u32[]{:S(2)}) collective-permute-start(f32[32,32,128]{2,1,0:T(8,128)S(1)} %get-tuple-element.57), channel_id=1, source_target_pairs={{0,1},{1,2},{2,3},{3,4},{4,5},{5,6},{6,7},{7,8},{8,9},{9,10},{10,1... | collective-permute-start | bytes 1572872 | tf_op jit(solution)/shard_map/ppermute | solution.py:642
  95.4 1.9 collective-permute-start.12
  97.3 5.8 %collective-permute-start.11 = (f32[64,32,128]{2,1,0:T(8,128)S(1)}, f32[64,32,128]{2,1,0:T(8,128)S(1)}, u32[]{:S(2)}, u32[]{:S(2)}) collective-permute-start(f32[64,32,128]{2,1,0:T(8,128)S(1)} %get-tuple-element.54), channel_id=1, source_target_pairs={{0,1},{1,2},{2,3},{3,4},{4,5},{5,6},{6,7},{7,8},{8,9},{9,10},{10,1... | collective-permute-start | bytes 3145736 | tf_op jit(solution)/shard_map/ppermute | solution.py:642
  103.1 7.7 %collective-permute-done.12.down = f32[96,16,128]{2,1,0:T(8,128)S(1)} collective-permute-done((f32[96,16,128]{2,1,0:T(8,128)S(1)}, f32[96,16,128]{2,1,0:T(8,128)S(1)}, u32[]{:S(2)}, u32[]{:S(2)}) %collective-permute-start.12) | collective-permute-done | bytes 786464 | tf_op jit(solution)/shard_map/ppermute | solution.py:642
  111.0 1.9 collective-permute-start.14
  112.9 3.4 %collective-permute-start.15 = (f32[32,16,128]{2,1,0:T(8,128)S(1)}, f32[32,16,128]{2,1,0:T(8,128)S(1)}, u32[]{:S(2)}, u32[]{:S(2)}) collective-permute-start(f32[32,16,128]{2,1,0:T(8,128)S(1)} %get-tuple-element.59), channel_id=1, source_target_pairs={{32,0},{64,32},{96,64},{33,1},{65,33},{97,65},{34,2},{66,34},{98,6... | collective-permute-start | bytes 786440 | tf_op jit(solution)/shard_map/ppermute | solution.py:651
  116.5 1.6 collective-permute-done.14.rights
  118.1 3.8 %collective-permute-done.15.lefts = f32[32,16,128]{2,1,0:T(8,128)S(1)} collective-permute-done((f32[32,16,128]{2,1,0:T(8,128)S(1)}, f32[32,16,128]{2,1,0:T(8,128)S(1)}, u32[]{:S(2)}, u32[]{:S(2)}) %collective-permute-start.15) | collective-permute-done | bytes 262176 | tf_op jit(solution)/shard_map/ppermute | solution.py:651
  123.0 1.8 collective-permute-start.19
  126.4 9.2 %shard_map.55 = (f32[96,16,128]{2,1,0:T(8,128)S(1)}, f32[64,32,128]{2,1,0:T(8,128)}, f32[64,32,128]{2,1,0:T(8,128)}, f32[32,32,128]{2,1,0:T(8,128)S(1)}, f32[32,32,128]{2,1,0:T(8,128)S(1)}) custom-call(s32[1]{0:T(128)} %bitcast.spot.refs_0_, bf16[160,256]{1,0:T(8,128)(2,1)S(1)} %get-tuple-element.39.refs_1_, ...), custom_call_target="tpu_custom_call" | custom-call | flops 1024 | bytes 1024 | tf_op jit(solution)/shard_map/pallas_call | solution.py:519
  135.6 3.6 %collective-permute-start.18 = (f32[32,32,128]{2,1,0:T(8,128)S(1)}, f32[32,32,128]{2,1,0:T(8,128)S(1)}, u32[]{:S(2)}, u32[]{:S(2)}) collective-permute-start(f32[32,32,128]{2,1,0:T(8,128)S(1)} %get-tuple-element.66), channel_id=1, source_target_pairs={{0,1},{1,2},{2,3},{3,4},{4,5},{5,6},{6,7},{7,8},{8,9},{9,10},{10,1... | collective-permute-start | bytes 1572872 | tf_op jit(solution)/shard_map/ppermute | solution.py:642
  139.2 1.9 collective-permute-start.17
  141.2 5.8 %collective-permute-start.16 = (f32[64,32,128]{2,1,0:T(8,128)}, f32[64,32,128]{2,1,0:T(8,128)S(1)}, u32[]{:S(2)}, u32[]{:S(2)}) collective-permute-start(f32[64,32,128]{2,1,0:T(8,128)} %get-tuple-element.63), channel_id=1, source_target_pairs={{0,1},{1,2},{2,3},{3,4},{4,5},{5,6},{6,7},{7,8},{8,9},{9,10},{10,1... | collective-permute-start | bytes 3145736 | tf_op jit(solution)/shard_map/ppermute | solution.py:642
  147.0 1.6 collective-permute-start.23
  148.5 6.1 %collective-permute-done.17.down = f32[96,16,128]{2,1,0:T(8,128)S(1)} collective-permute-done((f32[96,16,128]{2,1,0:T(8,128)S(1)}, f32[96,16,128]{2,1,0:T(8,128)S(1)}, u32[]{:S(2)}, u32[]{:S(2)}) %collective-permute-start.17) | collective-permute-done | bytes 786464 | tf_op jit(solution)/shard_map/ppermute | solution.py:642
  154.7 1.1 collective-permute-start.24
  156.0 2.4 %collective-permute-start.21 = (f32[32,16,128]{2,1,0:T(8,128)S(1)}, f32[32,16,128]{2,1,0:T(8,128)S(1)}, u32[]{:S(2)}, u32[]{:S(2)}) collective-permute-start(f32[32,16,128]{2,1,0:T(8,128)S(1)} %get-tuple-element.67), channel_id=1, source_target_pairs={{0,32},{32,64},{64,96},{1,33},{33,65},{65,97},{2,34},{34,66},{66,9... | collective-permute-start | bytes 786440 | tf_op jit(solution)/shard_map/ppermute | solution.py:651
  159.0 3.0 %collective-permute-start.22 = (f32[32,16,128]{2,1,0:T(8,128)S(1)}, f32[32,16,128]{2,1,0:T(8,128)S(1)}, u32[]{:S(2)}, u32[]{:S(2)}) collective-permute-start(f32[32,16,128]{2,1,0:T(8,128)S(1)} %get-tuple-element.68), channel_id=1, source_target_pairs={{32,0},{64,32},{96,64},{33,1},{65,33},{97,65},{34,2},{66,34},{98,6... | collective-permute-start | bytes 786440 | tf_op jit(solution)/shard_map/ppermute | solution.py:651
  162.2 4.1 %collective-permute-done.24.refs_1_.refs_3_ = f32[32,32,128]{2,1,0:T(8,128)S(1)} collective-permute-done((f32[32,32,128]{2,1,0:T(8,128)S(1)}, f32[32,32,128]{2,1,0:T(8,128)S(1)}, u32[]{:S(2)}, u32[]{:S(2)}) %collective-permute-start.24) | collective-permute-done | bytes 524320 | tf_op jit(solution)/shard_map/ppermute | solution.py:646
  166.3 2.9 %collective-permute-done.22.lefts = f32[32,16,128]{2,1,0:T(8,128)S(1)} collective-permute-done((f32[32,16,128]{2,1,0:T(8,128)S(1)}, f32[32,16,128]{2,1,0:T(8,128)S(1)}, u32[]{:S(2)}, u32[]{:S(2)}) %collective-permute-start.22) | collective-permute-done | bytes 262176 | tf_op jit(solution)/shard_map/ppermute | solution.py:651
  170.3 1.5 collective-permute-start.27
  171.8 1.4 collective-permute-start.32
  173.7 10.6 %collective-permute-done.27.refs_4_.refs_2_ = f32[32,32,128]{2,1,0:T(8,128)S(1)} collective-permute-done((f32[32,32,128]{2,1,0:T(8,128)S(1)}, f32[32,32,128]{2,1,0:T(8,128)S(1)}, u32[]{:S(2)}, u32[]{:S(2)}) %collective-permute-start.27) | collective-permute-done | bytes 524320 | tf_op jit(solution)/shard_map/ppermute | solution.py:646
  184.3 1.4 collective-permute-start.28
  186.2 2.3 %shard_map.60.refs_4_ = f32[32,128,512]{2,1,0:T(8,128)} custom-call(s32[1]{0:T(128)} %bitcast.spot.refs_0_, f32[32,128,512]{2,1,0:T(8,128)} %refs_1_.15, f32[32,32,128]{2,1,0:T(8,128)S(1)} %get-tuple-element.60.refs_12_.refs_2_, f32[32,32,128]{2,1,0:T(8,128)S(1)} %get-tuple-element.61.refs_13_.refs_3_, ...), custom_call_target="tpu_custom_call" | custom-call | flops 1024 | bytes 1024 | tf_op jit(solution)/shard_map/pallas_call | solution.py:626
  188.5 2.3 %shard_map.61.refs_4_ = f32[32,128,512]{2,1,0:T(8,128)} custom-call(s32[1]{0:T(128)} %bitcast.spot.refs_0_, f32[32,128,512]{2,1,0:T(8,128)} %refs_1_.15, f32[32,32,128]{2,1,0:T(8,128)S(1)} %collective-permute-done.19.refs_0_.refs_2_, f32[32,32,128]{2,1,0:T(8,128)S(1)} %collective-permute-done.25.refs_2_.refs_3_, ...), custom_call_target="tpu_custom_call", output_to_operand_aliasing={{}: (4, {})} | custom-call | flops 1024 | bytes 1024 | tf_op jit(solution)/shard_map/pallas_call | solution.py:626
  190.9 2.3 %shard_map.62.refs_4_ = f32[32,128,512]{2,1,0:T(8,128)} custom-call(s32[1]{0:T(128)} %bitcast.spot.refs_0_, f32[32,128,512]{2,1,0:T(8,128)} %refs_1_.15, f32[32,32,128]{2,1,0:T(8,128)S(1)} %collective-permute-done.26.refs_3_.refs_2_, f32[32,32,128]{2,1,0:T(8,128)S(1)} %collective-permute-done.20.refs_1_.refs_3_, ...), custom_call_target="tpu_custom_call", output_to_operand_aliasing={{}: (4, {})} | custom-call | flops 1024 | bytes 1024 | tf_op jit(solution)/shard_map/pallas_call | solution.py:626
  193.2 2.3 %shard_map.63.refs_4_ = f32[32,128,512]{2,1,0:T(8,128)} custom-call(s32[1]{0:T(128)} %bitcast.spot.refs_0_, f32[32,128,512]{2,1,0:T(8,128)} %refs_1_.15, f32[32,32,128]{2,1,0:T(8,128)S(1)} %collective-permute-done.23.refs_0_.refs_2_, f32[32,32,128]{2,1,0:T(8,128)S(1)} %collective-permute-done.24.refs_1_.refs_3_, ...), custom_call_target="tpu_custom_call", output_to_operand_aliasing={{}: (4, {})} | custom-call | flops 1024 | bytes 1024 | tf_op jit(solution)/shard_map/pallas_call | solution.py:626
  195.5 2.3 %shard_map.64.refs_4_ = f32[32,128,512]{2,1,0:T(8,128)} custom-call(s32[1]{0:T(128)} %bitcast.spot.refs_0_, f32[32,128,512]{2,1,0:T(8,128)} %refs_1_.15, f32[32,32,128]{2,1,0:T(8,128)S(1)} %get-tuple-element.69.refs_2_, f32[32,32,128]{2,1,0:T(8,128)S(1)} %get-tuple-element.70.refs_3_, f32[32,128,512]{2,1,0:T(8,128)} %shard_map.63.refs_4_), custom_call_target="tpu_custom_call", output_to_operand_aliasing={{}: (4, {})} | custom-call | flops 1024 | bytes 1024 | tf_op jit(solution)/shard_map/pallas_call | solution.py:626
  197.9 2.3 %shard_map.65.refs_4_ = f32[32,128,512]{2,1,0:T(8,128)} custom-call(s32[1]{0:T(128)} %bitcast.spot.refs_0_, f32[32,128,512]{2,1,0:T(8,128)} %refs_1_.15, f32[32,32,128]{2,1,0:T(8,128)S(1)} %collective-permute-done.27.refs_4_.refs_2_, f32[32,32,128]{2,1,0:T(8,128)S(1)} %collective-permute-done.32.refs_3_, ...), custom_call_target="tpu_custom_call", output_to_operand_aliasing={{}: (4, {})} | custom-call | flops 1024 | bytes 1024 | tf_op jit(solution)/shard_map/pallas_call | solution.py:626
  200.2 2.3 %shard_map.66.refs_4_ = f32[32,128,512]{2,1,0:T(8,128)} custom-call(s32[1]{0:T(128)} %bitcast.spot.refs_0_, f32[32,128,512]{2,1,0:T(8,128)} %refs_1_.15, f32[32,32,128]{2,1,0:T(8,128)S(1)} %collective-permute-done.31.refs_2_, f32[32,32,128]{2,1,0:T(8,128)S(1)} %collective-permute-done.29.refs_5_.refs_3_, ...), custom_call_target="tpu_custom_call", output_to_operand_aliasing={{}: (4, {})} | custom-call | flops 1024 | bytes 1024 | tf_op jit(solution)/shard_map/pallas_call | solution.py:626
  202.5 2.9 %collective-permute-done.28.refs_2_ = f32[32,32,128]{2,1,0:T(8,128)S(1)} collective-permute-done((f32[32,32,128]{2,1,0:T(8,128)S(1)}, f32[32,32,128]{2,1,0:T(8,128)S(1)}, u32[]{:S(2)}, u32[]{:S(2)}) %collective-permute-start.28) | collective-permute-done | bytes 524320 | tf_op jit(solution)/shard_map/ppermute | solution.py:646
  205.5 1.4 collective-permute-done.30.refs_3_
  206.9 2.3 %shard_map.67 = f32[32,128,512]{2,1,0:T(8,128)} custom-call(s32[1]{0:T(128)} %bitcast.spot.refs_0_, f32[32,128,512]{2,1,0:T(8,128)} %refs_1_.15, f32[32,32,128]{2,1,0:T(8,128)S(1)} %collective-permute-done.28.refs_2_, f32[32,32,128]{2,1,0:T(8,128)S(1)} %collective-permute-done.30.refs_3_, ...), custom_call_target="tpu_custom_call", output_to_operand_aliasing={{}: (4, {})} | custom-call | flops 1024 | bytes 1024 | tf_op jit(solution)/shard_map/pallas_call | solution.py:626
  (62 shorter events, 8.1 us)
Async XLA Ops:
  0.0 15.3 %copy-start.7 = (s32[1,3]{1,0:T(1,128)S(1)}, s32[1,3]{1,0:T(1,128)}, u32[]{:S(2)}) copy-start(s32[1,3]{1,0:T(1,128)} %param.7) | copy-start | bytes 40
  0.0 15.4 %copy-start.6 = (f32[1,3,33]{2,0,1:T(1,128)S(1)}, f32[1,3,33]{2,0,1:T(1,128)}, u32[]{:S(2)}) copy-start(f32[1,3,33]{2,0,1:T(1,128)} %param.6) | copy-start | bytes 1192
  7.6 38.2 %collective-permute-start.4 = (f32[176,32,128]{2,1,0:T(8,128)}, f32[176,32,128]{2,1,0:T(8,128)}, u32[]{:S(2)}, u32[]{:S(2)}) collective-permute-start(f32[176,32,128]{2,1,0:T(8,128)} %get-tuple-element.38.refs_0_.middle), channel_id=1, source_target_pairs={{1,0},{2,1},{3,2},{4,3},{5,4},{6,5},{7,6},{8,7},{9,8},{10,9},{11,1... | collective-permute-start | bytes 8650760 | tf_op jit(solution)/shard_map/ppermute | solution.py:642
  10.2 21.3 %collective-permute-start.3 = (f32[176,16,128]{2,1,0:T(8,128)}, f32[176,16,128]{2,1,0:T(8,128)S(1)}, u32[]{:S(2)}, u32[]{:S(2)}) collective-permute-start(f32[176,16,128]{2,1,0:T(8,128)} %get-tuple-element.45), channel_id=1, source_target_pairs={{0,1},{1,2},{2,3},{3,4},{4,5},{5,6},{6,7},{7,8},{8,9},{9,10},{10,1... | collective-permute-start | bytes 4325384 | tf_op jit(solution)/shard_map/ppermute | solution.py:642
  15.4 1.8 copy-start
  17.3 3.9 %collective-permute-start.2 = (f32[3,34]{1,0:T(4,128)S(1)}, f32[3,34]{1,0:T(4,128)S(1)}, u32[]{:S(2)}, u32[]{:S(2)}) collective-permute-start(f32[3,34]{1,0:T(4,128)S(1)} %shard_map.47), channel_id=1, source_target_pairs={{0,96},{32,0},{64,32},{96,64},{1,97},{33,1},{65,33},{97,65},{2,98}... | collective-permute-start | bytes 1232 | tf_op jit(solution)/shard_map/ppermute | solution.py:646
  17.4 3.9 %collective-permute-start.1 = (f32[3,34]{1,0:T(4,128)S(1)}, f32[3,34]{1,0:T(4,128)S(1)}, u32[]{:S(2)}, u32[]{:S(2)}) collective-permute-start(f32[3,34]{1,0:T(4,128)S(1)} %shard_map.47), channel_id=1, source_target_pairs={{0,64},{32,96},{64,0},{96,32},{1,65},{33,97},{65,1},{97,33},{2,66}... | collective-permute-start | bytes 1232 | tf_op jit(solution)/shard_map/ppermute | solution.py:646
  19.7 4.4 %collective-permute-start = (f32[3,34]{1,0:T(4,128)S(1)}, f32[3,34]{1,0:T(4,128)S(1)}, u32[]{:S(2)}, u32[]{:S(2)}) collective-permute-start(f32[3,34]{1,0:T(4,128)S(1)} %shard_map.47), channel_id=1, source_target_pairs={{0,32},{32,64},{64,96},{96,0},{1,33},{33,65},{65,97},{97,1},{2,34}... | collective-permute-start | bytes 1232 | tf_op jit(solution)/shard_map/ppermute | solution.py:646
  21.2 41.2 %collective-permute-start.5 = (f32[32,80,128]{2,1,0:T(8,128)}, f32[32,80,128]{2,1,0:T(8,128)S(1)}, u32[]{:S(2)}, u32[]{:S(2)}) collective-permute-start(f32[32,80,128]{2,1,0:T(8,128)} %get-tuple-element.47), channel_id=1, source_target_pairs={{0,32},{32,64},{64,96},{96,0},{1,33},{33,65},{65,97},{97,1},{2,34}... | collective-permute-start | bytes 3932168 | tf_op jit(solution)/shard_map/ppermute | solution.py:646
  21.4 42.9 %collective-permute-start.7 = (f32[32,80,128]{2,1,0:T(8,128)}, f32[32,80,128]{2,1,0:T(8,128)S(1)}, u32[]{:S(2)}, u32[]{:S(2)}) collective-permute-start(f32[32,80,128]{2,1,0:T(8,128)} %get-tuple-element.49), channel_id=1, source_target_pairs={{0,96},{32,0},{64,32},{96,64},{1,97},{33,1},{65,33},{97,65},{2,98}... | collective-permute-start | bytes 3932168 | tf_op jit(solution)/shard_map/ppermute | solution.py:646
  24.1 57.5 %collective-permute-start.9 = (f32[32,80,128]{2,1,0:T(8,128)}, f32[32,80,128]{2,1,0:T(8,128)S(1)}, u32[]{:S(2)}, u32[]{:S(2)}) collective-permute-start(f32[32,80,128]{2,1,0:T(8,128)} %get-tuple-element.51), channel_id=1, source_target_pairs={{0,64},{32,96},{64,0},{96,32},{1,65},{33,97},{65,1},{97,33},{2,66}... | collective-permute-start | bytes 3932168 | tf_op jit(solution)/shard_map/ppermute | solution.py:646
  60.9 36.4 %collective-permute-start.6 = (f32[32,48,128]{2,1,0:T(8,128)S(1)}, f32[32,48,128]{2,1,0:T(8,128)S(1)}, u32[]{:S(2)}, u32[]{:S(2)}) collective-permute-start(f32[32,48,128]{2,1,0:T(8,128)S(1)} %get-tuple-element.48), channel_id=1, source_target_pairs={{0,32},{32,64},{64,96},{96,0},{1,33},{33,65},{65,97},{97,1},{2,34}... | collective-permute-start | bytes 2359304 | tf_op jit(solution)/shard_map/ppermute | solution.py:646
  62.2 40.8 %collective-permute-start.8 = (f32[32,48,128]{2,1,0:T(8,128)S(1)}, f32[32,48,128]{2,1,0:T(8,128)S(1)}, u32[]{:S(2)}, u32[]{:S(2)}) collective-permute-start(f32[32,48,128]{2,1,0:T(8,128)S(1)} %get-tuple-element.50), channel_id=1, source_target_pairs={{0,96},{32,0},{64,32},{96,64},{1,97},{33,1},{65,33},{97,65},{2,98}... | collective-permute-start | bytes 2359304 | tf_op jit(solution)/shard_map/ppermute | solution.py:646
  62.5 20.2 %copy-start.3 = (f32[32,80,128]{2,1,0:T(8,128)}, f32[32,80,128]{2,1,0:T(8,128)S(1)}, u32[]{:S(2)}) copy-start(f32[32,80,128]{2,1,0:T(8,128)S(1)} %collective-permute-done.5.refs_6_) | copy-start | bytes 3932164
  62.5 53.8 %collective-permute-start.10 = (f32[32,48,128]{2,1,0:T(8,128)S(1)}, f32[32,48,128]{2,1,0:T(8,128)S(1)}, u32[]{:S(2)}, u32[]{:S(2)}) collective-permute-start(f32[32,48,128]{2,1,0:T(8,128)S(1)} %get-tuple-element.52), channel_id=1, source_target_pairs={{0,64},{32,96},{64,0},{96,32},{1,65},{33,97},{65,1},{97,33},{2,66}... | collective-permute-start | bytes 2359304 | tf_op jit(solution)/shard_map/ppermute | solution.py:646
  64.3 18.4 %copy-start.4 = (f32[32,80,128]{2,1,0:T(8,128)}, f32[32,80,128]{2,1,0:T(8,128)S(1)}, u32[]{:S(2)}) copy-start(f32[32,80,128]{2,1,0:T(8,128)S(1)} %collective-permute-done.7.refs_7_.refs_8_) | copy-start | bytes 3932164
  81.6 1.1 copy-start.5
  90.8 12.3 %collective-permute-start.13 = (f32[32,32,128]{2,1,0:T(8,128)S(1)}, f32[32,32,128]{2,1,0:T(8,128)S(1)}, u32[]{:S(2)}, u32[]{:S(2)}) collective-permute-start(f32[32,32,128]{2,1,0:T(8,128)S(1)} %get-tuple-element.57), channel_id=1, source_target_pairs={{0,1},{1,2},{2,3},{3,4},{4,5},{5,6},{6,7},{7,8},{8,9},{9,10},{10,1... | collective-permute-start | bytes 1572872 | tf_op jit(solution)/shard_map/ppermute | solution.py:642
  95.4 15.4 %collective-permute-start.12 = (f32[96,16,128]{2,1,0:T(8,128)S(1)}, f32[96,16,128]{2,1,0:T(8,128)S(1)}, u32[]{:S(2)}, u32[]{:S(2)}) collective-permute-start(f32[96,16,128]{2,1,0:T(8,128)S(1)} %get-tuple-element.55), channel_id=1, source_target_pairs={{1,0},{2,1},{3,2},{4,3},{5,4},{6,5},{7,6},{8,7},{9,8},{10,9},{11,1... | collective-permute-start | bytes 2359304 | tf_op jit(solution)/shard_map/ppermute | solution.py:642
  97.3 19.0 %collective-permute-start.11 = (f32[64,32,128]{2,1,0:T(8,128)S(1)}, f32[64,32,128]{2,1,0:T(8,128)S(1)}, u32[]{:S(2)}, u32[]{:S(2)}) collective-permute-start(f32[64,32,128]{2,1,0:T(8,128)S(1)} %get-tuple-element.54), channel_id=1, source_target_pairs={{0,1},{1,2},{2,3},{3,4},{4,5},{5,6},{6,7},{7,8},{8,9},{9,10},{10,1... | collective-permute-start | bytes 3145736 | tf_op jit(solution)/shard_map/ppermute | solution.py:642
  111.0 7.1 %collective-permute-start.14 = (f32[32,16,128]{2,1,0:T(8,128)S(1)}, f32[32,16,128]{2,1,0:T(8,128)S(1)}, u32[]{:S(2)}, u32[]{:S(2)}) collective-permute-start(f32[32,16,128]{2,1,0:T(8,128)S(1)} %get-tuple-element.58), channel_id=1, source_target_pairs={{0,32},{32,64},{64,96},{1,33},{33,65},{65,97},{2,34},{34,66},{66,9... | collective-permute-start | bytes 786440 | tf_op jit(solution)/shard_map/ppermute | solution.py:651
  112.9 9.0 %collective-permute-start.15 = (f32[32,16,128]{2,1,0:T(8,128)S(1)}, f32[32,16,128]{2,1,0:T(8,128)S(1)}, u32[]{:S(2)}, u32[]{:S(2)}) collective-permute-start(f32[32,16,128]{2,1,0:T(8,128)S(1)} %get-tuple-element.59), channel_id=1, source_target_pairs={{32,0},{64,32},{96,64},{33,1},{65,33},{97,65},{34,2},{66,34},{98,6... | collective-permute-start | bytes 786440 | tf_op jit(solution)/shard_map/ppermute | solution.py:651
  116.3 10.0 %copy-start.1 = (f32[32,48,128]{2,1,0:T(8,128)}, f32[32,48,128]{2,1,0:T(8,128)S(1)}, u32[]{:S(2)}) copy-start(f32[32,48,128]{2,1,0:T(8,128)S(1)} %collective-permute-done.10.refs_0_.refs_11_) | copy-start | bytes 2359300
  123.0 16.2 %collective-permute-start.19 = (f32[32,32,128]{2,1,0:T(8,128)S(1)}, f32[32,32,128]{2,1,0:T(8,128)S(1)}, u32[]{:S(2)}, u32[]{:S(2)}) collective-permute-start(f32[32,32,128]{2,1,0:T(8,128)S(1)} %get-tuple-element.60.refs_12_.refs_2_), channel_id=1, source_target_pairs={{0,32},{32,64},{64,96},{96,0},{1,33},{33,65},{65,97},{97,1},{2,34}... | collective-permute-start | bytes 1572872 | tf_op jit(solution)/shard_map/ppermute | solution.py:646
  124.8 16.3 %collective-permute-start.20 = (f32[32,32,128]{2,1,0:T(8,128)S(1)}, f32[32,32,128]{2,1,0:T(8,128)S(1)}, u32[]{:S(2)}, u32[]{:S(2)}) collective-permute-start(f32[32,32,128]{2,1,0:T(8,128)S(1)} %get-tuple-element.61.refs_13_.refs_3_), channel_id=1, source_target_pairs={{0,96},{32,0},{64,32},{96,64},{1,97},{33,1},{65,33},{97,65},{2,98}... | collective-permute-start | bytes 1572872 | tf_op jit(solution)/shard_map/ppermute | solution.py:646
  124.9 31.2 %collective-permute-start.26 = (f32[32,32,128]{2,1,0:T(8,128)S(1)}, f32[32,32,128]{2,1,0:T(8,128)S(1)}, u32[]{:S(2)}, u32[]{:S(2)}) collective-permute-start(f32[32,32,128]{2,1,0:T(8,128)S(1)} %get-tuple-element.60.refs_12_.refs_2_), channel_id=1, source_target_pairs={{0,96},{32,0},{64,32},{96,64},{1,97},{33,1},{65,33},{97,65},{2,98}... | collective-permute-start | bytes 1572872 | tf_op jit(solution)/shard_map/ppermute | solution.py:646
  125.3 36.8 %collective-permute-start.25 = (f32[32,32,128]{2,1,0:T(8,128)S(1)}, f32[32,32,128]{2,1,0:T(8,128)S(1)}, u32[]{:S(2)}, u32[]{:S(2)}) collective-permute-start(f32[32,32,128]{2,1,0:T(8,128)S(1)} %get-tuple-element.61.refs_13_.refs_3_), channel_id=1, source_target_pairs={{0,32},{32,64},{64,96},{96,0},{1,33},{33,65},{65,97},{97,1},{2,34}... | collective-permute-start | bytes 1572872 | tf_op jit(solution)/shard_map/ppermute | solution.py:646
  135.6 11.4 %collective-permute-start.18 = (f32[32,32,128]{2,1,0:T(8,128)S(1)}, f32[32,32,128]{2,1,0:T(8,128)S(1)}, u32[]{:S(2)}, u32[]{:S(2)}) collective-permute-start(f32[32,32,128]{2,1,0:T(8,128)S(1)} %get-tuple-element.66), channel_id=1, source_target_pairs={{0,1},{1,2},{2,3},{3,4},{4,5},{5,6},{6,7},{7,8},{8,9},{9,10},{10,1... | collective-permute-start | bytes 1572872 | tf_op jit(solution)/shard_map/ppermute | solution.py:642
  139.2 15.4 %collective-permute-start.17 = (f32[96,16,128]{2,1,0:T(8,128)S(1)}, f32[96,16,128]{2,1,0:T(8,128)S(1)}, u32[]{:S(2)}, u32[]{:S(2)}) collective-permute-start(f32[96,16,128]{2,1,0:T(8,128)S(1)} %get-tuple-element.64), channel_id=1, source_target_pairs={{1,0},{2,1},{3,2},{4,3},{5,4},{6,5},{7,6},{8,7},{9,8},{10,9},{11,1... | collective-permute-start | bytes 2359304 | tf_op jit(solution)/shard_map/ppermute | solution.py:642
  141.2 17.8 %collective-permute-start.16 = (f32[64,32,128]{2,1,0:T(8,128)}, f32[64,32,128]{2,1,0:T(8,128)S(1)}, u32[]{:S(2)}, u32[]{:S(2)}) collective-permute-start(f32[64,32,128]{2,1,0:T(8,128)} %get-tuple-element.63), channel_id=1, source_target_pairs={{0,1},{1,2},{2,3},{3,4},{4,5},{5,6},{6,7},{7,8},{8,9},{9,10},{10,1... | collective-permute-start | bytes 3145736 | tf_op jit(solution)/shard_map/ppermute | solution.py:642
  147.0 15.2 %collective-permute-start.23 = (f32[32,32,128]{2,1,0:T(8,128)S(1)}, f32[32,32,128]{2,1,0:T(8,128)S(1)}, u32[]{:S(2)}, u32[]{:S(2)}) collective-permute-start(f32[32,32,128]{2,1,0:T(8,128)S(1)} %collective-permute-done.19.refs_0_.refs_2_), channel_id=1, source_target_pairs={{0,32},{32,64},{64,96},{96,0},{1,33},{33,65},{65,97},{97,1},{2,34}... | collective-permute-start | bytes 1572872 | tf_op jit(solution)/shard_map/ppermute | solution.py:646
  154.7 11.6 %collective-permute-start.24 = (f32[32,32,128]{2,1,0:T(8,128)S(1)}, f32[32,32,128]{2,1,0:T(8,128)S(1)}, u32[]{:S(2)}, u32[]{:S(2)}) collective-permute-start(f32[32,32,128]{2,1,0:T(8,128)S(1)} %collective-permute-done.20.refs_1_.refs_3_), channel_id=1, source_target_pairs={{0,96},{32,0},{64,32},{96,64},{1,97},{33,1},{65,33},{97,65},{2,98}... | collective-permute-start | bytes 1572872 | tf_op jit(solution)/shard_map/ppermute | solution.py:646
  155.8 6.2 %copy-start.2 = (f32[64,32,128]{2,1,0:T(8,128)S(1)}, f32[64,32,128]{2,1,0:T(8,128)}, u32[]{:S(2)}) copy-start(f32[64,32,128]{2,1,0:T(8,128)} %get-tuple-element.62.own) | copy-start | bytes 3145732
  156.0 10.2 %collective-permute-start.21 = (f32[32,16,128]{2,1,0:T(8,128)S(1)}, f32[32,16,128]{2,1,0:T(8,128)S(1)}, u32[]{:S(2)}, u32[]{:S(2)}) collective-permute-start(f32[32,16,128]{2,1,0:T(8,128)S(1)} %get-tuple-element.67), channel_id=1, source_target_pairs={{0,32},{32,64},{64,96},{1,33},{33,65},{65,97},{2,34},{34,66},{66,9... | collective-permute-start | bytes 786440 | tf_op jit(solution)/shard_map/ppermute | solution.py:651
  159.0 10.2 %collective-permute-start.22 = (f32[32,16,128]{2,1,0:T(8,128)S(1)}, f32[32,16,128]{2,1,0:T(8,128)S(1)}, u32[]{:S(2)}, u32[]{:S(2)}) collective-permute-start(f32[32,16,128]{2,1,0:T(8,128)S(1)} %get-tuple-element.68), channel_id=1, source_target_pairs={{32,0},{64,32},{96,64},{33,1},{65,33},{97,65},{34,2},{66,34},{98,6... | collective-permute-start | bytes 786440 | tf_op jit(solution)/shard_map/ppermute | solution.py:651
  170.3 14.0 %collective-permute-start.27 = (f32[32,32,128]{2,1,0:T(8,128)S(1)}, f32[32,32,128]{2,1,0:T(8,128)S(1)}, u32[]{:S(2)}, u32[]{:S(2)}) collective-permute-start(f32[32,32,128]{2,1,0:T(8,128)S(1)} %get-tuple-element.69.refs_2_), channel_id=1, source_target_pairs={{0,32},{32,64},{64,96},{96,0},{1,33},{33,65},{65,97},{97,1},{2,34}... | collective-permute-start | bytes 1572872 | tf_op jit(solution)/shard_map/ppermute | solution.py:646
  171.8 14.0 %collective-permute-start.29 = (f32[32,32,128]{2,1,0:T(8,128)S(1)}, f32[32,32,128]{2,1,0:T(8,128)S(1)}, u32[]{:S(2)}, u32[]{:S(2)}) collective-permute-start(f32[32,32,128]{2,1,0:T(8,128)S(1)} %get-tuple-element.70.refs_3_), channel_id=1, source_target_pairs={{0,96},{32,0},{64,32},{96,64},{1,97},{33,1},{65,33},{97,65},{2,98}... | collective-permute-start | bytes 1572872 | tf_op jit(solution)/shard_map/ppermute | solution.py:646
  171.8 26.1 %collective-permute-start.32 = (f32[32,32,128]{2,1,0:T(8,128)S(1)}, f32[32,32,128]{2,1,0:T(8,128)S(1)}, u32[]{:S(2)}, u32[]{:S(2)}) collective-permute-start(f32[32,32,128]{2,1,0:T(8,128)S(1)} %get-tuple-element.70.refs_3_), channel_id=1, source_target_pairs={{0,32},{32,64},{64,96},{96,0},{1,33},{33,65},{65,97},{97,1},{2,34}... | collective-permute-start | bytes 1572872 | tf_op jit(solution)/shard_map/ppermute | solution.py:646
  173.2 27.0 %collective-permute-start.31 = (f32[32,32,128]{2,1,0:T(8,128)S(1)}, f32[32,32,128]{2,1,0:T(8,128)S(1)}, u32[]{:S(2)}, u32[]{:S(2)}) collective-permute-start(f32[32,32,128]{2,1,0:T(8,128)S(1)} %get-tuple-element.69.refs_2_), channel_id=1, source_target_pairs={{0,96},{32,0},{64,32},{96,64},{1,97},{33,1},{65,33},{97,65},{2,98}... | collective-permute-start | bytes 1572872 | tf_op jit(solution)/shard_map/ppermute | solution.py:646
  184.3 21.1 %collective-permute-start.28 = (f32[32,32,128]{2,1,0:T(8,128)S(1)}, f32[32,32,128]{2,1,0:T(8,128)S(1)}, u32[]{:S(2)}, u32[]{:S(2)}) collective-permute-start(f32[32,32,128]{2,1,0:T(8,128)S(1)} %collective-permute-done.27.refs_4_.refs_2_), channel_id=1, source_target_pairs={{0,32},{32,64},{64,96},{96,0},{1,33},{33,65},{65,97},{97,1},{2,34}... | collective-permute-start | bytes 1572872 | tf_op jit(solution)/shard_map/ppermute | solution.py:646
  185.7 21.1 %collective-permute-start.30 = (f32[32,32,128]{2,1,0:T(8,128)S(1)}, f32[32,32,128]{2,1,0:T(8,128)S(1)}, u32[]{:S(2)}, u32[]{:S(2)}) collective-permute-start(f32[32,32,128]{2,1,0:T(8,128)S(1)} %collective-permute-done.29.refs_5_.refs_3_), channel_id=1, source_target_pairs={{0,96},{32,0},{64,32},{96,64},{1,97},{33,1},{65,33},{97,65},{2,98}... | collective-permute-start | bytes 1572872 | tf_op jit(solution)/shard_map/ppermute | solution.py:646

commit v4 on v3

--- a/solution.py
+++ b/solution.py
@@ -255,7 +255,8 @@
     return done
 
 
-def window_kernel(spot, left, middle, right, recorded, out, low, *refs):
+def window_kernel(spot, left, middle, right, recorded, out, low, token, *refs):
+    token[...] = jnp.zeros(token.shape, f32)
     n = len(OTHERS)
     cuts, flat, holds, sems = refs[:n], refs[n], refs[n + 1 : 2 * n + 1], refs[-1]
     q = spot[0]
@@ -282,7 +283,8 @@
     block = (n, 128, QUARTER)
     return pl.pallas_call(
         window_kernel,
-        out_shape=(shape(WIDE, SLAB, 128), shape(WIDE, LEFT, 128)) + cut_shapes(CUT),
+        out_shape=(shape(WIDE, SLAB, 128), shape(WIDE, LEFT, 128), shape(8, 128))
+        + cut_shapes(CUT),
         grid_spec=pltpu.PrefetchScalarGridSpec(
             num_scalar_prefetch=1,
             grid=(SLAB // n,),
@@ -295,6 +297,7 @@
             out_specs=(
                 pl.BlockSpec((WIDE, n, 128), lambda i, s: (0, i, 0)),
                 pl.BlockSpec((WIDE, n, 128), lambda i, s: (0, 0, 0)),
+                pl.BlockSpec((8, 128), lambda i, s: (0, 0)),
             )
             + (hbm,) * len(OTHERS),
             scratch_shapes=[pltpu.VMEM((n * ODD + 7, 128), f32)] + cut_scratch(CUT),
@@ -608,7 +611,7 @@
 
 
 def finish(chunk, step, spot, estimate, pieces, before, after):
-    n = 32
+    n = 16
     place = pl.BlockSpec(
         (n, ROWS, QUARTER), lambda i, s: (i, chunk, lax.rem(s[0] + (VIEWS - step), VIEWS))
     )
@@ -655,11 +658,11 @@
     q = lax.axis_index("view")
     spot = q[None]
     recorded = views[0]
-    middle, last, *pieces = window(estimate, spot, recorded)
+    middle, last, token, *pieces = window(estimate, spot, recorded)
     upper = along_blk(middle, -1)
     lower = along_blk(last, 1)
 
-    mine = pack(psf[0], offsets[0].astype(f32)[:, None], (middle,))
+    mine = pack(psf[0], offsets[0].astype(f32)[:, None], (token,))
     params = jnp.stack([mine] + [around_view(mine, s) for s in (1, 2, 3)])
     measured = ({s: around_view(piece, s) for s, piece in zip(OTHERS, pieces)}, {})
     starts = jnp.concatenate([params[:, 2, KERN].astype(jnp.int32), spot])

time: 212 us -> 211 us (level)
  transfers between devices with their start and end apart: 33 -> 33, of which waited for: 13 -> 14; matrix products, arithmetic and copies ran while one was open for 0% -> 0% of each run, Pallas kernels for 27% -> 26%
where the time goes in v4:
time: 211 us; the launch traced here: 208 us
  waiting for transfers between devices  75.2 us (36%)
  Pallas kernels  66.5 us (32%)
  starting transfers between devices  63.5 us (30%)
    ppermute x21, waiting for transfers between devices, around_view(): lax.ppermute(x, 'view', [(i, (i + distance) % VIEWS) for i in range(VIEWS)])  37 us
    ppermute x8, starting transfers between devices, along_blk(): return lax.ppermute(x, 'blk', route)  31.3 us
    ppermute x8, waiting for transfers between devices, along_blk(): return lax.ppermute(x, 'blk', route)  29.8 us
    ppermute x21, starting transfers between devices, around_view(): lax.ppermute(x, 'view', [(i, (i + distance) % VIEWS) for i in range(VIEWS)])  21.5 us
    pallas_call x2, Pallas kernels, adjoint(): pl.pallas_call(lambda *refs: adjoint_kernel(chunk, len(after), *refs), ou...  17.3 us
    pallas_call x8, Pallas kernels, finish(): call(lambda *refs: finish_kernel(len(pieces), *refs), shape(*estimate.sha...  16.7 us
    pallas_call x1, Pallas kernels, forward_of(): pl.pallas_call(forward_kernel, out_shape=(shape(VIEWS * SLAB, 128, QUARTE...  15.1 us
    ppermute x4, starting transfers between devices, along_view(): return lax.ppermute(x, 'view', route)  10.7 us
  transfers between devices with their start and end apart: 33, of which 14 were waited for; matrix products, arithmetic and copies ran while one was open for 0% of the time, Pallas kernels for 26%

profile of v4, /device:TPU:59, one launch (start us, length us, event | category | flops | bytes accessed | tf_op | source)
XLA Modules:
  0.0 207.8 jit_solution(12923351560846580053)
XLA Ops:
  0.0 7.6 %shard_map.46 = (f32[176,32,128]{2,1,0:T(8,128)}, f32[176,16,128]{2,1,0:T(8,128)}, f32[8,128]{1,0:T(8,128)}, f32[32,80,128]{2,1,0:T(8,128)}, f32[32,80,128]{2,1,0:T(8,128)}, /*index=5*/f32[32,80,128]{2,1,0:T(8,128)}) custom-call(s32[1]{0:T(128)} %bitcast.spot.refs_0_, f32[32,128,512]{2,1,0:T(8,128)} %refs_1_.15, f32[32,128,512]{2,1,0:T(8,128)} %refs_1_.15, ...), custom_call_target="tpu_custom_call" | custom-call | flops 1024 | bytes 1024 | tf_op jit(solution)/shard_map/pallas_call | solution.py:284
  7.6 2.6 %collective-permute-start.4 = (f32[176,32,128]{2,1,0:T(8,128)}, f32[176,32,128]{2,1,0:T(8,128)}, u32[]{:S(2)}, u32[]{:S(2)}) collective-permute-start(f32[176,32,128]{2,1,0:T(8,128)} %get-tuple-element.47.middle), channel_id=1, source_target_pairs={{1,0},{2,1},{3,2},{4,3},{5,4},{6,5},{7,6},{8,7},{9,8},{10,9},{11,1... | collective-permute-start | bytes 8650760 | tf_op jit(solution)/shard_map/ppermute | solution.py:645
  10.2 5.1 %collective-permute-start.3 = (f32[176,16,128]{2,1,0:T(8,128)}, f32[176,16,128]{2,1,0:T(8,128)S(1)}, u32[]{:S(2)}, u32[]{:S(2)}) collective-permute-start(f32[176,16,128]{2,1,0:T(8,128)} %get-tuple-element.46), channel_id=1, source_target_pairs={{0,1},{1,2},{2,3},{3,4},{4,5},{5,6},{6,7},{7,8},{8,9},{9,10},{10,1... | collective-permute-start | bytes 4325384 | tf_op jit(solution)/shard_map/ppermute | solution.py:645
  16.3 2.3 %collective-permute-start.1 = (f32[3,34]{1,0:T(4,128)S(1)}, f32[3,34]{1,0:T(4,128)S(1)}, u32[]{:S(2)}, u32[]{:S(2)}) collective-permute-start(f32[3,34]{1,0:T(4,128)S(1)} %shard_map.47), channel_id=1, source_target_pairs={{0,64},{32,96},{64,0},{96,32},{1,65},{33,97},{65,1},{97,33},{2,66}... | collective-permute-start | bytes 1232 | tf_op jit(solution)/shard_map/ppermute | solution.py:649
  18.6 1.5 collective-permute-start
  20.2 2.7 %collective-permute-start.7 = (f32[32,80,128]{2,1,0:T(8,128)}, f32[32,80,128]{2,1,0:T(8,128)S(1)}, u32[]{:S(2)}, u32[]{:S(2)}) collective-permute-start(f32[32,80,128]{2,1,0:T(8,128)} %get-tuple-element.51), channel_id=1, source_target_pairs={{0,96},{32,0},{64,32},{96,64},{1,97},{33,1},{65,33},{97,65},{2,98}... | collective-permute-start | bytes 3932168 | tf_op jit(solution)/shard_map/ppermute | solution.py:649
  23.1 6.9 %shard_map.48 = (bf16[128,256]{1,0:T(8,128)(2,1)S(1)}, bf16[4,128,512]{2,1,0:T(8,128)(2,1)S(1)}, bf16[4,128,384]{2,1,0:T(8,128)(2,1)S(1)}, bf16[2,4,128,256]{3,2...) custom-call(f32[4,3,34]{2,1,0:T(4,128)S(1)} %pad_maximum_fusion.params), custom_call_target="tpu_custom_call" | custom-call | flops 1024 | bytes 1024 | tf_op jit(solution)/shard_map/pallas_call | solution.py:187
  30.4 1.2 collective-permute-done.3.lower
  31.6 14.3 %collective-permute-done.4.upper = f32[176,32,128]{2,1,0:T(8,128)} collective-permute-done((f32[176,32,128]{2,1,0:T(8,128)}, f32[176,32,128]{2,1,0:T(8,128)}, u32[]{:S(2)}, u32[]{:S(2)}) %collective-permute-start.4) | collective-permute-done | bytes 2883616 | tf_op jit(solution)/shard_map/ppermute | solution.py:645
  45.8 15.1 %shard_map.49 = (f32[128,128,128]{2,1,0:T(8,128)}, f32[32,48,128]{2,1,0:T(8,128)S(1)}, f32[32,48,128]{2,1,0:T(8,128)S(1)}, f32[32,48,128]{2,1,0:T(8,128)S(1)}) custom-call(s32[5]{0:T(128)S(1)} %pad_add_fusion.starts, bf16[128,256]{1,0:T(8,128)(2,1)S(1)} %get-tuple-element.43.ax, bf16[4,128,512]{2,1,0:T(8,128)(2,1)S(1)} %get-tuple-element.44.az, ...), custom_call_target="tpu_custom_call" | custom-call | flops 1024 | bytes 1024 | tf_op jit(solution)/shard_map/pallas_call | solution.py:378
  61.0 1.3 collective-permute-start.6
  62.5 1.8 collective-permute-start.10
  64.3 16.2 %collective-permute-done.9.refs_8_.refs_10_ = f32[32,80,128]{2,1,0:T(8,128)S(1)} collective-permute-done((f32[32,80,128]{2,1,0:T(8,128)}, f32[32,80,128]{2,1,0:T(8,128)S(1)}, u32[]{:S(2)}, u32[]{:S(2)}) %collective-permute-start.9) | collective-permute-done | bytes 1310752 | tf_op jit(solution)/shard_map/ppermute | solution.py:649
  81.5 8.1 %shard_map.50 = (f32[96,16,128]{2,1,0:T(8,128)S(1)}, f32[64,32,128]{2,1,0:T(8,128)S(1)}, f32[64,32,128]{2,1,0:T(8,128)S(1)}, f32[32,32,128]{2,1,0:T(8,128)S(1)}, f32[32,32,128]{2,1,0:T(8,128)S(1)}) custom-call(s32[1]{0:T(128)} %bitcast.spot.refs_0_, bf16[160,256]{1,0:T(8,128)(2,1)S(1)} %get-tuple-element.40.refs_1_, ...), custom_call_target="tpu_custom_call" | custom-call | flops 1024 | bytes 1024 | tf_op jit(solution)/shard_map/pallas_call | solution.py:522
  89.6 4.6 %collective-permute-start.13 = (f32[32,32,128]{2,1,0:T(8,128)S(1)}, f32[32,32,128]{2,1,0:T(8,128)S(1)}, u32[]{:S(2)}, u32[]{:S(2)}) collective-permute-start(f32[32,32,128]{2,1,0:T(8,128)S(1)} %get-tuple-element.59), channel_id=1, source_target_pairs={{0,1},{1,2},{2,3},{3,4},{4,5},{5,6},{6,7},{7,8},{8,9},{9,10},{10,1... | collective-permute-start | bytes 1572872 | tf_op jit(solution)/shard_map/ppermute | solution.py:645
  94.2 1.9 collective-permute-start.12
  96.1 5.8 %collective-permute-start.11 = (f32[64,32,128]{2,1,0:T(8,128)S(1)}, f32[64,32,128]{2,1,0:T(8,128)S(1)}, u32[]{:S(2)}, u32[]{:S(2)}) collective-permute-start(f32[64,32,128]{2,1,0:T(8,128)S(1)} %get-tuple-element.56), channel_id=1, source_target_pairs={{0,1},{1,2},{2,3},{3,4},{4,5},{5,6},{6,7},{7,8},{8,9},{9,10},{10,1... | collective-permute-start | bytes 3145736 | tf_op jit(solution)/shard_map/ppermute | solution.py:645
  101.9 7.7 %collective-permute-done.12.down = f32[96,16,128]{2,1,0:T(8,128)S(1)} collective-permute-done((f32[96,16,128]{2,1,0:T(8,128)S(1)}, f32[96,16,128]{2,1,0:T(8,128)S(1)}, u32[]{:S(2)}, u32[]{:S(2)}) %collective-permute-start.12) | collective-permute-done | bytes 786464 | tf_op jit(solution)/shard_map/ppermute | solution.py:645
  109.8 1.9 collective-permute-start.14
  111.8 3.4 %collective-permute-start.15 = (f32[32,16,128]{2,1,0:T(8,128)S(1)}, f32[32,16,128]{2,1,0:T(8,128)S(1)}, u32[]{:S(2)}, u32[]{:S(2)}) collective-permute-start(f32[32,16,128]{2,1,0:T(8,128)S(1)} %get-tuple-element.61), channel_id=1, source_target_pairs={{32,0},{64,32},{96,64},{33,1},{65,33},{97,65},{34,2},{66,34},{98,6... | collective-permute-start | bytes 786440 | tf_op jit(solution)/shard_map/ppermute | solution.py:654
  115.3 1.6 collective-permute-done.14.rights
  116.9 3.8 %collective-permute-done.15.lefts = f32[32,16,128]{2,1,0:T(8,128)S(1)} collective-permute-done((f32[32,16,128]{2,1,0:T(8,128)S(1)}, f32[32,16,128]{2,1,0:T(8,128)S(1)}, u32[]{:S(2)}, u32[]{:S(2)}) %collective-permute-start.15) | collective-permute-done | bytes 262176 | tf_op jit(solution)/shard_map/ppermute | solution.py:654
  121.9 1.8 collective-permute-start.19
  125.2 9.2 %shard_map.55 = (f32[96,16,128]{2,1,0:T(8,128)S(1)}, f32[64,32,128]{2,1,0:T(8,128)}, f32[64,32,128]{2,1,0:T(8,128)}, f32[32,32,128]{2,1,0:T(8,128)S(1)}, f32[32,32,128]{2,1,0:T(8,128)S(1)}) custom-call(s32[1]{0:T(128)} %bitcast.spot.refs_0_, bf16[160,256]{1,0:T(8,128)(2,1)S(1)} %get-tuple-element.40.refs_1_, ...), custom_call_target="tpu_custom_call" | custom-call | flops 1024 | bytes 1024 | tf_op jit(solution)/shard_map/pallas_call | solution.py:522
  134.4 3.7 %collective-permute-start.18 = (f32[32,32,128]{2,1,0:T(8,128)S(1)}, f32[32,32,128]{2,1,0:T(8,128)S(1)}, u32[]{:S(2)}, u32[]{:S(2)}) collective-permute-start(f32[32,32,128]{2,1,0:T(8,128)S(1)} %get-tuple-element.68), channel_id=1, source_target_pairs={{0,1},{1,2},{2,3},{3,4},{4,5},{5,6},{6,7},{7,8},{8,9},{9,10},{10,1... | collective-permute-start | bytes 1572872 | tf_op jit(solution)/shard_map/ppermute | solution.py:645
  138.1 1.9 collective-permute-start.17
  140.0 5.8 %collective-permute-start.16 = (f32[64,32,128]{2,1,0:T(8,128)}, f32[64,32,128]{2,1,0:T(8,128)S(1)}, u32[]{:S(2)}, u32[]{:S(2)}) collective-permute-start(f32[64,32,128]{2,1,0:T(8,128)} %get-tuple-element.65), channel_id=1, source_target_pairs={{0,1},{1,2},{2,3},{3,4},{4,5},{5,6},{6,7},{7,8},{8,9},{9,10},{10,1... | collective-permute-start | bytes 3145736 | tf_op jit(solution)/shard_map/ppermute | solution.py:645
  145.8 1.6 collective-permute-start.23
  147.4 6.1 %collective-permute-done.17.down = f32[96,16,128]{2,1,0:T(8,128)S(1)} collective-permute-done((f32[96,16,128]{2,1,0:T(8,128)S(1)}, f32[96,16,128]{2,1,0:T(8,128)S(1)}, u32[]{:S(2)}, u32[]{:S(2)}) %collective-permute-start.17) | collective-permute-done | bytes 786464 | tf_op jit(solution)/shard_map/ppermute | solution.py:645
  153.5 1.2 collective-permute-start.24
  154.9 2.4 %collective-permute-start.21 = (f32[32,16,128]{2,1,0:T(8,128)S(1)}, f32[32,16,128]{2,1,0:T(8,128)S(1)}, u32[]{:S(2)}, u32[]{:S(2)}) collective-permute-start(f32[32,16,128]{2,1,0:T(8,128)S(1)} %get-tuple-element.69), channel_id=1, source_target_pairs={{0,32},{32,64},{64,96},{1,33},{33,65},{65,97},{2,34},{34,66},{66,9... | collective-permute-start | bytes 786440 | tf_op jit(solution)/shard_map/ppermute | solution.py:654
  157.8 3.1 %collective-permute-start.22 = (f32[32,16,128]{2,1,0:T(8,128)S(1)}, f32[32,16,128]{2,1,0:T(8,128)S(1)}, u32[]{:S(2)}, u32[]{:S(2)}) collective-permute-start(f32[32,16,128]{2,1,0:T(8,128)S(1)} %get-tuple-element.70), channel_id=1, source_target_pairs={{32,0},{64,32},{96,64},{33,1},{65,33},{97,65},{34,2},{66,34},{98,6... | collective-permute-start | bytes 786440 | tf_op jit(solution)/shard_map/ppermute | solution.py:654
  161.1 4.0 %collective-permute-done.24.refs_1_.refs_3_ = f32[32,32,128]{2,1,0:T(8,128)S(1)} collective-permute-done((f32[32,32,128]{2,1,0:T(8,128)S(1)}, f32[32,32,128]{2,1,0:T(8,128)S(1)}, u32[]{:S(2)}, u32[]{:S(2)}) %collective-permute-start.24) | collective-permute-done | bytes 524320 | tf_op jit(solution)/shard_map/ppermute | solution.py:649
  165.1 2.9 %collective-permute-done.22.lefts = f32[32,16,128]{2,1,0:T(8,128)S(1)} collective-permute-done((f32[32,16,128]{2,1,0:T(8,128)S(1)}, f32[32,16,128]{2,1,0:T(8,128)S(1)}, u32[]{:S(2)}, u32[]{:S(2)}) %collective-permute-start.22) | collective-permute-done | bytes 262176 | tf_op jit(solution)/shard_map/ppermute | solution.py:654
  169.1 1.5 collective-permute-start.27
  170.6 1.4 collective-permute-start.32
  172.5 10.6 %collective-permute-done.27.refs_4_.refs_2_ = f32[32,32,128]{2,1,0:T(8,128)S(1)} collective-permute-done((f32[32,32,128]{2,1,0:T(8,128)S(1)}, f32[32,32,128]{2,1,0:T(8,128)S(1)}, u32[]{:S(2)}, u32[]{:S(2)}) %collective-permute-start.27) | collective-permute-done | bytes 524320 | tf_op jit(solution)/shard_map/ppermute | solution.py:649
  183.1 1.4 collective-permute-start.28
  185.0 2.1 %shard_map.60.refs_4_ = f32[32,128,512]{2,1,0:T(8,128)} custom-call(s32[1]{0:T(128)} %bitcast.spot.refs_0_, f32[32,128,512]{2,1,0:T(8,128)} %refs_1_.15, f32[32,32,128]{2,1,0:T(8,128)S(1)} %get-tuple-element.62.refs_12_.refs_2_, f32[32,32,128]{2,1,0:T(8,128)S(1)} %get-tuple-element.63.refs_13_.refs_3_, ...), custom_call_target="tpu_custom_call" | custom-call | flops 1024 | bytes 1024 | tf_op jit(solution)/shard_map/pallas_call | solution.py:629
  187.1 2.1 %shard_map.61.refs_4_ = f32[32,128,512]{2,1,0:T(8,128)} custom-call(s32[1]{0:T(128)} %bitcast.spot.refs_0_, f32[32,128,512]{2,1,0:T(8,128)} %refs_1_.15, f32[32,32,128]{2,1,0:T(8,128)S(1)} %collective-permute-done.19.refs_0_.refs_2_, f32[32,32,128]{2,1,0:T(8,128)S(1)} %collective-permute-done.25.refs_2_.refs_3_, ...), custom_call_target="tpu_custom_call", output_to_operand_aliasing={{}: (4, {})} | custom-call | flops 1024 | bytes 1024 | tf_op jit(solution)/shard_map/pallas_call | solution.py:629
  189.2 2.1 %shard_map.62.refs_4_ = f32[32,128,512]{2,1,0:T(8,128)} custom-call(s32[1]{0:T(128)} %bitcast.spot.refs_0_, f32[32,128,512]{2,1,0:T(8,128)} %refs_1_.15, f32[32,32,128]{2,1,0:T(8,128)S(1)} %collective-permute-done.26.refs_3_.refs_2_, f32[32,32,128]{2,1,0:T(8,128)S(1)} %collective-permute-done.20.refs_1_.refs_3_, ...), custom_call_target="tpu_custom_call", output_to_operand_aliasing={{}: (4, {})} | custom-call | flops 1024 | bytes 1024 | tf_op jit(solution)/shard_map/pallas_call | solution.py:629
  191.3 2.1 %shard_map.63.refs_4_ = f32[32,128,512]{2,1,0:T(8,128)} custom-call(s32[1]{0:T(128)} %bitcast.spot.refs_0_, f32[32,128,512]{2,1,0:T(8,128)} %refs_1_.15, f32[32,32,128]{2,1,0:T(8,128)S(1)} %collective-permute-done.23.refs_0_.refs_2_, f32[32,32,128]{2,1,0:T(8,128)S(1)} %collective-permute-done.24.refs_1_.refs_3_, ...), custom_call_target="tpu_custom_call", output_to_operand_aliasing={{}: (4, {})} | custom-call | flops 1024 | bytes 1024 | tf_op jit(solution)/shard_map/pallas_call | solution.py:629
  193.4 2.1 %shard_map.64.refs_4_ = f32[32,128,512]{2,1,0:T(8,128)} custom-call(s32[1]{0:T(128)} %bitcast.spot.refs_0_, f32[32,128,512]{2,1,0:T(8,128)} %refs_1_.15, f32[32,32,128]{2,1,0:T(8,128)S(1)} %get-tuple-element.71.refs_2_, f32[32,32,128]{2,1,0:T(8,128)S(1)} %get-tuple-element.72.refs_3_, f32[32,128,512]{2,1,0:T(8,128)} %shard_map.63.refs_4_), custom_call_target="tpu_custom_call", output_to_operand_aliasing={{}: (4, {})} | custom-call | flops 1024 | bytes 1024 | tf_op jit(solution)/shard_map/pallas_call | solution.py:629
  195.4 2.1 %shard_map.65.refs_4_ = f32[32,128,512]{2,1,0:T(8,128)} custom-call(s32[1]{0:T(128)} %bitcast.spot.refs_0_, f32[32,128,512]{2,1,0:T(8,128)} %refs_1_.15, f32[32,32,128]{2,1,0:T(8,128)S(1)} %collective-permute-done.27.refs_4_.refs_2_, f32[32,32,128]{2,1,0:T(8,128)S(1)} %collective-permute-done.32.refs_3_, ...), custom_call_target="tpu_custom_call", output_to_operand_aliasing={{}: (4, {})} | custom-call | flops 1024 | bytes 1024 | tf_op jit(solution)/shard_map/pallas_call | solution.py:629
  197.5 2.1 %shard_map.66.refs_4_ = f32[32,128,512]{2,1,0:T(8,128)} custom-call(s32[1]{0:T(128)} %bitcast.spot.refs_0_, f32[32,128,512]{2,1,0:T(8,128)} %refs_1_.15, f32[32,32,128]{2,1,0:T(8,128)S(1)} %collective-permute-done.31.refs_2_, f32[32,32,128]{2,1,0:T(8,128)S(1)} %collective-permute-done.29.refs_5_.refs_3_, ...), custom_call_target="tpu_custom_call", output_to_operand_aliasing={{}: (4, {})} | custom-call | flops 1024 | bytes 1024 | tf_op jit(solution)/shard_map/pallas_call | solution.py:629
  199.6 4.7 %collective-permute-done.28.refs_2_ = f32[32,32,128]{2,1,0:T(8,128)S(1)} collective-permute-done((f32[32,32,128]{2,1,0:T(8,128)S(1)}, f32[32,32,128]{2,1,0:T(8,128)S(1)}, u32[]{:S(2)}, u32[]{:S(2)}) %collective-permute-start.28) | collective-permute-done | bytes 524320 | tf_op jit(solution)/shard_map/ppermute | solution.py:649
  204.3 1.4 collective-permute-done.30.refs_3_
  205.7 2.1 %shard_map.67 = f32[32,128,512]{2,1,0:T(8,128)} custom-call(s32[1]{0:T(128)} %bitcast.spot.refs_0_, f32[32,128,512]{2,1,0:T(8,128)} %refs_1_.15, f32[32,32,128]{2,1,0:T(8,128)S(1)} %collective-permute-done.28.refs_2_, f32[32,32,128]{2,1,0:T(8,128)S(1)} %collective-permute-done.30.refs_3_, ...), custom_call_target="tpu_custom_call", output_to_operand_aliasing={{}: (4, {})} | custom-call | flops 1024 | bytes 1024 | tf_op jit(solution)/shard_map/pallas_call | solution.py:629
  (62 shorter events, 8.7 us)
Async XLA Ops:
  0.0 15.3 %copy-start.7 = (s32[1,3]{1,0:T(1,128)S(1)}, s32[1,3]{1,0:T(1,128)}, u32[]{:S(2)}) copy-start(s32[1,3]{1,0:T(1,128)} %param.7) | copy-start | bytes 40
  0.0 15.4 %copy-start.6 = (f32[1,3,33]{2,0,1:T(1,128)S(1)}, f32[1,3,33]{2,0,1:T(1,128)}, u32[]{:S(2)}) copy-start(f32[1,3,33]{2,0,1:T(1,128)} %param.6) | copy-start | bytes 1192
  7.6 38.2 %collective-permute-start.4 = (f32[176,32,128]{2,1,0:T(8,128)}, f32[176,32,128]{2,1,0:T(8,128)}, u32[]{:S(2)}, u32[]{:S(2)}) collective-permute-start(f32[176,32,128]{2,1,0:T(8,128)} %get-tuple-element.47.middle), channel_id=1, source_target_pairs={{1,0},{2,1},{3,2},{4,3},{5,4},{6,5},{7,6},{8,7},{9,8},{10,9},{11,1... | collective-permute-start | bytes 8650760 | tf_op jit(solution)/shard_map/ppermute | solution.py:645
  10.2 21.3 %collective-permute-start.3 = (f32[176,16,128]{2,1,0:T(8,128)}, f32[176,16,128]{2,1,0:T(8,128)S(1)}, u32[]{:S(2)}, u32[]{:S(2)}) collective-permute-start(f32[176,16,128]{2,1,0:T(8,128)} %get-tuple-element.46), channel_id=1, source_target_pairs={{0,1},{1,2},{2,3},{3,4},{4,5},{5,6},{6,7},{7,8},{8,9},{9,10},{10,1... | collective-permute-start | bytes 4325384 | tf_op jit(solution)/shard_map/ppermute | solution.py:645
  15.4 0.7 copy-start.2
  16.2 3.9 %collective-permute-start.2 = (f32[3,34]{1,0:T(4,128)S(1)}, f32[3,34]{1,0:T(4,128)S(1)}, u32[]{:S(2)}, u32[]{:S(2)}) collective-permute-start(f32[3,34]{1,0:T(4,128)S(1)} %shard_map.47), channel_id=1, source_target_pairs={{0,96},{32,0},{64,32},{96,64},{1,97},{33,1},{65,33},{97,65},{2,98}... | collective-permute-start | bytes 1232 | tf_op jit(solution)/shard_map/ppermute | solution.py:649
  16.3 3.9 %collective-permute-start.1 = (f32[3,34]{1,0:T(4,128)S(1)}, f32[3,34]{1,0:T(4,128)S(1)}, u32[]{:S(2)}, u32[]{:S(2)}) collective-permute-start(f32[3,34]{1,0:T(4,128)S(1)} %shard_map.47), channel_id=1, source_target_pairs={{0,64},{32,96},{64,0},{96,32},{1,65},{33,97},{65,1},{97,33},{2,66}... | collective-permute-start | bytes 1232 | tf_op jit(solution)/shard_map/ppermute | solution.py:649
  18.6 4.4 %collective-permute-start = (f32[3,34]{1,0:T(4,128)S(1)}, f32[3,34]{1,0:T(4,128)S(1)}, u32[]{:S(2)}, u32[]{:S(2)}) collective-permute-start(f32[3,34]{1,0:T(4,128)S(1)} %shard_map.47), channel_id=1, source_target_pairs={{0,32},{32,64},{64,96},{96,0},{1,33},{33,65},{65,97},{97,1},{2,34}... | collective-permute-start | bytes 1232 | tf_op jit(solution)/shard_map/ppermute | solution.py:649
  20.1 42.4 %collective-permute-start.5 = (f32[32,80,128]{2,1,0:T(8,128)}, f32[32,80,128]{2,1,0:T(8,128)S(1)}, u32[]{:S(2)}, u32[]{:S(2)}) collective-permute-start(f32[32,80,128]{2,1,0:T(8,128)} %get-tuple-element.49), channel_id=1, source_target_pairs={{0,32},{32,64},{64,96},{96,0},{1,33},{33,65},{65,97},{97,1},{2,34}... | collective-permute-start | bytes 3932168 | tf_op jit(solution)/shard_map/ppermute | solution.py:649
  20.2 44.1 %collective-permute-start.7 = (f32[32,80,128]{2,1,0:T(8,128)}, f32[32,80,128]{2,1,0:T(8,128)S(1)}, u32[]{:S(2)}, u32[]{:S(2)}) collective-permute-start(f32[32,80,128]{2,1,0:T(8,128)} %get-tuple-element.51), channel_id=1, source_target_pairs={{0,96},{32,0},{64,32},{96,64},{1,97},{33,1},{65,33},{97,65},{2,98}... | collective-permute-start | bytes 3932168 | tf_op jit(solution)/shard_map/ppermute | solution.py:649
  23.0 57.5 %collective-permute-start.9 = (f32[32,80,128]{2,1,0:T(8,128)}, f32[32,80,128]{2,1,0:T(8,128)S(1)}, u32[]{:S(2)}, u32[]{:S(2)}) collective-permute-start(f32[32,80,128]{2,1,0:T(8,128)} %get-tuple-element.53), channel_id=1, source_target_pairs={{0,64},{32,96},{64,0},{96,32},{1,65},{33,97},{65,1},{97,33},{2,66}... | collective-permute-start | bytes 3932168 | tf_op jit(solution)/shard_map/ppermute | solution.py:649
  61.0 35.2 %collective-permute-start.6 = (f32[32,48,128]{2,1,0:T(8,128)S(1)}, f32[32,48,128]{2,1,0:T(8,128)S(1)}, u32[]{:S(2)}, u32[]{:S(2)}) collective-permute-start(f32[32,48,128]{2,1,0:T(8,128)S(1)} %get-tuple-element.50), channel_id=1, source_target_pairs={{0,32},{32,64},{64,96},{96,0},{1,33},{33,65},{65,97},{97,1},{2,34}... | collective-permute-start | bytes 2359304 | tf_op jit(solution)/shard_map/ppermute | solution.py:649
  62.2 39.7 %collective-permute-start.8 = (f32[32,48,128]{2,1,0:T(8,128)S(1)}, f32[32,48,128]{2,1,0:T(8,128)S(1)}, u32[]{:S(2)}, u32[]{:S(2)}) collective-permute-start(f32[32,48,128]{2,1,0:T(8,128)S(1)} %get-tuple-element.52), channel_id=1, source_target_pairs={{0,96},{32,0},{64,32},{96,64},{1,97},{33,1},{65,33},{97,65},{2,98}... | collective-permute-start | bytes 2359304 | tf_op jit(solution)/shard_map/ppermute | solution.py:649
  62.5 19.0 %copy-start.3 = (f32[32,80,128]{2,1,0:T(8,128)}, f32[32,80,128]{2,1,0:T(8,128)S(1)}, u32[]{:S(2)}) copy-start(f32[32,80,128]{2,1,0:T(8,128)S(1)} %collective-permute-done.5.refs_6_) | copy-start | bytes 3932164
  62.5 52.6 %collective-permute-start.10 = (f32[32,48,128]{2,1,0:T(8,128)S(1)}, f32[32,48,128]{2,1,0:T(8,128)S(1)}, u32[]{:S(2)}, u32[]{:S(2)}) collective-permute-start(f32[32,48,128]{2,1,0:T(8,128)S(1)} %get-tuple-element.54), channel_id=1, source_target_pairs={{0,64},{32,96},{64,0},{96,32},{1,65},{33,97},{65,1},{97,33},{2,66}... | collective-permute-start | bytes 2359304 | tf_op jit(solution)/shard_map/ppermute | solution.py:649
  64.3 17.2 %copy-start.4 = (f32[32,80,128]{2,1,0:T(8,128)}, f32[32,80,128]{2,1,0:T(8,128)S(1)}, u32[]{:S(2)}) copy-start(f32[32,80,128]{2,1,0:T(8,128)S(1)} %collective-permute-done.7.refs_7_.refs_8_) | copy-start | bytes 3932164
  80.5 1.1 copy-start.5
  89.6 12.3 %collective-permute-start.13 = (f32[32,32,128]{2,1,0:T(8,128)S(1)}, f32[32,32,128]{2,1,0:T(8,128)S(1)}, u32[]{:S(2)}, u32[]{:S(2)}) collective-permute-start(f32[32,32,128]{2,1,0:T(8,128)S(1)} %get-tuple-element.59), channel_id=1, source_target_pairs={{0,1},{1,2},{2,3},{3,4},{4,5},{5,6},{6,7},{7,8},{8,9},{9,10},{10,1... | collective-permute-start | bytes 1572872 | tf_op jit(solution)/shard_map/ppermute | solution.py:645
  94.2 15.4 %collective-permute-start.12 = (f32[96,16,128]{2,1,0:T(8,128)S(1)}, f32[96,16,128]{2,1,0:T(8,128)S(1)}, u32[]{:S(2)}, u32[]{:S(2)}) collective-permute-start(f32[96,16,128]{2,1,0:T(8,128)S(1)} %get-tuple-element.57), channel_id=1, source_target_pairs={{1,0},{2,1},{3,2},{4,3},{5,4},{6,5},{7,6},{8,7},{9,8},{10,9},{11,1... | collective-permute-start | bytes 2359304 | tf_op jit(solution)/shard_map/ppermute | solution.py:645
  96.1 19.0 %collective-permute-start.11 = (f32[64,32,128]{2,1,0:T(8,128)S(1)}, f32[64,32,128]{2,1,0:T(8,128)S(1)}, u32[]{:S(2)}, u32[]{:S(2)}) collective-permute-start(f32[64,32,128]{2,1,0:T(8,128)S(1)} %get-tuple-element.56), channel_id=1, source_target_pairs={{0,1},{1,2},{2,3},{3,4},{4,5},{5,6},{6,7},{7,8},{8,9},{9,10},{10,1... | collective-permute-start | bytes 3145736 | tf_op jit(solution)/shard_map/ppermute | solution.py:645
  109.8 7.1 %collective-permute-start.14 = (f32[32,16,128]{2,1,0:T(8,128)S(1)}, f32[32,16,128]{2,1,0:T(8,128)S(1)}, u32[]{:S(2)}, u32[]{:S(2)}) collective-permute-start(f32[32,16,128]{2,1,0:T(8,128)S(1)} %get-tuple-element.60), channel_id=1, source_target_pairs={{0,32},{32,64},{64,96},{1,33},{33,65},{65,97},{2,34},{34,66},{66,9... | collective-permute-start | bytes 786440 | tf_op jit(solution)/shard_map/ppermute | solution.py:654
  111.8 9.0 %collective-permute-start.15 = (f32[32,16,128]{2,1,0:T(8,128)S(1)}, f32[32,16,128]{2,1,0:T(8,128)S(1)}, u32[]{:S(2)}, u32[]{:S(2)}) collective-permute-start(f32[32,16,128]{2,1,0:T(8,128)S(1)} %get-tuple-element.61), channel_id=1, source_target_pairs={{32,0},{64,32},{96,64},{33,1},{65,33},{97,65},{34,2},{66,34},{98,6... | collective-permute-start | bytes 786440 | tf_op jit(solution)/shard_map/ppermute | solution.py:654
  115.2 10.0 %copy-start = (f32[32,48,128]{2,1,0:T(8,128)}, f32[32,48,128]{2,1,0:T(8,128)S(1)}, u32[]{:S(2)}) copy-start(f32[32,48,128]{2,1,0:T(8,128)S(1)} %collective-permute-done.10.refs_0_.refs_11_) | copy-start | bytes 2359300
  121.9 16.2 %collective-permute-start.19 = (f32[32,32,128]{2,1,0:T(8,128)S(1)}, f32[32,32,128]{2,1,0:T(8,128)S(1)}, u32[]{:S(2)}, u32[]{:S(2)}) collective-permute-start(f32[32,32,128]{2,1,0:T(8,128)S(1)} %get-tuple-element.62.refs_12_.refs_2_), channel_id=1, source_target_pairs={{0,32},{32,64},{64,96},{96,0},{1,33},{33,65},{65,97},{97,1},{2,34}... | collective-permute-start | bytes 1572872 | tf_op jit(solution)/shard_map/ppermute | solution.py:649
  123.7 16.3 %collective-permute-start.20 = (f32[32,32,128]{2,1,0:T(8,128)S(1)}, f32[32,32,128]{2,1,0:T(8,128)S(1)}, u32[]{:S(2)}, u32[]{:S(2)}) collective-permute-start(f32[32,32,128]{2,1,0:T(8,128)S(1)} %get-tuple-element.63.refs_13_.refs_3_), channel_id=1, source_target_pairs={{0,96},{32,0},{64,32},{96,64},{1,97},{33,1},{65,33},{97,65},{2,98}... | collective-permute-start | bytes 1572872 | tf_op jit(solution)/shard_map/ppermute | solution.py:649
  123.7 31.2 %collective-permute-start.26 = (f32[32,32,128]{2,1,0:T(8,128)S(1)}, f32[32,32,128]{2,1,0:T(8,128)S(1)}, u32[]{:S(2)}, u32[]{:S(2)}) collective-permute-start(f32[32,32,128]{2,1,0:T(8,128)S(1)} %get-tuple-element.62.refs_12_.refs_2_), channel_id=1, source_target_pairs={{0,96},{32,0},{64,32},{96,64},{1,97},{33,1},{65,33},{97,65},{2,98}... | collective-permute-start | bytes 1572872 | tf_op jit(solution)/shard_map/ppermute | solution.py:649
  124.2 36.9 %collective-permute-start.25 = (f32[32,32,128]{2,1,0:T(8,128)S(1)}, f32[32,32,128]{2,1,0:T(8,128)S(1)}, u32[]{:S(2)}, u32[]{:S(2)}) collective-permute-start(f32[32,32,128]{2,1,0:T(8,128)S(1)} %get-tuple-element.63.refs_13_.refs_3_), channel_id=1, source_target_pairs={{0,32},{32,64},{64,96},{96,0},{1,33},{33,65},{65,97},{97,1},{2,34}... | collective-permute-start | bytes 1572872 | tf_op jit(solution)/shard_map/ppermute | solution.py:649
  134.4 11.4 %collective-permute-start.18 = (f32[32,32,128]{2,1,0:T(8,128)S(1)}, f32[32,32,128]{2,1,0:T(8,128)S(1)}, u32[]{:S(2)}, u32[]{:S(2)}) collective-permute-start(f32[32,32,128]{2,1,0:T(8,128)S(1)} %get-tuple-element.68), channel_id=1, source_target_pairs={{0,1},{1,2},{2,3},{3,4},{4,5},{5,6},{6,7},{7,8},{8,9},{9,10},{10,1... | collective-permute-start | bytes 1572872 | tf_op jit(solution)/shard_map/ppermute | solution.py:645
  138.1 15.4 %collective-permute-start.17 = (f32[96,16,128]{2,1,0:T(8,128)S(1)}, f32[96,16,128]{2,1,0:T(8,128)S(1)}, u32[]{:S(2)}, u32[]{:S(2)}) collective-permute-start(f32[96,16,128]{2,1,0:T(8,128)S(1)} %get-tuple-element.66), channel_id=1, source_target_pairs={{1,0},{2,1},{3,2},{4,3},{5,4},{6,5},{7,6},{8,7},{9,8},{10,9},{11,1... | collective-permute-start | bytes 2359304 | tf_op jit(solution)/shard_map/ppermute | solution.py:645
  140.0 17.8 %collective-permute-start.16 = (f32[64,32,128]{2,1,0:T(8,128)}, f32[64,32,128]{2,1,0:T(8,128)S(1)}, u32[]{:S(2)}, u32[]{:S(2)}) collective-permute-start(f32[64,32,128]{2,1,0:T(8,128)} %get-tuple-element.65), channel_id=1, source_target_pairs={{0,1},{1,2},{2,3},{3,4},{4,5},{5,6},{6,7},{7,8},{8,9},{9,10},{10,1... | collective-permute-start | bytes 3145736 | tf_op jit(solution)/shard_map/ppermute | solution.py:645
  145.8 15.2 %collective-permute-start.23 = (f32[32,32,128]{2,1,0:T(8,128)S(1)}, f32[32,32,128]{2,1,0:T(8,128)S(1)}, u32[]{:S(2)}, u32[]{:S(2)}) collective-permute-start(f32[32,32,128]{2,1,0:T(8,128)S(1)} %collective-permute-done.19.refs_0_.refs_2_), channel_id=1, source_target_pairs={{0,32},{32,64},{64,96},{96,0},{1,33},{33,65},{65,97},{97,1},{2,34}... | collective-permute-start | bytes 1572872 | tf_op jit(solution)/shard_map/ppermute | solution.py:649
  153.5 11.6 %collective-permute-start.24 = (f32[32,32,128]{2,1,0:T(8,128)S(1)}, f32[32,32,128]{2,1,0:T(8,128)S(1)}, u32[]{:S(2)}, u32[]{:S(2)}) collective-permute-start(f32[32,32,128]{2,1,0:T(8,128)S(1)} %collective-permute-done.20.refs_1_.refs_3_), channel_id=1, source_target_pairs={{0,96},{32,0},{64,32},{96,64},{1,97},{33,1},{65,33},{97,65},{2,98}... | collective-permute-start | bytes 1572872 | tf_op jit(solution)/shard_map/ppermute | solution.py:649
  154.7 6.2 %copy-start.1 = (f32[64,32,128]{2,1,0:T(8,128)S(1)}, f32[64,32,128]{2,1,0:T(8,128)}, u32[]{:S(2)}) copy-start(f32[64,32,128]{2,1,0:T(8,128)} %get-tuple-element.64.own) | copy-start | bytes 3145732
  154.9 10.2 %collective-permute-start.21 = (f32[32,16,128]{2,1,0:T(8,128)S(1)}, f32[32,16,128]{2,1,0:T(8,128)S(1)}, u32[]{:S(2)}, u32[]{:S(2)}) collective-permute-start(f32[32,16,128]{2,1,0:T(8,128)S(1)} %get-tuple-element.69), channel_id=1, source_target_pairs={{0,32},{32,64},{64,96},{1,33},{33,65},{65,97},{2,34},{34,66},{66,9... | collective-permute-start | bytes 786440 | tf_op jit(solution)/shard_map/ppermute | solution.py:654
  157.8 10.2 %collective-permute-start.22 = (f32[32,16,128]{2,1,0:T(8,128)S(1)}, f32[32,16,128]{2,1,0:T(8,128)S(1)}, u32[]{:S(2)}, u32[]{:S(2)}) collective-permute-start(f32[32,16,128]{2,1,0:T(8,128)S(1)} %get-tuple-element.70), channel_id=1, source_target_pairs={{32,0},{64,32},{96,64},{33,1},{65,33},{97,65},{34,2},{66,34},{98,6... | collective-permute-start | bytes 786440 | tf_op jit(solution)/shard_map/ppermute | solution.py:654
  169.1 14.0 %collective-permute-start.27 = (f32[32,32,128]{2,1,0:T(8,128)S(1)}, f32[32,32,128]{2,1,0:T(8,128)S(1)}, u32[]{:S(2)}, u32[]{:S(2)}) collective-permute-start(f32[32,32,128]{2,1,0:T(8,128)S(1)} %get-tuple-element.71.refs_2_), channel_id=1, source_target_pairs={{0,32},{32,64},{64,96},{96,0},{1,33},{33,65},{65,97},{97,1},{2,34}... | collective-permute-start | bytes 1572872 | tf_op jit(solution)/shard_map/ppermute | solution.py:649
  170.6 14.0 %collective-permute-start.29 = (f32[32,32,128]{2,1,0:T(8,128)S(1)}, f32[32,32,128]{2,1,0:T(8,128)S(1)}, u32[]{:S(2)}, u32[]{:S(2)}) collective-permute-start(f32[32,32,128]{2,1,0:T(8,128)S(1)} %get-tuple-element.72.refs_3_), channel_id=1, source_target_pairs={{0,96},{32,0},{64,32},{96,64},{1,97},{33,1},{65,33},{97,65},{2,98}... | collective-permute-start | bytes 1572872 | tf_op jit(solution)/shard_map/ppermute | solution.py:649
  170.6 24.8 %collective-permute-start.32 = (f32[32,32,128]{2,1,0:T(8,128)S(1)}, f32[32,32,128]{2,1,0:T(8,128)S(1)}, u32[]{:S(2)}, u32[]{:S(2)}) collective-permute-start(f32[32,32,128]{2,1,0:T(8,128)S(1)} %get-tuple-element.72.refs_3_), channel_id=1, source_target_pairs={{0,32},{32,64},{64,96},{96,0},{1,33},{33,65},{65,97},{97,1},{2,34}... | collective-permute-start | bytes 1572872 | tf_op jit(solution)/shard_map/ppermute | solution.py:649
  172.1 25.5 %collective-permute-start.31 = (f32[32,32,128]{2,1,0:T(8,128)S(1)}, f32[32,32,128]{2,1,0:T(8,128)S(1)}, u32[]{:S(2)}, u32[]{:S(2)}) collective-permute-start(f32[32,32,128]{2,1,0:T(8,128)S(1)} %get-tuple-element.71.refs_2_), channel_id=1, source_target_pairs={{0,96},{32,0},{64,32},{96,64},{1,97},{33,1},{65,33},{97,65},{2,98}... | collective-permute-start | bytes 1572872 | tf_op jit(solution)/shard_map/ppermute | solution.py:649
  183.1 21.1 %collective-permute-start.28 = (f32[32,32,128]{2,1,0:T(8,128)S(1)}, f32[32,32,128]{2,1,0:T(8,128)S(1)}, u32[]{:S(2)}, u32[]{:S(2)}) collective-permute-start(f32[32,32,128]{2,1,0:T(8,128)S(1)} %collective-permute-done.27.refs_4_.refs_2_), channel_id=1, source_target_pairs={{0,32},{32,64},{64,96},{96,0},{1,33},{33,65},{65,97},{97,1},{2,34}... | collective-permute-start | bytes 1572872 | tf_op jit(solution)/shard_map/ppermute | solution.py:649
  184.6 21.1 %collective-permute-start.30 = (f32[32,32,128]{2,1,0:T(8,128)S(1)}, f32[32,32,128]{2,1,0:T(8,128)S(1)}, u32[]{:S(2)}, u32[]{:S(2)}) collective-permute-start(f32[32,32,128]{2,1,0:T(8,128)S(1)} %collective-permute-done.29.refs_5_.refs_3_), channel_id=1, source_target_pairs={{0,96},{32,0},{64,32},{96,64},{1,97},{33,1},{65,33},{97,65},{2,98}... | collective-permute-start | bytes 1572872 | tf_op jit(solution)/shard_map/ppermute | solution.py:649

commit v5 on v4

--- a/solution.py
+++ b/solution.py
@@ -300,7 +300,7 @@
                 pl.BlockSpec((8, 128), lambda i, s: (0, 0)),
             )
             + (hbm,) * len(OTHERS),
-            scratch_shapes=[pltpu.VMEM((n * ODD + 7, 128), f32)] + cut_scratch(CUT),
+            scratch_shapes=[pltpu.VMEM(((n + 1) * ODD + 7, 128), f32)] + cut_scratch(CUT),
         ),
         compiler_params=pltpu.CompilerParams(vmem_limit_bytes=62 * 1024 * 1024),
         cost_estimate=pl.CostEstimate(flops=FREE, bytes_accessed=FREE, transcendentals=0),
@@ -392,7 +392,7 @@
             ],
             out_specs=(pl.BlockSpec((SLAB, 128, QUARTER), lambda v, s: (v, 0, 0)),)
             + (hbm,) * len(OTHERS),
-            scratch_shapes=[pltpu.VMEM((VIEWS * SLAB * ODD + 8, 128), f32)]
+            scratch_shapes=[pltpu.VMEM(((VIEWS * SLAB + 1) * ODD + 7, 128), f32)]
             + [pltpu.VMEM(x.shape, f32) for x in (lower, middle, upper)]
             + [pltpu.SemaphoreType.DMA((3, WIDE // 16))]
             + cut_scratch(rows),
@@ -527,7 +527,7 @@
         out_specs=(hbm,) * 5,
         scratch_shapes=[pltpu.VMEM((n, SLAB, last - first, QUARTER), f32)]
         + [pltpu.VMEM((n, SLAB, k, QUARTER), f32) for k in rows]
-        + [pltpu.VMEM((n * SLAB * SKEW + 8, 128), f32)]
+        + [pltpu.VMEM(((n * SLAB + 1) * SKEW + 7, 128), f32)]
         + [pltpu.VMEM((CHUNK, k, 128), f32) for k in sizes]
         + [
             pltpu.SemaphoreType.DMA((n, chunk + 2)),

time: 211 us -> 211 us (level)
  no operation moved by 1% of the time
where the time goes in v5:
time: 211 us; the launch traced here: 208 us
  waiting for transfers between devices  75.4 us (36%)
  Pallas kernels  66.4 us (31%)
  starting transfers between devices  63.5 us (30%)
    ppermute x21, waiting for transfers between devices, around_view(): lax.ppermute(x, 'view', [(i, (i + distance) % VIEWS) for i in range(VIEWS)])  37.2 us
    ppermute x8, starting transfers between devices, along_blk(): return lax.ppermute(x, 'blk', route)  31.3 us
    ppermute x8, waiting for transfers between devices, along_blk(): return lax.ppermute(x, 'blk', route)  29.8 us
    ppermute x21, starting transfers between devices, around_view(): lax.ppermute(x, 'view', [(i, (i + distance) % VIEWS) for i in range(VIEWS)])  21.5 us
    pallas_call x2, Pallas kernels, adjoint(): pl.pallas_call(lambda *refs: adjoint_kernel(chunk, len(after), *refs), ou...  17.3 us
    pallas_call x8, Pallas kernels, finish(): call(lambda *refs: finish_kernel(len(pieces), *refs), shape(*estimate.sha...  16.7 us
    pallas_call x1, Pallas kernels, forward_of(): pl.pallas_call(forward_kernel, out_shape=(shape(VIEWS * SLAB, 128, QUARTE...  14.9 us
    ppermute x4, starting transfers between devices, along_view(): return lax.ppermute(x, 'view', route)  10.7 us
  transfers between devices with their start and end apart: 33, of which 14 were waited for; matrix products, arithmetic and copies ran while one was open for 0% of the time, Pallas kernels for 26%

profile of v5, /device:TPU:59, one launch (start us, length us, event | category | flops | bytes accessed | tf_op | source)
XLA Modules:
  0.0 207.8 jit_solution(12411730841859058258)
XLA Ops:
  0.0 7.6 %shard_map.46 = (f32[176,32,128]{2,1,0:T(8,128)}, f32[176,16,128]{2,1,0:T(8,128)}, f32[8,128]{1,0:T(8,128)}, f32[32,80,128]{2,1,0:T(8,128)}, f32[32,80,128]{2,1,0:T(8,128)}, /*index=5*/f32[32,80,128]{2,1,0:T(8,128)}) custom-call(s32[1]{0:T(128)} %bitcast.spot.refs_0_, f32[32,128,512]{2,1,0:T(8,128)} %refs_1_.15, f32[32,128,512]{2,1,0:T(8,128)} %refs_1_.15, ...), custom_call_target="tpu_custom_call" | custom-call | flops 1024 | bytes 1024 | tf_op jit(solution)/shard_map/pallas_call | solution.py:284
  7.6 2.6 %collective-permute-start.4 = (f32[176,32,128]{2,1,0:T(8,128)}, f32[176,32,128]{2,1,0:T(8,128)}, u32[]{:S(2)}, u32[]{:S(2)}) collective-permute-start(f32[176,32,128]{2,1,0:T(8,128)} %get-tuple-element.47.middle), channel_id=1, source_target_pairs={{1,0},{2,1},{3,2},{4,3},{5,4},{6,5},{7,6},{8,7},{9,8},{10,9},{11,1... | collective-permute-start | bytes 8650760 | tf_op jit(solution)/shard_map/ppermute | solution.py:645
  10.2 5.1 %collective-permute-start.3 = (f32[176,16,128]{2,1,0:T(8,128)}, f32[176,16,128]{2,1,0:T(8,128)S(1)}, u32[]{:S(2)}, u32[]{:S(2)}) collective-permute-start(f32[176,16,128]{2,1,0:T(8,128)} %get-tuple-element.46), channel_id=1, source_target_pairs={{0,1},{1,2},{2,3},{3,4},{4,5},{5,6},{6,7},{7,8},{8,9},{9,10},{10,1... | collective-permute-start | bytes 4325384 | tf_op jit(solution)/shard_map/ppermute | solution.py:645
  16.3 2.3 %collective-permute-start.1 = (f32[3,34]{1,0:T(4,128)S(1)}, f32[3,34]{1,0:T(4,128)S(1)}, u32[]{:S(2)}, u32[]{:S(2)}) collective-permute-start(f32[3,34]{1,0:T(4,128)S(1)} %shard_map.47), channel_id=1, source_target_pairs={{0,64},{32,96},{64,0},{96,32},{1,65},{33,97},{65,1},{97,33},{2,66}... | collective-permute-start | bytes 1232 | tf_op jit(solution)/shard_map/ppermute | solution.py:649
  18.6 1.5 collective-permute-start
  20.2 2.7 %collective-permute-start.7 = (f32[32,80,128]{2,1,0:T(8,128)}, f32[32,80,128]{2,1,0:T(8,128)S(1)}, u32[]{:S(2)}, u32[]{:S(2)}) collective-permute-start(f32[32,80,128]{2,1,0:T(8,128)} %get-tuple-element.51), channel_id=1, source_target_pairs={{0,96},{32,0},{64,32},{96,64},{1,97},{33,1},{65,33},{97,65},{2,98}... | collective-permute-start | bytes 3932168 | tf_op jit(solution)/shard_map/ppermute | solution.py:649
  23.1 6.9 %shard_map.48 = (bf16[128,256]{1,0:T(8,128)(2,1)S(1)}, bf16[4,128,512]{2,1,0:T(8,128)(2,1)S(1)}, bf16[4,128,384]{2,1,0:T(8,128)(2,1)S(1)}, bf16[2,4,128,256]{3,2...) custom-call(f32[4,3,34]{2,1,0:T(4,128)S(1)} %pad_maximum_fusion.params), custom_call_target="tpu_custom_call" | custom-call | flops 1024 | bytes 1024 | tf_op jit(solution)/shard_map/pallas_call | solution.py:187
  30.4 1.2 collective-permute-done.3.lower
  31.6 14.3 %collective-permute-done.4.upper = f32[176,32,128]{2,1,0:T(8,128)} collective-permute-done((f32[176,32,128]{2,1,0:T(8,128)}, f32[176,32,128]{2,1,0:T(8,128)}, u32[]{:S(2)}, u32[]{:S(2)}) %collective-permute-start.4) | collective-permute-done | bytes 2883616 | tf_op jit(solution)/shard_map/ppermute | solution.py:645
  45.8 14.9 %shard_map.49 = (f32[128,128,128]{2,1,0:T(8,128)}, f32[32,48,128]{2,1,0:T(8,128)S(1)}, f32[32,48,128]{2,1,0:T(8,128)S(1)}, f32[32,48,128]{2,1,0:T(8,128)S(1)}) custom-call(s32[5]{0:T(128)S(1)} %pad_add_fusion.starts, bf16[128,256]{1,0:T(8,128)(2,1)S(1)} %get-tuple-element.43.ax, bf16[4,128,512]{2,1,0:T(8,128)(2,1)S(1)} %get-tuple-element.44.az, ...), custom_call_target="tpu_custom_call" | custom-call | flops 1024 | bytes 1024 | tf_op jit(solution)/shard_map/pallas_call | solution.py:378
  60.8 1.3 collective-permute-start.6
  62.3 1.8 collective-permute-start.10
  64.1 16.3 %collective-permute-done.9.refs_8_.refs_10_ = f32[32,80,128]{2,1,0:T(8,128)S(1)} collective-permute-done((f32[32,80,128]{2,1,0:T(8,128)}, f32[32,80,128]{2,1,0:T(8,128)S(1)}, u32[]{:S(2)}, u32[]{:S(2)}) %collective-permute-start.9) | collective-permute-done | bytes 1310752 | tf_op jit(solution)/shard_map/ppermute | solution.py:649
  81.5 8.1 %shard_map.50 = (f32[96,16,128]{2,1,0:T(8,128)S(1)}, f32[64,32,128]{2,1,0:T(8,128)S(1)}, f32[64,32,128]{2,1,0:T(8,128)S(1)}, f32[32,32,128]{2,1,0:T(8,128)S(1)}, f32[32,32,128]{2,1,0:T(8,128)S(1)}) custom-call(s32[1]{0:T(128)} %bitcast.spot.refs_0_, bf16[160,256]{1,0:T(8,128)(2,1)S(1)} %get-tuple-element.40.refs_1_, ...), custom_call_target="tpu_custom_call" | custom-call | flops 1024 | bytes 1024 | tf_op jit(solution)/shard_map/pallas_call | solution.py:522
  89.6 4.6 %collective-permute-start.13 = (f32[32,32,128]{2,1,0:T(8,128)S(1)}, f32[32,32,128]{2,1,0:T(8,128)S(1)}, u32[]{:S(2)}, u32[]{:S(2)}) collective-permute-start(f32[32,32,128]{2,1,0:T(8,128)S(1)} %get-tuple-element.59), channel_id=1, source_target_pairs={{0,1},{1,2},{2,3},{3,4},{4,5},{5,6},{6,7},{7,8},{8,9},{9,10},{10,1... | collective-permute-start | bytes 1572872 | tf_op jit(solution)/shard_map/ppermute | solution.py:645
  94.2 1.9 collective-permute-start.12
  96.2 5.8 %collective-permute-start.11 = (f32[64,32,128]{2,1,0:T(8,128)S(1)}, f32[64,32,128]{2,1,0:T(8,128)S(1)}, u32[]{:S(2)}, u32[]{:S(2)}) collective-permute-start(f32[64,32,128]{2,1,0:T(8,128)S(1)} %get-tuple-element.56), channel_id=1, source_target_pairs={{0,1},{1,2},{2,3},{3,4},{4,5},{5,6},{6,7},{7,8},{8,9},{9,10},{10,1... | collective-permute-start | bytes 3145736 | tf_op jit(solution)/shard_map/ppermute | solution.py:645
  101.9 7.7 %collective-permute-done.12.down = f32[96,16,128]{2,1,0:T(8,128)S(1)} collective-permute-done((f32[96,16,128]{2,1,0:T(8,128)S(1)}, f32[96,16,128]{2,1,0:T(8,128)S(1)}, u32[]{:S(2)}, u32[]{:S(2)}) %collective-permute-start.12) | collective-permute-done | bytes 786464 | tf_op jit(solution)/shard_map/ppermute | solution.py:645
  109.8 1.9 collective-permute-start.14
  111.8 3.4 %collective-permute-start.15 = (f32[32,16,128]{2,1,0:T(8,128)S(1)}, f32[32,16,128]{2,1,0:T(8,128)S(1)}, u32[]{:S(2)}, u32[]{:S(2)}) collective-permute-start(f32[32,16,128]{2,1,0:T(8,128)S(1)} %get-tuple-element.61), channel_id=1, source_target_pairs={{32,0},{64,32},{96,64},{33,1},{65,33},{97,65},{34,2},{66,34},{98,6... | collective-permute-start | bytes 786440 | tf_op jit(solution)/shard_map/ppermute | solution.py:654
  115.3 1.6 collective-permute-done.14.rights
  117.0 3.8 %collective-permute-done.15.lefts = f32[32,16,128]{2,1,0:T(8,128)S(1)} collective-permute-done((f32[32,16,128]{2,1,0:T(8,128)S(1)}, f32[32,16,128]{2,1,0:T(8,128)S(1)}, u32[]{:S(2)}, u32[]{:S(2)}) %collective-permute-start.15) | collective-permute-done | bytes 262176 | tf_op jit(solution)/shard_map/ppermute | solution.py:654
  121.9 1.8 collective-permute-start.19
  125.2 9.2 %shard_map.55 = (f32[96,16,128]{2,1,0:T(8,128)S(1)}, f32[64,32,128]{2,1,0:T(8,128)}, f32[64,32,128]{2,1,0:T(8,128)}, f32[32,32,128]{2,1,0:T(8,128)S(1)}, f32[32,32,128]{2,1,0:T(8,128)S(1)}) custom-call(s32[1]{0:T(128)} %bitcast.spot.refs_0_, bf16[160,256]{1,0:T(8,128)(2,1)S(1)} %get-tuple-element.40.refs_1_, ...), custom_call_target="tpu_custom_call" | custom-call | flops 1024 | bytes 1024 | tf_op jit(solution)/shard_map/pallas_call | solution.py:522
  134.4 3.7 %collective-permute-start.18 = (f32[32,32,128]{2,1,0:T(8,128)S(1)}, f32[32,32,128]{2,1,0:T(8,128)S(1)}, u32[]{:S(2)}, u32[]{:S(2)}) collective-permute-start(f32[32,32,128]{2,1,0:T(8,128)S(1)} %get-tuple-element.68), channel_id=1, source_target_pairs={{0,1},{1,2},{2,3},{3,4},{4,5},{5,6},{6,7},{7,8},{8,9},{9,10},{10,1... | collective-permute-start | bytes 1572872 | tf_op jit(solution)/shard_map/ppermute | solution.py:645
  138.1 1.9 collective-permute-start.17
  140.0 5.8 %collective-permute-start.16 = (f32[64,32,128]{2,1,0:T(8,128)}, f32[64,32,128]{2,1,0:T(8,128)S(1)}, u32[]{:S(2)}, u32[]{:S(2)}) collective-permute-start(f32[64,32,128]{2,1,0:T(8,128)} %get-tuple-element.65), channel_id=1, source_target_pairs={{0,1},{1,2},{2,3},{3,4},{4,5},{5,6},{6,7},{7,8},{8,9},{9,10},{10,1... | collective-permute-start | bytes 3145736 | tf_op jit(solution)/shard_map/ppermute | solution.py:645
  145.8 1.6 collective-permute-start.23
  147.4 6.1 %collective-permute-done.17.down = f32[96,16,128]{2,1,0:T(8,128)S(1)} collective-permute-done((f32[96,16,128]{2,1,0:T(8,128)S(1)}, f32[96,16,128]{2,1,0:T(8,128)S(1)}, u32[]{:S(2)}, u32[]{:S(2)}) %collective-permute-start.17) | collective-permute-done | bytes 786464 | tf_op jit(solution)/shard_map/ppermute | solution.py:645
  153.5 1.2 collective-permute-start.24
  154.9 2.4 %collective-permute-start.21 = (f32[32,16,128]{2,1,0:T(8,128)S(1)}, f32[32,16,128]{2,1,0:T(8,128)S(1)}, u32[]{:S(2)}, u32[]{:S(2)}) collective-permute-start(f32[32,16,128]{2,1,0:T(8,128)S(1)} %get-tuple-element.69), channel_id=1, source_target_pairs={{0,32},{32,64},{64,96},{1,33},{33,65},{65,97},{2,34},{34,66},{66,9... | collective-permute-start | bytes 786440 | tf_op jit(solution)/shard_map/ppermute | solution.py:654
  157.8 3.1 %collective-permute-start.22 = (f32[32,16,128]{2,1,0:T(8,128)S(1)}, f32[32,16,128]{2,1,0:T(8,128)S(1)}, u32[]{:S(2)}, u32[]{:S(2)}) collective-permute-start(f32[32,16,128]{2,1,0:T(8,128)S(1)} %get-tuple-element.70), channel_id=1, source_target_pairs={{32,0},{64,32},{96,64},{33,1},{65,33},{97,65},{34,2},{66,34},{98,6... | collective-permute-start | bytes 786440 | tf_op jit(solution)/shard_map/ppermute | solution.py:654
  161.1 4.0 %collective-permute-done.24.refs_1_.refs_3_ = f32[32,32,128]{2,1,0:T(8,128)S(1)} collective-permute-done((f32[32,32,128]{2,1,0:T(8,128)S(1)}, f32[32,32,128]{2,1,0:T(8,128)S(1)}, u32[]{:S(2)}, u32[]{:S(2)}) %collective-permute-start.24) | collective-permute-done | bytes 524320 | tf_op jit(solution)/shard_map/ppermute | solution.py:649
  165.1 2.9 %collective-permute-done.22.lefts = f32[32,16,128]{2,1,0:T(8,128)S(1)} collective-permute-done((f32[32,16,128]{2,1,0:T(8,128)S(1)}, f32[32,16,128]{2,1,0:T(8,128)S(1)}, u32[]{:S(2)}, u32[]{:S(2)}) %collective-permute-start.22) | collective-permute-done | bytes 262176 | tf_op jit(solution)/shard_map/ppermute | solution.py:654
  169.1 1.5 collective-permute-start.27
  170.6 1.4 collective-permute-start.32
  172.5 10.6 %collective-permute-done.27.refs_4_.refs_2_ = f32[32,32,128]{2,1,0:T(8,128)S(1)} collective-permute-done((f32[32,32,128]{2,1,0:T(8,128)S(1)}, f32[32,32,128]{2,1,0:T(8,128)S(1)}, u32[]{:S(2)}, u32[]{:S(2)}) %collective-permute-start.27) | collective-permute-done | bytes 524320 | tf_op jit(solution)/shard_map/ppermute | solution.py:649
  183.2 1.4 collective-permute-start.28
  185.0 2.1 %shard_map.60.refs_4_ = f32[32,128,512]{2,1,0:T(8,128)} custom-call(s32[1]{0:T(128)} %bitcast.spot.refs_0_, f32[32,128,512]{2,1,0:T(8,128)} %refs_1_.15, f32[32,32,128]{2,1,0:T(8,128)S(1)} %get-tuple-element.62.refs_12_.refs_2_, f32[32,32,128]{2,1,0:T(8,128)S(1)} %get-tuple-element.63.refs_13_.refs_3_, ...), custom_call_target="tpu_custom_call" | custom-call | flops 1024 | bytes 1024 | tf_op jit(solution)/shard_map/pallas_call | solution.py:629
  187.1 2.1 %shard_map.61.refs_4_ = f32[32,128,512]{2,1,0:T(8,128)} custom-call(s32[1]{0:T(128)} %bitcast.spot.refs_0_, f32[32,128,512]{2,1,0:T(8,128)} %refs_1_.15, f32[32,32,128]{2,1,0:T(8,128)S(1)} %collective-permute-done.19.refs_0_.refs_2_, f32[32,32,128]{2,1,0:T(8,128)S(1)} %collective-permute-done.25.refs_2_.refs_3_, ...), custom_call_target="tpu_custom_call", output_to_operand_aliasing={{}: (4, {})} | custom-call | flops 1024 | bytes 1024 | tf_op jit(solution)/shard_map/pallas_call | solution.py:629
  189.2 2.1 %shard_map.62.refs_4_ = f32[32,128,512]{2,1,0:T(8,128)} custom-call(s32[1]{0:T(128)} %bitcast.spot.refs_0_, f32[32,128,512]{2,1,0:T(8,128)} %refs_1_.15, f32[32,32,128]{2,1,0:T(8,128)S(1)} %collective-permute-done.26.refs_3_.refs_2_, f32[32,32,128]{2,1,0:T(8,128)S(1)} %collective-permute-done.20.refs_1_.refs_3_, ...), custom_call_target="tpu_custom_call", output_to_operand_aliasing={{}: (4, {})} | custom-call | flops 1024 | bytes 1024 | tf_op jit(solution)/shard_map/pallas_call | solution.py:629
  191.3 2.1 %shard_map.63.refs_4_ = f32[32,128,512]{2,1,0:T(8,128)} custom-call(s32[1]{0:T(128)} %bitcast.spot.refs_0_, f32[32,128,512]{2,1,0:T(8,128)} %refs_1_.15, f32[32,32,128]{2,1,0:T(8,128)S(1)} %collective-permute-done.23.refs_0_.refs_2_, f32[32,32,128]{2,1,0:T(8,128)S(1)} %collective-permute-done.24.refs_1_.refs_3_, ...), custom_call_target="tpu_custom_call", output_to_operand_aliasing={{}: (4, {})} | custom-call | flops 1024 | bytes 1024 | tf_op jit(solution)/shard_map/pallas_call | solution.py:629
  193.4 2.1 %shard_map.64.refs_4_ = f32[32,128,512]{2,1,0:T(8,128)} custom-call(s32[1]{0:T(128)} %bitcast.spot.refs_0_, f32[32,128,512]{2,1,0:T(8,128)} %refs_1_.15, f32[32,32,128]{2,1,0:T(8,128)S(1)} %get-tuple-element.71.refs_2_, f32[32,32,128]{2,1,0:T(8,128)S(1)} %get-tuple-element.72.refs_3_, f32[32,128,512]{2,1,0:T(8,128)} %shard_map.63.refs_4_), custom_call_target="tpu_custom_call", output_to_operand_aliasing={{}: (4, {})} | custom-call | flops 1024 | bytes 1024 | tf_op jit(solution)/shard_map/pallas_call | solution.py:629
  195.5 2.1 %shard_map.65.refs_4_ = f32[32,128,512]{2,1,0:T(8,128)} custom-call(s32[1]{0:T(128)} %bitcast.spot.refs_0_, f32[32,128,512]{2,1,0:T(8,128)} %refs_1_.15, f32[32,32,128]{2,1,0:T(8,128)S(1)} %collective-permute-done.27.refs_4_.refs_2_, f32[32,32,128]{2,1,0:T(8,128)S(1)} %collective-permute-done.32.refs_3_, ...), custom_call_target="tpu_custom_call", output_to_operand_aliasing={{}: (4, {})} | custom-call | flops 1024 | bytes 1024 | tf_op jit(solution)/shard_map/pallas_call | solution.py:629
  197.6 2.1 %shard_map.66.refs_4_ = f32[32,128,512]{2,1,0:T(8,128)} custom-call(s32[1]{0:T(128)} %bitcast.spot.refs_0_, f32[32,128,512]{2,1,0:T(8,128)} %refs_1_.15, f32[32,32,128]{2,1,0:T(8,128)S(1)} %collective-permute-done.31.refs_2_, f32[32,32,128]{2,1,0:T(8,128)S(1)} %collective-permute-done.29.refs_5_.refs_3_, ...), custom_call_target="tpu_custom_call", output_to_operand_aliasing={{}: (4, {})} | custom-call | flops 1024 | bytes 1024 | tf_op jit(solution)/shard_map/pallas_call | solution.py:629
  199.6 4.7 %collective-permute-done.28.refs_2_ = f32[32,32,128]{2,1,0:T(8,128)S(1)} collective-permute-done((f32[32,32,128]{2,1,0:T(8,128)S(1)}, f32[32,32,128]{2,1,0:T(8,128)S(1)}, u32[]{:S(2)}, u32[]{:S(2)}) %collective-permute-start.28) | collective-permute-done | bytes 524320 | tf_op jit(solution)/shard_map/ppermute | solution.py:649
  204.3 1.4 collective-permute-done.30.refs_3_
  205.7 2.1 %shard_map.67 = f32[32,128,512]{2,1,0:T(8,128)} custom-call(s32[1]{0:T(128)} %bitcast.spot.refs_0_, f32[32,128,512]{2,1,0:T(8,128)} %refs_1_.15, f32[32,32,128]{2,1,0:T(8,128)S(1)} %collective-permute-done.28.refs_2_, f32[32,32,128]{2,1,0:T(8,128)S(1)} %collective-permute-done.30.refs_3_, ...), custom_call_target="tpu_custom_call", output_to_operand_aliasing={{}: (4, {})} | custom-call | flops 1024 | bytes 1024 | tf_op jit(solution)/shard_map/pallas_call | solution.py:629
  (62 shorter events, 8.7 us)
Async XLA Ops:
  0.0 15.3 %copy-start.7 = (s32[1,3]{1,0:T(1,128)S(1)}, s32[1,3]{1,0:T(1,128)}, u32[]{:S(2)}) copy-start(s32[1,3]{1,0:T(1,128)} %param.7) | copy-start | bytes 40
  0.0 15.4 %copy-start.6 = (f32[1,3,33]{2,0,1:T(1,128)S(1)}, f32[1,3,33]{2,0,1:T(1,128)}, u32[]{:S(2)}) copy-start(f32[1,3,33]{2,0,1:T(1,128)} %param.6) | copy-start | bytes 1192
  7.6 38.2 %collective-permute-start.4 = (f32[176,32,128]{2,1,0:T(8,128)}, f32[176,32,128]{2,1,0:T(8,128)}, u32[]{:S(2)}, u32[]{:S(2)}) collective-permute-start(f32[176,32,128]{2,1,0:T(8,128)} %get-tuple-element.47.middle), channel_id=1, source_target_pairs={{1,0},{2,1},{3,2},{4,3},{5,4},{6,5},{7,6},{8,7},{9,8},{10,9},{11,1... | collective-permute-start | bytes 8650760 | tf_op jit(solution)/shard_map/ppermute | solution.py:645
  10.2 21.3 %collective-permute-start.3 = (f32[176,16,128]{2,1,0:T(8,128)}, f32[176,16,128]{2,1,0:T(8,128)S(1)}, u32[]{:S(2)}, u32[]{:S(2)}) collective-permute-start(f32[176,16,128]{2,1,0:T(8,128)} %get-tuple-element.46), channel_id=1, source_target_pairs={{0,1},{1,2},{2,3},{3,4},{4,5},{5,6},{6,7},{7,8},{8,9},{9,10},{10,1... | collective-permute-start | bytes 4325384 | tf_op jit(solution)/shard_map/ppermute | solution.py:645
  15.4 0.7 copy-start.2
  16.2 3.9 %collective-permute-start.2 = (f32[3,34]{1,0:T(4,128)S(1)}, f32[3,34]{1,0:T(4,128)S(1)}, u32[]{:S(2)}, u32[]{:S(2)}) collective-permute-start(f32[3,34]{1,0:T(4,128)S(1)} %shard_map.47), channel_id=1, source_target_pairs={{0,96},{32,0},{64,32},{96,64},{1,97},{33,1},{65,33},{97,65},{2,98}... | collective-permute-start | bytes 1232 | tf_op jit(solution)/shard_map/ppermute | solution.py:649
  16.3 3.9 %collective-permute-start.1 = (f32[3,34]{1,0:T(4,128)S(1)}, f32[3,34]{1,0:T(4,128)S(1)}, u32[]{:S(2)}, u32[]{:S(2)}) collective-permute-start(f32[3,34]{1,0:T(4,128)S(1)} %shard_map.47), channel_id=1, source_target_pairs={{0,64},{32,96},{64,0},{96,32},{1,65},{33,97},{65,1},{97,33},{2,66}... | collective-permute-start | bytes 1232 | tf_op jit(solution)/shard_map/ppermute | solution.py:649
  18.6 4.4 %collective-permute-start = (f32[3,34]{1,0:T(4,128)S(1)}, f32[3,34]{1,0:T(4,128)S(1)}, u32[]{:S(2)}, u32[]{:S(2)}) collective-permute-start(f32[3,34]{1,0:T(4,128)S(1)} %shard_map.47), channel_id=1, source_target_pairs={{0,32},{32,64},{64,96},{96,0},{1,33},{33,65},{65,97},{97,1},{2,34}... | collective-permute-start | bytes 1232 | tf_op jit(solution)/shard_map/ppermute | solution.py:649
  20.1 42.2 %collective-permute-start.5 = (f32[32,80,128]{2,1,0:T(8,128)}, f32[32,80,128]{2,1,0:T(8,128)S(1)}, u32[]{:S(2)}, u32[]{:S(2)}) collective-permute-start(f32[32,80,128]{2,1,0:T(8,128)} %get-tuple-element.49), channel_id=1, source_target_pairs={{0,32},{32,64},{64,96},{96,0},{1,33},{33,65},{65,97},{97,1},{2,34}... | collective-permute-start | bytes 3932168 | tf_op jit(solution)/shard_map/ppermute | solution.py:649
  20.2 43.9 %collective-permute-start.7 = (f32[32,80,128]{2,1,0:T(8,128)}, f32[32,80,128]{2,1,0:T(8,128)S(1)}, u32[]{:S(2)}, u32[]{:S(2)}) collective-permute-start(f32[32,80,128]{2,1,0:T(8,128)} %get-tuple-element.51), channel_id=1, source_target_pairs={{0,96},{32,0},{64,32},{96,64},{1,97},{33,1},{65,33},{97,65},{2,98}... | collective-permute-start | bytes 3932168 | tf_op jit(solution)/shard_map/ppermute | solution.py:649
  23.0 57.5 %collective-permute-start.9 = (f32[32,80,128]{2,1,0:T(8,128)}, f32[32,80,128]{2,1,0:T(8,128)S(1)}, u32[]{:S(2)}, u32[]{:S(2)}) collective-permute-start(f32[32,80,128]{2,1,0:T(8,128)} %get-tuple-element.53), channel_id=1, source_target_pairs={{0,64},{32,96},{64,0},{96,32},{1,65},{33,97},{65,1},{97,33},{2,66}... | collective-permute-start | bytes 3932168 | tf_op jit(solution)/shard_map/ppermute | solution.py:649
  60.8 35.4 %collective-permute-start.6 = (f32[32,48,128]{2,1,0:T(8,128)S(1)}, f32[32,48,128]{2,1,0:T(8,128)S(1)}, u32[]{:S(2)}, u32[]{:S(2)}) collective-permute-start(f32[32,48,128]{2,1,0:T(8,128)S(1)} %get-tuple-element.50), channel_id=1, source_target_pairs={{0,32},{32,64},{64,96},{96,0},{1,33},{33,65},{65,97},{97,1},{2,34}... | collective-permute-start | bytes 2359304 | tf_op jit(solution)/shard_map/ppermute | solution.py:649
  62.1 39.9 %collective-permute-start.8 = (f32[32,48,128]{2,1,0:T(8,128)S(1)}, f32[32,48,128]{2,1,0:T(8,128)S(1)}, u32[]{:S(2)}, u32[]{:S(2)}) collective-permute-start(f32[32,48,128]{2,1,0:T(8,128)S(1)} %get-tuple-element.52), channel_id=1, source_target_pairs={{0,96},{32,0},{64,32},{96,64},{1,97},{33,1},{65,33},{97,65},{2,98}... | collective-permute-start | bytes 2359304 | tf_op jit(solution)/shard_map/ppermute | solution.py:649
  62.3 19.2 %copy-start.3 = (f32[32,80,128]{2,1,0:T(8,128)}, f32[32,80,128]{2,1,0:T(8,128)S(1)}, u32[]{:S(2)}) copy-start(f32[32,80,128]{2,1,0:T(8,128)S(1)} %collective-permute-done.5.refs_6_) | copy-start | bytes 3932164
  62.3 52.8 %collective-permute-start.10 = (f32[32,48,128]{2,1,0:T(8,128)S(1)}, f32[32,48,128]{2,1,0:T(8,128)S(1)}, u32[]{:S(2)}, u32[]{:S(2)}) collective-permute-start(f32[32,48,128]{2,1,0:T(8,128)S(1)} %get-tuple-element.54), channel_id=1, source_target_pairs={{0,64},{32,96},{64,0},{96,32},{1,65},{33,97},{65,1},{97,33},{2,66}... | collective-permute-start | bytes 2359304 | tf_op jit(solution)/shard_map/ppermute | solution.py:649
  64.1 17.4 %copy-start.4 = (f32[32,80,128]{2,1,0:T(8,128)}, f32[32,80,128]{2,1,0:T(8,128)S(1)}, u32[]{:S(2)}) copy-start(f32[32,80,128]{2,1,0:T(8,128)S(1)} %collective-permute-done.7.refs_7_.refs_8_) | copy-start | bytes 3932164
  80.5 1.1 copy-start.5
  89.6 12.3 %collective-permute-start.13 = (f32[32,32,128]{2,1,0:T(8,128)S(1)}, f32[32,32,128]{2,1,0:T(8,128)S(1)}, u32[]{:S(2)}, u32[]{:S(2)}) collective-permute-start(f32[32,32,128]{2,1,0:T(8,128)S(1)} %get-tuple-element.59), channel_id=1, source_target_pairs={{0,1},{1,2},{2,3},{3,4},{4,5},{5,6},{6,7},{7,8},{8,9},{9,10},{10,1... | collective-permute-start | bytes 1572872 | tf_op jit(solution)/shard_map/ppermute | solution.py:645
  94.2 15.4 %collective-permute-start.12 = (f32[96,16,128]{2,1,0:T(8,128)S(1)}, f32[96,16,128]{2,1,0:T(8,128)S(1)}, u32[]{:S(2)}, u32[]{:S(2)}) collective-permute-start(f32[96,16,128]{2,1,0:T(8,128)S(1)} %get-tuple-element.57), channel_id=1, source_target_pairs={{1,0},{2,1},{3,2},{4,3},{5,4},{6,5},{7,6},{8,7},{9,8},{10,9},{11,1... | collective-permute-start | bytes 2359304 | tf_op jit(solution)/shard_map/ppermute | solution.py:645
  96.2 19.0 %collective-permute-start.11 = (f32[64,32,128]{2,1,0:T(8,128)S(1)}, f32[64,32,128]{2,1,0:T(8,128)S(1)}, u32[]{:S(2)}, u32[]{:S(2)}) collective-permute-start(f32[64,32,128]{2,1,0:T(8,128)S(1)} %get-tuple-element.56), channel_id=1, source_target_pairs={{0,1},{1,2},{2,3},{3,4},{4,5},{5,6},{6,7},{7,8},{8,9},{9,10},{10,1... | collective-permute-start | bytes 3145736 | tf_op jit(solution)/shard_map/ppermute | solution.py:645
  109.8 7.1 %collective-permute-start.14 = (f32[32,16,128]{2,1,0:T(8,128)S(1)}, f32[32,16,128]{2,1,0:T(8,128)S(1)}, u32[]{:S(2)}, u32[]{:S(2)}) collective-permute-start(f32[32,16,128]{2,1,0:T(8,128)S(1)} %get-tuple-element.60), channel_id=1, source_target_pairs={{0,32},{32,64},{64,96},{1,33},{33,65},{65,97},{2,34},{34,66},{66,9... | collective-permute-start | bytes 786440 | tf_op jit(solution)/shard_map/ppermute | solution.py:654
  111.8 9.0 %collective-permute-start.15 = (f32[32,16,128]{2,1,0:T(8,128)S(1)}, f32[32,16,128]{2,1,0:T(8,128)S(1)}, u32[]{:S(2)}, u32[]{:S(2)}) collective-permute-start(f32[32,16,128]{2,1,0:T(8,128)S(1)} %get-tuple-element.61), channel_id=1, source_target_pairs={{32,0},{64,32},{96,64},{33,1},{65,33},{97,65},{34,2},{66,34},{98,6... | collective-permute-start | bytes 786440 | tf_op jit(solution)/shard_map/ppermute | solution.py:654
  115.2 10.0 %copy-start = (f32[32,48,128]{2,1,0:T(8,128)}, f32[32,48,128]{2,1,0:T(8,128)S(1)}, u32[]{:S(2)}) copy-start(f32[32,48,128]{2,1,0:T(8,128)S(1)} %collective-permute-done.10.refs_0_.refs_11_) | copy-start | bytes 2359300
  121.9 16.2 %collective-permute-start.19 = (f32[32,32,128]{2,1,0:T(8,128)S(1)}, f32[32,32,128]{2,1,0:T(8,128)S(1)}, u32[]{:S(2)}, u32[]{:S(2)}) collective-permute-start(f32[32,32,128]{2,1,0:T(8,128)S(1)} %get-tuple-element.62.refs_12_.refs_2_), channel_id=1, source_target_pairs={{0,32},{32,64},{64,96},{96,0},{1,33},{33,65},{65,97},{97,1},{2,34}... | collective-permute-start | bytes 1572872 | tf_op jit(solution)/shard_map/ppermute | solution.py:649
  123.7 16.3 %collective-permute-start.20 = (f32[32,32,128]{2,1,0:T(8,128)S(1)}, f32[32,32,128]{2,1,0:T(8,128)S(1)}, u32[]{:S(2)}, u32[]{:S(2)}) collective-permute-start(f32[32,32,128]{2,1,0:T(8,128)S(1)} %get-tuple-element.63.refs_13_.refs_3_), channel_id=1, source_target_pairs={{0,96},{32,0},{64,32},{96,64},{1,97},{33,1},{65,33},{97,65},{2,98}... | collective-permute-start | bytes 1572872 | tf_op jit(solution)/shard_map/ppermute | solution.py:649
  123.7 31.2 %collective-permute-start.26 = (f32[32,32,128]{2,1,0:T(8,128)S(1)}, f32[32,32,128]{2,1,0:T(8,128)S(1)}, u32[]{:S(2)}, u32[]{:S(2)}) collective-permute-start(f32[32,32,128]{2,1,0:T(8,128)S(1)} %get-tuple-element.62.refs_12_.refs_2_), channel_id=1, source_target_pairs={{0,96},{32,0},{64,32},{96,64},{1,97},{33,1},{65,33},{97,65},{2,98}... | collective-permute-start | bytes 1572872 | tf_op jit(solution)/shard_map/ppermute | solution.py:649
  124.2 36.8 %collective-permute-start.25 = (f32[32,32,128]{2,1,0:T(8,128)S(1)}, f32[32,32,128]{2,1,0:T(8,128)S(1)}, u32[]{:S(2)}, u32[]{:S(2)}) collective-permute-start(f32[32,32,128]{2,1,0:T(8,128)S(1)} %get-tuple-element.63.refs_13_.refs_3_), channel_id=1, source_target_pairs={{0,32},{32,64},{64,96},{96,0},{1,33},{33,65},{65,97},{97,1},{2,34}... | collective-permute-start | bytes 1572872 | tf_op jit(solution)/shard_map/ppermute | solution.py:649
  134.4 11.4 %collective-permute-start.18 = (f32[32,32,128]{2,1,0:T(8,128)S(1)}, f32[32,32,128]{2,1,0:T(8,128)S(1)}, u32[]{:S(2)}, u32[]{:S(2)}) collective-permute-start(f32[32,32,128]{2,1,0:T(8,128)S(1)} %get-tuple-element.68), channel_id=1, source_target_pairs={{0,1},{1,2},{2,3},{3,4},{4,5},{5,6},{6,7},{7,8},{8,9},{9,10},{10,1... | collective-permute-start | bytes 1572872 | tf_op jit(solution)/shard_map/ppermute | solution.py:645
  138.1 15.4 %collective-permute-start.17 = (f32[96,16,128]{2,1,0:T(8,128)S(1)}, f32[96,16,128]{2,1,0:T(8,128)S(1)}, u32[]{:S(2)}, u32[]{:S(2)}) collective-permute-start(f32[96,16,128]{2,1,0:T(8,128)S(1)} %get-tuple-element.66), channel_id=1, source_target_pairs={{1,0},{2,1},{3,2},{4,3},{5,4},{6,5},{7,6},{8,7},{9,8},{10,9},{11,1... | collective-permute-start | bytes 2359304 | tf_op jit(solution)/shard_map/ppermute | solution.py:645
  140.0 17.8 %collective-permute-start.16 = (f32[64,32,128]{2,1,0:T(8,128)}, f32[64,32,128]{2,1,0:T(8,128)S(1)}, u32[]{:S(2)}, u32[]{:S(2)}) collective-permute-start(f32[64,32,128]{2,1,0:T(8,128)} %get-tuple-element.65), channel_id=1, source_target_pairs={{0,1},{1,2},{2,3},{3,4},{4,5},{5,6},{6,7},{7,8},{8,9},{9,10},{10,1... | collective-permute-start | bytes 3145736 | tf_op jit(solution)/shard_map/ppermute | solution.py:645
  145.8 15.2 %collective-permute-start.23 = (f32[32,32,128]{2,1,0:T(8,128)S(1)}, f32[32,32,128]{2,1,0:T(8,128)S(1)}, u32[]{:S(2)}, u32[]{:S(2)}) collective-permute-start(f32[32,32,128]{2,1,0:T(8,128)S(1)} %collective-permute-done.19.refs_0_.refs_2_), channel_id=1, source_target_pairs={{0,32},{32,64},{64,96},{96,0},{1,33},{33,65},{65,97},{97,1},{2,34}... | collective-permute-start | bytes 1572872 | tf_op jit(solution)/shard_map/ppermute | solution.py:649
  153.5 11.6 %collective-permute-start.24 = (f32[32,32,128]{2,1,0:T(8,128)S(1)}, f32[32,32,128]{2,1,0:T(8,128)S(1)}, u32[]{:S(2)}, u32[]{:S(2)}) collective-permute-start(f32[32,32,128]{2,1,0:T(8,128)S(1)} %collective-permute-done.20.refs_1_.refs_3_), channel_id=1, source_target_pairs={{0,96},{32,0},{64,32},{96,64},{1,97},{33,1},{65,33},{97,65},{2,98}... | collective-permute-start | bytes 1572872 | tf_op jit(solution)/shard_map/ppermute | solution.py:649
  154.7 6.2 %copy-start.1 = (f32[64,32,128]{2,1,0:T(8,128)S(1)}, f32[64,32,128]{2,1,0:T(8,128)}, u32[]{:S(2)}) copy-start(f32[64,32,128]{2,1,0:T(8,128)} %get-tuple-element.64.own) | copy-start | bytes 3145732
  154.9 10.2 %collective-permute-start.21 = (f32[32,16,128]{2,1,0:T(8,128)S(1)}, f32[32,16,128]{2,1,0:T(8,128)S(1)}, u32[]{:S(2)}, u32[]{:S(2)}) collective-permute-start(f32[32,16,128]{2,1,0:T(8,128)S(1)} %get-tuple-element.69), channel_id=1, source_target_pairs={{0,32},{32,64},{64,96},{1,33},{33,65},{65,97},{2,34},{34,66},{66,9... | collective-permute-start | bytes 786440 | tf_op jit(solution)/shard_map/ppermute | solution.py:654
  157.8 10.2 %collective-permute-start.22 = (f32[32,16,128]{2,1,0:T(8,128)S(1)}, f32[32,16,128]{2,1,0:T(8,128)S(1)}, u32[]{:S(2)}, u32[]{:S(2)}) collective-permute-start(f32[32,16,128]{2,1,0:T(8,128)S(1)} %get-tuple-element.70), channel_id=1, source_target_pairs={{32,0},{64,32},{96,64},{33,1},{65,33},{97,65},{34,2},{66,34},{98,6... | collective-permute-start | bytes 786440 | tf_op jit(solution)/shard_map/ppermute | solution.py:654
  169.1 14.0 %collective-permute-start.27 = (f32[32,32,128]{2,1,0:T(8,128)S(1)}, f32[32,32,128]{2,1,0:T(8,128)S(1)}, u32[]{:S(2)}, u32[]{:S(2)}) collective-permute-start(f32[32,32,128]{2,1,0:T(8,128)S(1)} %get-tuple-element.71.refs_2_), channel_id=1, source_target_pairs={{0,32},{32,64},{64,96},{96,0},{1,33},{33,65},{65,97},{97,1},{2,34}... | collective-permute-start | bytes 1572872 | tf_op jit(solution)/shard_map/ppermute | solution.py:649
  170.6 14.0 %collective-permute-start.29 = (f32[32,32,128]{2,1,0:T(8,128)S(1)}, f32[32,32,128]{2,1,0:T(8,128)S(1)}, u32[]{:S(2)}, u32[]{:S(2)}) collective-permute-start(f32[32,32,128]{2,1,0:T(8,128)S(1)} %get-tuple-element.72.refs_3_), channel_id=1, source_target_pairs={{0,96},{32,0},{64,32},{96,64},{1,97},{33,1},{65,33},{97,65},{2,98}... | collective-permute-start | bytes 1572872 | tf_op jit(solution)/shard_map/ppermute | solution.py:649
  170.6 24.8 %collective-permute-start.32 = (f32[32,32,128]{2,1,0:T(8,128)S(1)}, f32[32,32,128]{2,1,0:T(8,128)S(1)}, u32[]{:S(2)}, u32[]{:S(2)}) collective-permute-start(f32[32,32,128]{2,1,0:T(8,128)S(1)} %get-tuple-element.72.refs_3_), channel_id=1, source_target_pairs={{0,32},{32,64},{64,96},{96,0},{1,33},{33,65},{65,97},{97,1},{2,34}... | collective-permute-start | bytes 1572872 | tf_op jit(solution)/shard_map/ppermute | solution.py:649
  172.1 25.5 %collective-permute-start.31 = (f32[32,32,128]{2,1,0:T(8,128)S(1)}, f32[32,32,128]{2,1,0:T(8,128)S(1)}, u32[]{:S(2)}, u32[]{:S(2)}) collective-permute-start(f32[32,32,128]{2,1,0:T(8,128)S(1)} %get-tuple-element.71.refs_2_), channel_id=1, source_target_pairs={{0,96},{32,0},{64,32},{96,64},{1,97},{33,1},{65,33},{97,65},{2,98}... | collective-permute-start | bytes 1572872 | tf_op jit(solution)/shard_map/ppermute | solution.py:649
  183.2 21.1 %collective-permute-start.28 = (f32[32,32,128]{2,1,0:T(8,128)S(1)}, f32[32,32,128]{2,1,0:T(8,128)S(1)}, u32[]{:S(2)}, u32[]{:S(2)}) collective-permute-start(f32[32,32,128]{2,1,0:T(8,128)S(1)} %collective-permute-done.27.refs_4_.refs_2_), channel_id=1, source_target_pairs={{0,32},{32,64},{64,96},{96,0},{1,33},{33,65},{65,97},{97,1},{2,34}... | collective-permute-start | bytes 1572872 | tf_op jit(solution)/shard_map/ppermute | solution.py:649
  184.6 21.1 %collective-permute-start.30 = (f32[32,32,128]{2,1,0:T(8,128)S(1)}, f32[32,32,128]{2,1,0:T(8,128)S(1)}, u32[]{:S(2)}, u32[]{:S(2)}) collective-permute-start(f32[32,32,128]{2,1,0:T(8,128)S(1)} %collective-permute-done.29.refs_5_.refs_3_), channel_id=1, source_target_pairs={{0,96},{32,0},{64,32},{96,64},{1,97},{33,1},{65,33},{97,65},{2,98}... | collective-permute-start | bytes 1572872 | tf_op jit(solution)/shard_map/ppermute | solution.py:649
